TPU v7x, 128 devices: a whole 4x4x4 slice. The times are simulated.
128 devices in a mesh: row: 16 (over y, x_lo, core), col: 8 (over x_hi, z).
Axes of the slice: x: 4 (x_hi: 2, x_lo: 2; x = x_hi * 2 + x_lo), y: 4, z: 4, core: 2. Of those that a mesh axis runs over, the one named last changes fastest.
Arguments:
- spectra: bfloat16 [2, 16, 16, 512, 1024], P(None, 'row', None, 'col'), may hold values from -200 to 200
- block_pairs: int32 [16, 2], replicated, may hold values from 0 to 15
- band_bins: int32 [1024], P('col'), may hold values from 0 to 4095
Outputs:
- correlations: float32 [16, 512, 12, 512], P('row', 'col')
Inputs may be any that keep to these rules, and one draw needn't show every extreme that they name: `block_pairs`: each row names the row block and the column block of one pair; the two may be equal and blocks may repeat across pairs. `band_bins`: bins of a transform of 8192 samples; entries may repeat.
All inputs are finite; a program needn't handle non-finite values.
Results may differ from a plain program's by a relative error of at most 0.014.
Values may be sent and summed in bfloat16 or wider, within the bound.
No kernel may reach another device: no remote copies, remote signals or barrier semaphores. Data moves between devices by JAX's collectives and lax.ppermute only.
A program may use at most 128 MiB of HBM per device.

v0:
```python
import math

import jax
import jax.numpy as jnp
from jax import lax
from jax.sharding import PartitionSpec as P

L = 8192
LAGS = 12


epsilon = 1e-06


def whiten(values_in):
    values = values_in.astype(jnp.float32)
    energy = jnp.mean(jnp.sum(values * values, axis=-4, keepdims=True), axis=-1, keepdims=True)
    return (values * lax.rsqrt(energy + epsilon)).astype(jnp.bfloat16)


def phase_tables(band_bins, lag_offsets):
    steps_mod = jnp.mod(band_bins[None, :] * lag_offsets[:, None], L)
    angle = steps_mod.astype(jnp.float32) * (2.0 * math.pi / L)
    return (jnp.cos(angle), jnp.sin(angle))


def lag_product(rows_part, right_cols, cos_row, sin_row, scaling):
    turned = jnp.stack(
        [
            rows_part[0] * cos_row - rows_part[1] * sin_row,
            rows_part[0] * sin_row + rows_part[1] * cos_row,
        ]
    ).astype(jnp.bfloat16)
    product = lax.dot_general(
        turned, right_cols, (((0, 1, 3), (0, 1, 3)), ((), ())), preferred_element_type=jnp.float32
    )
    return product * scaling


def body(spectra, block_pairs, band_bins):
    col_count = lax.axis_size("col")
    row_count = lax.axis_size("row")
    whitened = whiten(jnp.moveaxis(spectra, 2, 0))
    seg_local = whitened.shape[2]
    chan_local = whitened.shape[3]
    freq_all = whitened.shape[4]
    band_width = freq_all // col_count
    pair_count = block_pairs.shape[0]
    chosen = jnp.take(whitened, block_pairs.reshape(-1), axis=0)
    outgoing = chosen.reshape(pair_count, 2, 2, seg_local, chan_local, freq_all)
    split_up = outgoing.reshape(pair_count, 2, 2, seg_local, chan_local, col_count, band_width)
    split_up = jnp.transpose(split_up, (0, 5, 1, 2, 3, 4, 6))
    split_up = split_up.reshape(pair_count * col_count, 2, 2, seg_local, chan_local, band_width)
    landed = lax.all_to_all(split_up, ("row", "col"), split_axis=0, concat_axis=0, tiled=True)
    landed = landed.reshape(row_count, col_count, 2, 2, seg_local, chan_local, band_width)
    arrived = jnp.transpose(landed, (2, 3, 0, 4, 1, 5, 6))
    arrived = arrived.reshape(2, 2, row_count * seg_local, col_count * chan_local, band_width)
    left_rows = arrived[0]
    right_cols = arrived[1]
    scaling = 1.0 / math.sqrt(row_count * seg_local * band_width * col_count)
    lag_offsets = jnp.arange(LAGS, dtype=jnp.int32) - LAGS // 2
    cosine, sine_table = phase_tables(band_bins, lag_offsets)
    rows_part = left_rows.astype(jnp.float32)

    def one_lag(tables):
        return lag_product(rows_part, right_cols, tables[0], tables[1], scaling)

    per_lag = lax.map(one_lag, (cosine, sine_table))
    stacked = lax.psum_scatter(
        jnp.moveaxis(per_lag, 0, 1).astype(jnp.bfloat16), "col", scatter_dimension=0, tiled=True
    ).astype(jnp.float32)
    return stacked[None]


def solution(mesh):
    in_specs = (P(None, "row", None, "col", None), P(), P("col"))
    out_specs = P("row", "col", None, None)
    return jax.shard_map(body, mesh=mesh, in_specs=in_specs, out_specs=out_specs, check_vma=False)
```

profile of v0, /device:TPU:1, one launch (start us, length us, event | category | flops | bytes accessed | tf_op | source)
XLA Modules:
  0.0 380.8 jit_solution(7173298719051707553)
XLA Ops:
  8.1 3.3 fusion.19
  14.2 7.2 %gather_fusion = bf16[32,2,64,1024]{3,2,1,0:T(8,128)(2,1)} fusion(bf16[16,2,64,1024]{3,2,0,1:T(8,128)(2,1)} %fusion.21, s32[1024]{0:T(1024)S(1)} %pad_clamp_fusion), kind=kCustom, calls=%fused_computation | custom fusion | bytes 16777344 | tf_op jit(solution)/shard_map/jit(_take)/gather | solution.py:49
  21.4 8.8 %copy.22 = bf16[512,8,8,128]{3,2,1,0:T(8,128)(2,1)} copy(bf16[512,8,8,128]{3,1,2,0:T(8,128)(2,1)} %bitcast.56) | data formatting | bytes 16777216
  30.3 7.5 %select_bitcast_fusion = bf16[16,8,2,2,1,64,128]{6,1,5,3,2,0,4:T(8,128)(2,1)} fusion(bf16[16,2,2,1,64,8,128]{6,5,4,2,1,0,3:T(8,128)(2,1)} %bitcast.58, pred[16,2]{1,0:T(8,128)(4,1)S(1)} %copy.15), kind=kLoop, calls=%fused_computation.20 | loop fusion | flops 4194304 | bytes 16777248 | tf_op jit(solution)/shard_map/transpose | solution.py:52
  37.8 9.1 %copy.17 = bf16[16,8,2,2,1,64,128]{6,5,3,2,1,0,4:T(8,128)(2,1)} copy(bf16[16,8,2,2,1,64,128]{6,1,5,3,2,0,4:T(8,128)(2,1)} %select_bitcast_fusion) | data formatting | bytes 16777216 | tf_op jit(solution)/shard_map/transpose | solution.py:52
  46.9 12.0 %all-to-all-start = ((bf16[128,2,2,1,64,128]{5,4,2,1,3,0:T(8,128)(2,1)}), bf16[128,2,2,1,64,128]{5,4,2,1,3,0:T(8,128)(2,1)}, u32[]{:S(2)}, u32[]{:S(2)}) async-start(bf16[128,2,2,1,64,128]{5,4,2,1,3,0:T(8,128)(2,1)} %bitcast.57), calls=%async_computation | async-start | bytes 16777216 | tf_op jit(solution)/shard_map/all_to_all | solution.py:54
  59.3 101.3 %all-to-all-done = bf16[128,2,2,1,64,128]{5,4,2,1,3,0:T(8,128)(2,1)} async-done(((bf16[128,2,2,1,64,128]{5,4,2,1,3,0:T(8,128)(2,1)}), bf16[128,2,2,1,64,128]{5,4,2,1,3,0:T(8,128)(2,1)}, u32[]{:S(2)}, u32[]{:S(2)}) %all-to-all-start) | async-done | bytes 8388640 | tf_op jit(solution)/shard_map/all_to_all | solution.py:54
  160.5 4.4 %fusion.28 = (bf16[1,2,16,1,8,64,128]{6,5,1,0,4,2,3:T(8,128)(2,1)S(1)}, f32[1,2,16,1,8,64,128]{6,5,1,0,4,2,3:T(8,128)S(1)}) fusion(bf16[2,2,16,1,8,64,128]{6,5,1,0,4,2,3:T(8,128)(2,1)} %bitcast.12), kind=kLoop, calls=%fused_computation.42 | loop fusion | flops 2097152 | bytes 20971520 | tf_op jit(solution)/shard_map/slice | solution.py:59
  165.0 4.1 %copy.19 = f32[1,2,16,1,8,64,128]{6,5,4,2,1,3,0:T(8,128)} copy(f32[1,2,16,1,8,64,128]{6,5,1,0,4,2,3:T(8,128)S(1)} %get-tuple-element.55) | data formatting | bytes 16777216 | tf_op jit(solution)/shard_map/convert_element_type | solution.py:63
  172.0 95.7 %while.10 = (s32[]{:T(128)}, bf16[12,512,512]{2,1,0:T(8,128)(2,1)}, f32[2,16,512,128]{3,2,1,0:T(8,128)}, f32[12,128]{1,0:T(8,128)S(1)}, f32[12,128]{1,0:T(8,128)...) while((s32[]{:T(128)}, bf16[12,512,512]{2,1,0:T(8,128)(2,1)}, f32[2,16,512,128]{3,2,1,0:T(8,128)}, ...), condition=%wide.region_2.3_spmd, body=%wide.region_1.0_spmd.sunk | while | flops 2158231552 | bytes 38801004 | solution.py:68
  172.0 4.8 %subtract_convert_fusion.2 = (bf16[1,16,512,128]{3,2,1,0:T(8,128)(2,1)S(1)}, bf16[1,16,512,128]{3,2,1,0:T(8,128)(2,1)S(1)}) fusion(f32[2,16,512,128]{3,2,1,0:T(8,128)} %get-tuple-element.119, f32[128]{0:T(128)S(1)} %get-tuple-element.99, f32[128]{0:T(128)S(1)} %get-tuple-element.100), kind=kLoop, calls=%fused_computation.6.clone.1 | loop fusion | flops 8388608 | bytes 12583936 | tf_op jit(solution)/shard_map/convert
  180.0 4.8 %subtract_convert_fusion.2 = (bf16[1,16,512,128]{3,2,1,0:T(8,128)(2,1)S(1)}, bf16[1,16,512,128]{3,2,1,0:T(8,128)(2,1)S(1)}) fusion(f32[2,16,512,128]{3,2,1,0:T(8,128)} %get-tuple-element.119, f32[128]{0:T(128)S(1)} %get-tuple-element.99, f32[128]{0:T(128)S(1)} %get-tuple-element.100), kind=kLoop, calls=%fused_computation.6.clone.1 | loop fusion | flops 8388608 | bytes 12583936 | tf_op jit(solution)/shard_map/convert
  187.9 4.8 %subtract_convert_fusion.2 = (bf16[1,16,512,128]{3,2,1,0:T(8,128)(2,1)S(1)}, bf16[1,16,512,128]{3,2,1,0:T(8,128)(2,1)S(1)}) fusion(f32[2,16,512,128]{3,2,1,0:T(8,128)} %get-tuple-element.119, f32[128]{0:T(128)S(1)} %get-tuple-element.99, f32[128]{0:T(128)S(1)} %get-tuple-element.100), kind=kLoop, calls=%fused_computation.6.clone.1 | loop fusion | flops 8388608 | bytes 12583936 | tf_op jit(solution)/shard_map/convert
  195.9 4.8 %subtract_convert_fusion.2 = (bf16[1,16,512,128]{3,2,1,0:T(8,128)(2,1)S(1)}, bf16[1,16,512,128]{3,2,1,0:T(8,128)(2,1)S(1)}) fusion(f32[2,16,512,128]{3,2,1,0:T(8,128)} %get-tuple-element.119, f32[128]{0:T(128)S(1)} %get-tuple-element.99, f32[128]{0:T(128)S(1)} %get-tuple-element.100), kind=kLoop, calls=%fused_computation.6.clone.1 | loop fusion | flops 8388608 | bytes 12583936 | tf_op jit(solution)/shard_map/convert
  203.9 4.8 %subtract_convert_fusion.2 = (bf16[1,16,512,128]{3,2,1,0:T(8,128)(2,1)S(1)}, bf16[1,16,512,128]{3,2,1,0:T(8,128)(2,1)S(1)}) fusion(f32[2,16,512,128]{3,2,1,0:T(8,128)} %get-tuple-element.119, f32[128]{0:T(128)S(1)} %get-tuple-element.99, f32[128]{0:T(128)S(1)} %get-tuple-element.100), kind=kLoop, calls=%fused_computation.6.clone.1 | loop fusion | flops 8388608 | bytes 12583936 | tf_op jit(solution)/shard_map/convert
  211.9 4.8 %subtract_convert_fusion.2 = (bf16[1,16,512,128]{3,2,1,0:T(8,128)(2,1)S(1)}, bf16[1,16,512,128]{3,2,1,0:T(8,128)(2,1)S(1)}) fusion(f32[2,16,512,128]{3,2,1,0:T(8,128)} %get-tuple-element.119, f32[128]{0:T(128)S(1)} %get-tuple-element.99, f32[128]{0:T(128)S(1)} %get-tuple-element.100), kind=kLoop, calls=%fused_computation.6.clone.1 | loop fusion | flops 8388608 | bytes 12583936 | tf_op jit(solution)/shard_map/convert
  219.9 4.8 %subtract_convert_fusion.2 = (bf16[1,16,512,128]{3,2,1,0:T(8,128)(2,1)S(1)}, bf16[1,16,512,128]{3,2,1,0:T(8,128)(2,1)S(1)}) fusion(f32[2,16,512,128]{3,2,1,0:T(8,128)} %get-tuple-element.119, f32[128]{0:T(128)S(1)} %get-tuple-element.99, f32[128]{0:T(128)S(1)} %get-tuple-element.100), kind=kLoop, calls=%fused_computation.6.clone.1 | loop fusion | flops 8388608 | bytes 12583936 | tf_op jit(solution)/shard_map/convert
  227.8 4.8 %subtract_convert_fusion.2 = (bf16[1,16,512,128]{3,2,1,0:T(8,128)(2,1)S(1)}, bf16[1,16,512,128]{3,2,1,0:T(8,128)(2,1)S(1)}) fusion(f32[2,16,512,128]{3,2,1,0:T(8,128)} %get-tuple-element.119, f32[128]{0:T(128)S(1)} %get-tuple-element.99, f32[128]{0:T(128)S(1)} %get-tuple-element.100), kind=kLoop, calls=%fused_computation.6.clone.1 | loop fusion | flops 8388608 | bytes 12583936 | tf_op jit(solution)/shard_map/convert
  235.8 4.8 %subtract_convert_fusion.2 = (bf16[1,16,512,128]{3,2,1,0:T(8,128)(2,1)S(1)}, bf16[1,16,512,128]{3,2,1,0:T(8,128)(2,1)S(1)}) fusion(f32[2,16,512,128]{3,2,1,0:T(8,128)} %get-tuple-element.119, f32[128]{0:T(128)S(1)} %get-tuple-element.99, f32[128]{0:T(128)S(1)} %get-tuple-element.100), kind=kLoop, calls=%fused_computation.6.clone.1 | loop fusion | flops 8388608 | bytes 12583936 | tf_op jit(solution)/shard_map/convert
  243.8 4.8 %subtract_convert_fusion.2 = (bf16[1,16,512,128]{3,2,1,0:T(8,128)(2,1)S(1)}, bf16[1,16,512,128]{3,2,1,0:T(8,128)(2,1)S(1)}) fusion(f32[2,16,512,128]{3,2,1,0:T(8,128)} %get-tuple-element.119, f32[128]{0:T(128)S(1)} %get-tuple-element.99, f32[128]{0:T(128)S(1)} %get-tuple-element.100), kind=kLoop, calls=%fused_computation.6.clone.1 | loop fusion | flops 8388608 | bytes 12583936 | tf_op jit(solution)/shard_map/convert
  251.7 4.8 %subtract_convert_fusion.2 = (bf16[1,16,512,128]{3,2,1,0:T(8,128)(2,1)S(1)}, bf16[1,16,512,128]{3,2,1,0:T(8,128)(2,1)S(1)}) fusion(f32[2,16,512,128]{3,2,1,0:T(8,128)} %get-tuple-element.119, f32[128]{0:T(128)S(1)} %get-tuple-element.99, f32[128]{0:T(128)S(1)} %get-tuple-element.100), kind=kLoop, calls=%fused_computation.6.clone.1 | loop fusion | flops 8388608 | bytes 12583936 | tf_op jit(solution)/shard_map/convert
  256.6 3.2 fusion.37
  259.7 4.8 %subtract_convert_fusion.2 = (bf16[1,16,512,128]{3,2,1,0:T(8,128)(2,1)S(1)}, bf16[1,16,512,128]{3,2,1,0:T(8,128)(2,1)S(1)}) fusion(f32[2,16,512,128]{3,2,1,0:T(8,128)} %get-tuple-element.119, f32[128]{0:T(128)S(1)} %get-tuple-element.99, f32[128]{0:T(128)S(1)} %get-tuple-element.100), kind=kLoop, calls=%fused_computation.6.clone.1 | loop fusion | flops 8388608 | bytes 12583936 | tf_op jit(solution)/shard_map/convert
  267.7 103.8 %reduce-scatter.2.cloned.1.call-done = bf16[64,12,512]{2,0,1:T(8,128)(2,1)} async-done(((bf16[512,12,512]{2,0,1:T(8,128)(2,1)}), bf16[64,12,512]{2,0,1:T(8,128)(2,1)}) %reduce-scatter.2.cloned.1.call-update) | async-done | bytes 786448 | tf_op jit(solution)/shard_map/reduce_scatter | solution.py:69
  (66 shorter events, 45.1 us)
Async XLA Ops:
  7.3 4.1 %copy-start = (bf16[2,1,16,64,1024]{4,3,2,1,0:T(8,128)(2,1)S(1)}, bf16[2,1,16,64,1024]{4,3,2,1,0:T(8,128)(2,1)}, u32[]{:S(2)}) copy-start(bf16[2,1,16,64,1024]{4,3,2,1,0:T(8,128)(2,1)} %param.5) | copy-start | bytes 12582916
  46.9 12.2 %copy-start.2 = (s32[128]{0:T(128)S(1)}, s32[128]{0:T(128)}, u32[]{:S(2)}) copy-start(s32[128]{0:T(128)} %param.7) | copy-start | bytes 1540
  46.9 113.6 %all-to-all-start = ((bf16[128,2,2,1,64,128]{5,4,2,1,3,0:T(8,128)(2,1)}), bf16[128,2,2,1,64,128]{5,4,2,1,3,0:T(8,128)(2,1)}, u32[]{:S(2)}, u32[]{:S(2)}) async-start(bf16[128,2,2,1,64,128]{5,4,2,1,3,0:T(8,128)(2,1)} %bitcast.57), calls=%async_computation | async-start | bytes 16777216 | tf_op jit(solution)/shard_map/all_to_all | solution.py:54
  58.9 312.6 %reduce-scatter.2.cloned.1.call-start = ((), (), s32[]{:S(2)}) async-start(), calls=%async_computation.2 | async-start | bytes 7077888 | tf_op jit(solution)/shard_map/reduce_scatter | solution.py:69
  172.0 4.8 %copy-start.1 = (bf16[2,16,512,128]{3,2,1,0:T(8,128)(2,1)S(1)}, bf16[2,16,512,128]{3,2,1,0:T(8,128)(2,1)}, u32[]{:S(2)}) copy-start(bf16[2,16,512,128]{3,2,1,0:T(8,128)(2,1)} %get-tuple-element.122) | copy-start | bytes 12582916 | tf_op jit(solution)/shard_map/while
  180.0 4.8 %copy-start.1 = (bf16[2,16,512,128]{3,2,1,0:T(8,128)(2,1)S(1)}, bf16[2,16,512,128]{3,2,1,0:T(8,128)(2,1)}, u32[]{:S(2)}) copy-start(bf16[2,16,512,128]{3,2,1,0:T(8,128)(2,1)} %get-tuple-element.122) | copy-start | bytes 12582916 | tf_op jit(solution)/shard_map/while
  187.9 4.8 %copy-start.1 = (bf16[2,16,512,128]{3,2,1,0:T(8,128)(2,1)S(1)}, bf16[2,16,512,128]{3,2,1,0:T(8,128)(2,1)}, u32[]{:S(2)}) copy-start(bf16[2,16,512,128]{3,2,1,0:T(8,128)(2,1)} %get-tuple-element.122) | copy-start | bytes 12582916 | tf_op jit(solution)/shard_map/while
  195.9 4.8 %copy-start.1 = (bf16[2,16,512,128]{3,2,1,0:T(8,128)(2,1)S(1)}, bf16[2,16,512,128]{3,2,1,0:T(8,128)(2,1)}, u32[]{:S(2)}) copy-start(bf16[2,16,512,128]{3,2,1,0:T(8,128)(2,1)} %get-tuple-element.122) | copy-start | bytes 12582916 | tf_op jit(solution)/shard_map/while
  203.9 4.8 %copy-start.1 = (bf16[2,16,512,128]{3,2,1,0:T(8,128)(2,1)S(1)}, bf16[2,16,512,128]{3,2,1,0:T(8,128)(2,1)}, u32[]{:S(2)}) copy-start(bf16[2,16,512,128]{3,2,1,0:T(8,128)(2,1)} %get-tuple-element.122) | copy-start | bytes 12582916 | tf_op jit(solution)/shard_map/while
  211.9 4.8 %copy-start.1 = (bf16[2,16,512,128]{3,2,1,0:T(8,128)(2,1)S(1)}, bf16[2,16,512,128]{3,2,1,0:T(8,128)(2,1)}, u32[]{:S(2)}) copy-start(bf16[2,16,512,128]{3,2,1,0:T(8,128)(2,1)} %get-tuple-element.122) | copy-start | bytes 12582916 | tf_op jit(solution)/shard_map/while
  219.9 4.8 %copy-start.1 = (bf16[2,16,512,128]{3,2,1,0:T(8,128)(2,1)S(1)}, bf16[2,16,512,128]{3,2,1,0:T(8,128)(2,1)}, u32[]{:S(2)}) copy-start(bf16[2,16,512,128]{3,2,1,0:T(8,128)(2,1)} %get-tuple-element.122) | copy-start | bytes 12582916 | tf_op jit(solution)/shard_map/while
  227.8 4.8 %copy-start.1 = (bf16[2,16,512,128]{3,2,1,0:T(8,128)(2,1)S(1)}, bf16[2,16,512,128]{3,2,1,0:T(8,128)(2,1)}, u32[]{:S(2)}) copy-start(bf16[2,16,512,128]{3,2,1,0:T(8,128)(2,1)} %get-tuple-element.122) | copy-start | bytes 12582916 | tf_op jit(solution)/shard_map/while
  235.8 4.8 %copy-start.1 = (bf16[2,16,512,128]{3,2,1,0:T(8,128)(2,1)S(1)}, bf16[2,16,512,128]{3,2,1,0:T(8,128)(2,1)}, u32[]{:S(2)}) copy-start(bf16[2,16,512,128]{3,2,1,0:T(8,128)(2,1)} %get-tuple-element.122) | copy-start | bytes 12582916 | tf_op jit(solution)/shard_map/while
  243.8 4.8 %copy-start.1 = (bf16[2,16,512,128]{3,2,1,0:T(8,128)(2,1)S(1)}, bf16[2,16,512,128]{3,2,1,0:T(8,128)(2,1)}, u32[]{:S(2)}) copy-start(bf16[2,16,512,128]{3,2,1,0:T(8,128)(2,1)} %get-tuple-element.122) | copy-start | bytes 12582916 | tf_op jit(solution)/shard_map/while
  251.7 4.8 %copy-start.1 = (bf16[2,16,512,128]{3,2,1,0:T(8,128)(2,1)S(1)}, bf16[2,16,512,128]{3,2,1,0:T(8,128)(2,1)}, u32[]{:S(2)}) copy-start(bf16[2,16,512,128]{3,2,1,0:T(8,128)(2,1)} %get-tuple-element.122) | copy-start | bytes 12582916 | tf_op jit(solution)/shard_map/while
  259.7 4.8 %copy-start.1 = (bf16[2,16,512,128]{3,2,1,0:T(8,128)(2,1)S(1)}, bf16[2,16,512,128]{3,2,1,0:T(8,128)(2,1)}, u32[]{:S(2)}) copy-start(bf16[2,16,512,128]{3,2,1,0:T(8,128)(2,1)} %get-tuple-element.122) | copy-start | bytes 12582916 | tf_op jit(solution)/shard_map/while
Sparse Core Ops, SparseCore 0:
  267.8 103.6 reduce-scatter.1
where the time goes:
time: 381 us
  waiting for transfers between devices  205 us (54%)
  other arithmetic  78.8 us (21%)
  matrix products  37.9 us (10%)
  local copies, waits for them, and re-layouts  33.2 us (9%)
  between operations  13.5 us (4%)
  starting transfers between devices  12.2 us (3%)
    reduce_scatter x1, waiting for transfers between devices, body(): lax.psum_scatter(jnp.moveaxis(per_lag, 0, 1).astype(jnp.bfloat16), 'col',...  104 us
    all_to_all x1, waiting for transfers between devices, body(): lax.all_to_all(split_up, ('row', 'col'), split_axis=0, concat_axis=0, til...  101 us
    another operation x12, other arithmetic  57.4 us
    dot_general x12, matrix products, lag_product(): lax.dot_general(turned, right_cols, (((0, 1, 3), (0, 1, 3)), ((), ())), p...  37.9 us
    all_to_all x1, starting transfers between devices, body(): lax.all_to_all(split_up, ('row', 'col'), split_axis=0, concat_axis=0, til...  12 us
    unnamed x6, local copies, waits for them, and re-layouts  9.53 us
    transpose x1, local copies, waits for them, and re-layouts, body(): split_up = jnp.transpose(split_up, (0, 5, 1, 2, 3, 4, 6))  9.14 us
  transfers between devices with their start and end apart: 2, of which 2 were waited for; matrix products, arithmetic and copies ran while one was open for 0% of the time, Pallas kernels for 0%

commit v1 on v0

v1 whole, which is shorter than its diff:
```python
import math

import jax
import jax.numpy as jnp
from jax import lax
from jax.experimental import pallas as pl
from jax.experimental.pallas import tpu as pltpu
from jax.sharding import PartitionSpec as P

L = 8192
LAGS = 12
HALF = LAGS // 2
EPS = 1e-06

NZ = 4
CH = 64
FQ = 256
GROUP = 2
BF = jnp.bfloat16
F32 = jnp.float32


def pack_kernel(sel, first, second, out):
    for core, ref in enumerate((first, second)):
        re = ref[0, 0, 0].astype(F32)
        im = ref[1, 0, 0].astype(F32)
        energy = jnp.mean(re * re + im * im, axis=-1, keepdims=True)
        gain = lax.rsqrt(energy + EPS)
        for comp, val in enumerate((re, im)):
            white = (val * gain).astype(BF)
            for z in range(NZ):
                out[0, core, 0, z, comp, :, 0:128] = white[:, z * 128 : z * 128 + 128]
                out[0, core, 0, z, comp, :, 128:256] = white[:, (z + 4) * 128 : (z + 4) * 128 + 128]


def pack(spectra, sel):
    pairs = sel.shape[0]
    block = (2, 1, 1, CH, 1024)
    return pl.pallas_call(
        pack_kernel,
        grid_spec=pltpu.PrefetchScalarGridSpec(
            num_scalar_prefetch=1,
            grid=(pairs,),
            in_specs=[
                pl.BlockSpec(block, lambda p, sel: (0, 0, sel[p, 0], 0, 0)),
                pl.BlockSpec(block, lambda p, sel: (0, 0, sel[p, 1], 0, 0)),
            ],
            out_specs=pl.BlockSpec(
                (1, 2, 1, NZ, 2, CH, FQ), lambda p, sel: (p // 2, 0, p % 2, 0, 0, 0, 0)
            ),
        ),
        out_shape=jax.ShapeDtypeStruct((8, 2, 2, NZ, 2, CH, FQ), BF),
        compiler_params=pltpu.CompilerParams(vmem_limit_bytes=32 * 2**20),
        cost_estimate=pl.CostEstimate(flops=32 * 2**20, bytes_accessed=16 * 2**20, transcendentals=0),
        name="pack",
    )(sel, spectra, spectra)


def corr_kernel(where, left, right, cos_ref, sin_ref, o0, o1, o2, o3, acc, turned, flipped):
    step = pl.program_id(0)
    width = 2 * GROUP * FQ

    @pl.when(step == 0)
    def _():
        acc[...] = jnp.zeros_like(acc)

    for g in range(GROUP):
        for comp in range(2):
            col = (2 * g + comp) * FQ
            flipped[col : col + FQ, :] = right[g, 0, :, comp].reshape(NZ * CH, FQ).T

    def put(slot, g, dz, re, im):
        rows = slice(dz * CH, dz * CH + CH)
        turned[slot, rows, 2 * g * FQ : (2 * g + 1) * FQ] = re.astype(BF)
        turned[slot, rows, (2 * g + 1) * FQ : (2 * g + 2) * FQ] = im.astype(BF)

    def multiply(slot, lag):
        acc[lag] += jnp.dot(turned[slot], flipped[...], preferred_element_type=F32)

    for m in range(HALF + 1):
        plus = 2 * (m % 2)
        minus = plus + 1
        for g in range(GROUP):
            for dz in range(NZ):
                z = where[2 + dz]
                re = left[g, 0, z, 0]
                im = left[g, 0, z, 1]
                if m == 0:
                    put(plus, g, dz, re, im)
                    continue
                re = re.astype(F32)
                im = im.astype(F32)
                cos = cos_ref[m : m + 1, :]
                sin = sin_ref[m : m + 1, :]
                rc, rs, ic, isn = re * cos, re * sin, im * cos, im * sin
                put(minus, g, dz, rc + isn, ic - rs)
                if m < HALF:
                    put(plus, g, dz, rc - isn, rs + ic)
        if m == 0:
            multiply(plus, HALF)
            continue
        multiply(minus, HALF - m)
        if m < HALF:
            multiply(plus, HALF + m)

    @pl.when(step == pl.num_programs(0) - 1)
    def _():
        for dz, out in enumerate((o0, o1, o2, o3)):
            out[...] = (acc[:, dz * CH : dz * CH + CH, :] * (1.0 / 128.0)).astype(BF)


def corr(where, left, right, right_index, cosine, sine):
    segs = left.shape[0]
    block = (GROUP, 1, NZ, 2, CH, FQ)
    full = lambda s, where: (0, 0)
    piece = jax.ShapeDtypeStruct((LAGS, CH, NZ * CH), BF)
    return pl.pallas_call(
        corr_kernel,
        grid_spec=pltpu.PrefetchScalarGridSpec(
            num_scalar_prefetch=1,
            grid=(segs // GROUP,),
            in_specs=[
                pl.BlockSpec(block, lambda s, where: (s, where[0], 0, 0, 0, 0)),
                pl.BlockSpec(block, right_index),
                pl.BlockSpec(cosine.shape, full),
                pl.BlockSpec(sine.shape, full),
            ],
            out_specs=[pl.BlockSpec(piece.shape, lambda s, where: (0, 0, 0))] * NZ,
            scratch_shapes=[
                pltpu.VMEM((LAGS, NZ * CH, NZ * CH), F32),
                pltpu.VMEM((4, NZ * CH, 2 * GROUP * FQ), BF),
                pltpu.VMEM((2 * GROUP * FQ, NZ * CH), BF),
            ],
        ),
        out_shape=[piece] * NZ,
        compiler_params=pltpu.CompilerParams(vmem_limit_bytes=40 * 2**20),
        cost_estimate=pl.CostEstimate(flops=13 * 10**9, bytes_accessed=12 * 2**20, transcendentals=0),
        name="corr",
    )(where, left, right, cosine, sine)


def total_kernel(where, *refs):
    out = refs[-1]
    own, other = refs[:NZ], refs[NZ : 2 * NZ]
    width = NZ * CH
    for k, group in enumerate((own, other)):
        at = pl.multiple_of(where[k] * width, width)
        for t in range(LAGS):
            val = group[0][t].astype(F32)
            for ref in group[1:]:
                val = val + ref[t].astype(F32)
            out[0, :, t, pl.ds(at, width)] = val


def total(where, parts):
    shape = (1, CH, LAGS, 2 * NZ * CH)
    return pl.pallas_call(
        total_kernel,
        grid_spec=pltpu.PrefetchScalarGridSpec(
            num_scalar_prefetch=1,
            grid=(1,),
            in_specs=[pl.BlockSpec((LAGS, CH, NZ * CH), lambda i, where: (0, 0, 0))] * len(parts),
            out_specs=pl.BlockSpec(shape, lambda i, where: (0, 0, 0, 0)),
        ),
        out_shape=jax.ShapeDtypeStruct(shape, F32),
        compiler_params=pltpu.CompilerParams(vmem_limit_bytes=32 * 2**20),
        name="total",
    )(where, *parts)


def places():
    return [
        (y, xl, c, xh, z)
        for y in range(4)
        for xl in range(2)
        for c in range(2)
        for xh in range(2)
        for z in range(NZ)
    ]


def index(y, xl, c, xh, z):
    return ((y * 2 + xl) * 2 + c) * 8 + xh * 4 + z


def body(spectra, block_pairs, band_bins):
    both = ("row", "col")
    row = lax.axis_index("row")
    col = lax.axis_index("col")
    core = row % 2
    xh = col // 4
    z = col % 4

    sel = jnp.where(xh == 0, block_pairs[:, ::-1], block_pairs)
    packed = pack(spectra, sel).reshape(128, 2, CH, FQ)
    landed = lax.all_to_all(packed, both, split_axis=0, concat_axis=0, tiled=True)
    landed = landed.reshape(16, 2, NZ, 2, CH, FQ)

    bins_there = lax.ppermute(
        band_bins, both, [(index(*p), index(p[0], p[1], p[2], 1 - p[3], p[4])) for p in places()]
    )
    bins = jnp.where(
        xh == 0,
        jnp.concatenate([band_bins, bins_there]),
        jnp.concatenate([bins_there, band_bins]),
    )
    steps = jnp.arange(8, dtype=jnp.int32)
    angle = jnp.mod(bins[None, :] * steps[:, None], L).astype(F32) * (2.0 * math.pi / L)
    cosine, sine = jnp.cos(angle), jnp.sin(angle)

    where = jnp.stack([1 - core, core] + [(z + dz) % NZ for dz in range(NZ)]).astype(jnp.int32)
    mine = lax.dynamic_slice_in_dim(landed, core, 1, axis=1)
    theirs = lax.ppermute(
        mine, both, [(index(*p), index(p[0], p[1], 1 - p[2], p[3], p[4])) for p in places()]
    )

    def send(parts):
        return [
            lax.ppermute(
                part,
                both,
                [(index(*p), index(p[0], p[1], p[3], 1 - p[2], (p[4] + dz) % NZ)) for p in places()],
            )
            for dz, part in enumerate(parts)
        ]

    first = corr(where, landed, landed, lambda s, where: (s, where[1], 0, 0, 0, 0), cosine, sine)
    sent_first = send(first)
    second = corr(where, landed, theirs, lambda s, where: (s, 0, 0, 0, 0, 0), cosine, sine)
    sent_second = send(second)
    halves = jnp.stack([1 - xh, xh]).astype(jnp.int32)
    return total(halves, sent_first + sent_second)


def solution(mesh):
    in_specs = (P(None, "row", None, "col", None), P(), P("col"))
    out_specs = P("row", "col", None, None)
    return jax.shard_map(body, mesh=mesh, in_specs=in_specs, out_specs=out_specs, check_vma=False)
```

time: 381 us -> 216 us (0.57)
  waiting for transfers between devices: 205 us -> 121 us
  other arithmetic: 78.8 us -> 0.15 us
  Pallas kernels: 0 us -> 46.5 us
  matrix products: 37.9 us -> 0 us
  starting transfers between devices: 12.2 us -> 33.1 us
  local copies, waits for them, and re-layouts: 33.2 us -> 13.1 us
  between operations: 13.5 us -> 0.08 us
    reduce_scatter x1 -> x0, waiting for transfers between devices: 104 us -> none  [body(): lax.psum_scatter(jnp.moveaxis(per_lag, 0, 1).astype(jnp.bfloat16), 'col',...]
    another operation x12 -> x1, other arithmetic: 57.4 us -> 0.07 us  [body(): halves = jnp.stack([1 - xh, xh]).astype(jnp.int32)]
    pallas_call x0 -> x4, Pallas kernels: none -> 46.5 us  [the longest x2 39.2 us: corr(): pl.pallas_call(corr_kernel, grid_spec=pltpu.PrefetchScalarGridSpec(num_sc...]
    dot_general x12 -> x0, matrix products: 37.9 us -> none  [lag_product(): lax.dot_general(turned, right_cols, (((0, 1, 3), (0, 1, 3)), ((), ())), p...]
    ppermute x0 -> x10, starting transfers between devices: none -> 21.1 us  [the longest x8 14.4 us: send(): lax.ppermute(part, both, [(index(*p), index(p[0], p[1], p[3], 1 - p[2], (...]
    ppermute x0 -> x10, waiting for transfers between devices: none -> 19.8 us  [the longest x8 16.7 us: send(): lax.ppermute(part, both, [(index(*p), index(p[0], p[1], p[3], 1 - p[2], (...]
    transpose x1 -> x0, local copies, waits for them, and re-layouts: 9.14 us -> none  [body(): split_up = jnp.transpose(split_up, (0, 5, 1, 2, 3, 4, 6))]
    transpose x1 -> x0, other arithmetic: 7.48 us -> none  [body(): split_up = jnp.transpose(split_up, (0, 5, 1, 2, 3, 4, 6))]
  transfers between devices with their start and end apart: 2 -> 11, of which waited for: 2 -> 6; matrix products, arithmetic and copies ran while one was open for 0% -> 0% of each run, Pallas kernels for 0% -> 18%
where the time goes in v1:
time: 216 us; the launch traced here: 214 us
  waiting for transfers between devices  121 us (56%)
  Pallas kernels  46.5 us (22%)
  starting transfers between devices  33.1 us (15%)
  local copies, waits for them, and re-layouts  13.1 us (6%)
    all_to_all x1, waiting for transfers between devices, body(): lax.all_to_all(packed, both, split_axis=0, concat_axis=0, tiled=True)  102 us
    pallas_call x2, Pallas kernels, corr(): pl.pallas_call(corr_kernel, grid_spec=pltpu.PrefetchScalarGridSpec(num_sc...  39.2 us
    ppermute x8, waiting for transfers between devices, send(): lax.ppermute(part, both, [(index(*p), index(p[0], p[1], p[3], 1 - p[2], (...  16.7 us
    ppermute x8, starting transfers between devices, send(): lax.ppermute(part, both, [(index(*p), index(p[0], p[1], p[3], 1 - p[2], (...  14.4 us
    all_to_all x1, starting transfers between devices, body(): lax.all_to_all(packed, both, split_axis=0, concat_axis=0, tiled=True)  12 us
    unnamed x7, local copies, waits for them, and re-layouts  6.19 us
    ppermute x1, starting transfers between devices, body(): lax.ppermute(mine, both, [(index(*p), index(p[0], p[1], 1 - p[2], p[3], p...  6.07 us
    pallas_call x1, Pallas kernels, pack(): pl.pallas_call(pack_kernel, grid_spec=pltpu.PrefetchScalarGridSpec(num_sc...  5.86 us
  transfers between devices with their start and end apart: 11, of which 6 were waited for; matrix products, arithmetic and copies ran while one was open for 0% of the time, Pallas kernels for 18%

profile of v1, /device:TPU:1, one launch (start us, length us, event | category | flops | bytes accessed | tf_op | source)
XLA Modules:
  0.0 214.4 jit_solution(17064942971522476710)
XLA Ops:
  0.0 0.8 copy.4
  0.8 2.2 %copy-done.1 = bf16[2,1,16,64,1024]{4,3,2,1,0:T(8,128)(2,1)S(1)} copy-done((bf16[2,1,16,64,1024]{4,3,2,1,0:T(8,128)(2,1)S(1)}, bf16[2,1,16,64,1024]{4,3,2,1,0:T(8,128)(2,1)}, u32[]{:S(2)}) %copy-start.1) | copy-done | bytes 4194328
  3.0 5.9 %pack.1 = bf16[8,2,2,4,2,64,256]{6,5,4,3,2,1,0:T(8,128)(2,1)S(1)} custom-call(s32[16,2]{1,0:T(8,128)S(1)} %broadcast_select_fusion.sel, bf16[2,1,16,64,1024]{4,3,2,1,0:T(8,128)(2,1)S(1)} %copy-done.1, bf16[2,1,16,64,1024]{4,3,2,1,0:T(8,128)(2,1)S(1)} %copy-done.1), custom_call_target="tpu_custom_call" | custom-call | flops 33554432 | bytes 16777216 | tf_op jit(solution)/shard_map/pack/pallas_call | solution.py:39
  8.9 3.2 %copy-done = bf16[8,2,2,4,2,64,256]{6,5,4,3,2,1,0:T(8,128)(2,1)} copy-done((bf16[8,2,2,4,2,64,256]{6,5,4,3,2,1,0:T(8,128)(2,1)}, bf16[8,2,2,4,2,64,256]{6,5,4,3,2,1,0:T(8,128)(2,1)S(1)}, u32[]{:S(2)}) %copy-start) | copy-done | bytes 8388632
  12.1 12.0 %all-to-all-start = ((bf16[128,2,64,256]{3,2,1,0:T(8,128)(2,1)}), bf16[128,2,64,256]{3,2,1,0:T(8,128)(2,1)}, u32[]{:S(2)}, u32[]{:S(2)}) async-start(bf16[128,2,64,256]{3,2,1,0:T(8,128)(2,1)} %bitcast.10), calls=%async_computation | async-start | bytes 16777216 | tf_op jit(solution)/shard_map/all_to_all | solution.py:196
  24.1 101.6 %all-to-all-done = bf16[128,2,64,256]{3,2,1,0:T(8,128)(2,1)} async-done(((bf16[128,2,64,256]{3,2,1,0:T(8,128)(2,1)}), bf16[128,2,64,256]{3,2,1,0:T(8,128)(2,1)}, u32[]{:S(2)}, u32[]{:S(2)}) %all-to-all-start) | async-done | bytes 8388640 | tf_op jit(solution)/shard_map/all_to_all | solution.py:196
  125.8 4.7 %constant_dynamic-slice_fusion = bf16[16,1,4,2,64,256]{5,4,3,2,1,0:T(8,128)(2,1)} fusion(bf16[16,2,4,2,64,256]{5,4,3,2,1,0:T(8,128)(2,1)} %bitcast.9.left.right, s32[]{:T(128)S(6)} %select_n.72), kind=kLoop, calls=%fused_computation.14 | loop fusion | bytes 8388612 | tf_op jit(solution)/shard_map/dynamic_slice | solution.py:212
  130.5 6.1 %collective-permute-start.5 = (bf16[16,1,4,2,64,256]{5,4,3,2,1,0:T(8,128)(2,1)}, bf16[16,1,4,2,64,256]{5,4,3,2,1,0:T(8,128)(2,1)}, u32[]{:S(2)}, u32[]{:S(2)}) collective-permute-start(bf16[16,1,4,2,64,256]{5,4,3,2,1,0:T(8,128)(2,1)} %constant_dynamic-slice_fusion), channel_id=1, source_target_pairs={{0,8},{1,9},{2,10},{3,11},{4,12},{5,13},{6,14},{7,15},{8,0},{9,1},... | collective-permute-start | bytes 12582920 | tf_op jit(solution)/shard_map/ppermute | solution.py:213
  136.6 0.7 collective-permute-start
  137.2 0.1 stack.39.where
  137.3 3.1 %collective-permute-done = s32[128]{0:T(128)S(1)} collective-permute-done((s32[128]{0:T(128)S(1)}, s32[128]{0:T(128)S(1)}, u32[]{:S(2)}, u32[]{:S(2)}) %collective-permute-start) | collective-permute-done | bytes 544 | tf_op jit(solution)/shard_map/ppermute | solution.py:199
  140.5 19.1 %corr.2 = (bf16[12,64,256]{2,1,0:T(8,128)(2,1)S(1)}, bf16[12,64,256]{2,1,0:T(8,128)(2,1)S(1)}, bf16[12,64,256]{2,1,0:T(8,128)(2,1)S(1)}, bf16[12,64,256]{2,1,0:T(8,128)(2,1)S(1)}) custom-call(s32[6]{0:T(128)S(1)} %stack.39.where, bf16[16,2,4,2,64,256]{5,4,3,2,1,0:T(8,128)(2,1)} %bitcast.9.left.right, bf16[16,2,4,2,64,256]{5,4,3,2,1,0:T(8,128)(2,1)} %bitcast.9.left.right, ...), custom_call_target="tpu_custom_call" | custom-call | flops 12999999488 | bytes 12582912 | tf_op jit(solution)/shard_map/corr/pallas_call | solution.py:117
  159.6 1.2 collective-permute-start.1
  160.8 0.1 collective-permute-start.2
  160.9 5.9 %collective-permute-start.3 = (bf16[12,64,256]{2,1,0:T(8,128)(2,1)S(1)}, bf16[12,64,256]{2,1,0:T(8,128)(2,1)S(1)}, u32[]{:S(2)}, u32[]{:S(2)}) collective-permute-start(bf16[12,64,256]{2,1,0:T(8,128)(2,1)S(1)} %get-tuple-element.15), channel_id=1, source_target_pairs={{0,6},{1,7},{2,4},{3,5},{4,14},{5,15},{6,12},{7,13},{8,2},{9,3},{1... | collective-permute-start | bytes 1179656 | tf_op jit(solution)/shard_map/ppermute | solution.py:219
  166.8 20.2 %corr.3 = (bf16[12,64,256]{2,1,0:T(8,128)(2,1)}, bf16[12,64,256]{2,1,0:T(8,128)(2,1)}, bf16[12,64,256]{2,1,0:T(8,128)(2,1)}, bf16[12,64,256]{2,1,0:T(8,128)(2,1)}) custom-call(s32[6]{0:T(128)S(1)} %stack.39.where, bf16[16,2,4,2,64,256]{5,4,3,2,1,0:T(8,128)(2,1)} %bitcast.9.left.right, bf16[16,1,4,2,64,256]{5,4,3,2,1,0:T(8,128)(2,1)} %collective-permute-done.5.right, ...), custom_call_target="tpu_custom_call" | custom-call | flops 12999999488 | bytes 12582912 | tf_op jit(solution)/shard_map/corr/pallas_call | solution.py:117
  187.0 4.9 %collective-permute-start.7 = (bf16[12,64,256]{2,1,0:T(8,128)(2,1)}, bf16[12,64,256]{2,1,0:T(8,128)(2,1)S(1)}, u32[]{:S(2)}, u32[]{:S(2)}) collective-permute-start(bf16[12,64,256]{2,1,0:T(8,128)(2,1)} %get-tuple-element.18), channel_id=1, source_target_pairs={{0,5},{1,6},{2,7},{3,4},{4,13},{5,14},{6,15},{7,12},{8,1},{9,2},{1... | collective-permute-start | bytes 1179656 | tf_op jit(solution)/shard_map/ppermute | solution.py:219
  191.9 2.3 %collective-permute-start.9 = (bf16[12,64,256]{2,1,0:T(8,128)(2,1)}, bf16[12,64,256]{2,1,0:T(8,128)(2,1)S(1)}, u32[]{:S(2)}, u32[]{:S(2)}) collective-permute-start(bf16[12,64,256]{2,1,0:T(8,128)(2,1)} %get-tuple-element.20), channel_id=1, source_target_pairs={{0,7},{1,4},{2,5},{3,6},{4,15},{5,12},{6,13},{7,14},{8,3},{9,0},{1... | collective-permute-start | bytes 1179656 | tf_op jit(solution)/shard_map/ppermute | solution.py:219
  194.2 1.1 collective-permute-done.6.refs_4_
  195.3 10.0 %collective-permute-done.7.refs_5_ = bf16[12,64,256]{2,1,0:T(8,128)(2,1)S(1)} collective-permute-done((bf16[12,64,256]{2,1,0:T(8,128)(2,1)}, bf16[12,64,256]{2,1,0:T(8,128)(2,1)S(1)}, u32[]{:S(2)}, u32[]{:S(2)}) %collective-permute-start.7) | collective-permute-done | bytes 393248 | tf_op jit(solution)/shard_map/ppermute | solution.py:219
  205.3 4.2 %collective-permute-done.8.refs_6_ = bf16[12,64,256]{2,1,0:T(8,128)(2,1)S(1)} collective-permute-done((bf16[12,64,256]{2,1,0:T(8,128)(2,1)}, bf16[12,64,256]{2,1,0:T(8,128)(2,1)S(1)}, u32[]{:S(2)}, u32[]{:S(2)}) %collective-permute-start.8) | collective-permute-done | bytes 393248 | tf_op jit(solution)/shard_map/ppermute | solution.py:219
  209.5 1.3 collective-permute-done.9.refs_7_
  210.9 1.4 total.1
  212.3 2.1 copy.6
  (17 shorter events, 0.3 us)
Async XLA Ops:
  0.8 2.2 %copy-start.1 = (bf16[2,1,16,64,1024]{4,3,2,1,0:T(8,128)(2,1)S(1)}, bf16[2,1,16,64,1024]{4,3,2,1,0:T(8,128)(2,1)}, u32[]{:S(2)}) copy-start(bf16[2,1,16,64,1024]{4,3,2,1,0:T(8,128)(2,1)} %second.1) | copy-start | bytes 12582916
  8.9 3.2 %copy-start = (bf16[8,2,2,4,2,64,256]{6,5,4,3,2,1,0:T(8,128)(2,1)}, bf16[8,2,2,4,2,64,256]{6,5,4,3,2,1,0:T(8,128)(2,1)S(1)}, u32[]{:S(2)}) copy-start(bf16[8,2,2,4,2,64,256]{6,5,4,3,2,1,0:T(8,128)(2,1)S(1)} %pack.1) | copy-start | bytes 25165828
  12.1 113.6 %all-to-all-start = ((bf16[128,2,64,256]{3,2,1,0:T(8,128)(2,1)}), bf16[128,2,64,256]{3,2,1,0:T(8,128)(2,1)}, u32[]{:S(2)}, u32[]{:S(2)}) async-start(bf16[128,2,64,256]{3,2,1,0:T(8,128)(2,1)} %bitcast.10), calls=%async_computation | async-start | bytes 16777216 | tf_op jit(solution)/shard_map/all_to_all | solution.py:196
  125.8 10.8 %copy-start.2 = (s32[128]{0:T(128)S(1)}, s32[128]{0:T(128)}, u32[]{:S(2)}) copy-start(s32[128]{0:T(128)} %param.5) | copy-start | bytes 1540
  130.5 36.3 %collective-permute-start.5 = (bf16[16,1,4,2,64,256]{5,4,3,2,1,0:T(8,128)(2,1)}, bf16[16,1,4,2,64,256]{5,4,3,2,1,0:T(8,128)(2,1)}, u32[]{:S(2)}, u32[]{:S(2)}) collective-permute-start(bf16[16,1,4,2,64,256]{5,4,3,2,1,0:T(8,128)(2,1)} %constant_dynamic-slice_fusion), channel_id=1, source_target_pairs={{0,8},{1,9},{2,10},{3,11},{4,12},{5,13},{6,14},{7,15},{8,0},{9,1},... | collective-permute-start | bytes 12582920 | tf_op jit(solution)/shard_map/ppermute | solution.py:213
  136.6 3.9 %collective-permute-start = (s32[128]{0:T(128)S(1)}, s32[128]{0:T(128)S(1)}, u32[]{:S(2)}, u32[]{:S(2)}) collective-permute-start(s32[128]{0:T(128)S(1)} %copy-done.2), channel_id=1, source_target_pairs={{0,4},{1,5},{2,6},{3,7},{4,0},{5,1},{6,2},{7,3},{8,12},{9,13},{10,... | collective-permute-start | bytes 1544 | tf_op jit(solution)/shard_map/ppermute | solution.py:199
  159.6 27.4 %collective-permute-start.1 = (bf16[12,64,256]{2,1,0:T(8,128)(2,1)S(1)}, bf16[12,64,256]{2,1,0:T(8,128)(2,1)S(1)}, u32[]{:S(2)}, u32[]{:S(2)}) collective-permute-start(bf16[12,64,256]{2,1,0:T(8,128)(2,1)S(1)} %get-tuple-element.13), channel_id=1, source_target_pairs={{0,4},{1,5},{2,6},{3,7},{4,12},{5,13},{6,14},{7,15},{8,0},{9,1},{1... | collective-permute-start | bytes 1179656 | tf_op jit(solution)/shard_map/ppermute | solution.py:219
  160.8 31.0 %collective-permute-start.2 = (bf16[12,64,256]{2,1,0:T(8,128)(2,1)S(1)}, bf16[12,64,256]{2,1,0:T(8,128)(2,1)S(1)}, u32[]{:S(2)}, u32[]{:S(2)}) collective-permute-start(bf16[12,64,256]{2,1,0:T(8,128)(2,1)S(1)} %get-tuple-element.14), channel_id=1, source_target_pairs={{0,5},{1,6},{2,7},{3,4},{4,13},{5,14},{6,15},{7,12},{8,1},{9,2},{1... | collective-permute-start | bytes 1179656 | tf_op jit(solution)/shard_map/ppermute | solution.py:219
  160.9 31.0 %collective-permute-start.3 = (bf16[12,64,256]{2,1,0:T(8,128)(2,1)S(1)}, bf16[12,64,256]{2,1,0:T(8,128)(2,1)S(1)}, u32[]{:S(2)}, u32[]{:S(2)}) collective-permute-start(bf16[12,64,256]{2,1,0:T(8,128)(2,1)S(1)} %get-tuple-element.15), channel_id=1, source_target_pairs={{0,6},{1,7},{2,4},{3,5},{4,14},{5,15},{6,12},{7,13},{8,2},{9,3},{1... | collective-permute-start | bytes 1179656 | tf_op jit(solution)/shard_map/ppermute | solution.py:219
  166.8 27.5 %collective-permute-start.4 = (bf16[12,64,256]{2,1,0:T(8,128)(2,1)S(1)}, bf16[12,64,256]{2,1,0:T(8,128)(2,1)S(1)}, u32[]{:S(2)}, u32[]{:S(2)}) collective-permute-start(bf16[12,64,256]{2,1,0:T(8,128)(2,1)S(1)} %get-tuple-element.16), channel_id=1, source_target_pairs={{0,7},{1,4},{2,5},{3,6},{4,15},{5,12},{6,13},{7,14},{8,3},{9,0},{1... | collective-permute-start | bytes 1179656 | tf_op jit(solution)/shard_map/ppermute | solution.py:219
  187.0 8.3 %collective-permute-start.6 = (bf16[12,64,256]{2,1,0:T(8,128)(2,1)}, bf16[12,64,256]{2,1,0:T(8,128)(2,1)S(1)}, u32[]{:S(2)}, u32[]{:S(2)}) collective-permute-start(bf16[12,64,256]{2,1,0:T(8,128)(2,1)} %get-tuple-element.17), channel_id=1, source_target_pairs={{0,4},{1,5},{2,6},{3,7},{4,12},{5,13},{6,14},{7,15},{8,0},{9,1},{1... | collective-permute-start | bytes 1179656 | tf_op jit(solution)/shard_map/ppermute | solution.py:219
  187.0 18.4 %collective-permute-start.7 = (bf16[12,64,256]{2,1,0:T(8,128)(2,1)}, bf16[12,64,256]{2,1,0:T(8,128)(2,1)S(1)}, u32[]{:S(2)}, u32[]{:S(2)}) collective-permute-start(bf16[12,64,256]{2,1,0:T(8,128)(2,1)} %get-tuple-element.18), channel_id=1, source_target_pairs={{0,5},{1,6},{2,7},{3,4},{4,13},{5,14},{6,15},{7,12},{8,1},{9,2},{1... | collective-permute-start | bytes 1179656 | tf_op jit(solution)/shard_map/ppermute | solution.py:219
  191.9 17.7 %collective-permute-start.8 = (bf16[12,64,256]{2,1,0:T(8,128)(2,1)}, bf16[12,64,256]{2,1,0:T(8,128)(2,1)S(1)}, u32[]{:S(2)}, u32[]{:S(2)}) collective-permute-start(bf16[12,64,256]{2,1,0:T(8,128)(2,1)} %get-tuple-element.19), channel_id=1, source_target_pairs={{0,6},{1,7},{2,4},{3,5},{4,14},{5,15},{6,12},{7,13},{8,2},{9,3},{1... | collective-permute-start | bytes 1179656 | tf_op jit(solution)/shard_map/ppermute | solution.py:219
  191.9 19.0 %collective-permute-start.9 = (bf16[12,64,256]{2,1,0:T(8,128)(2,1)}, bf16[12,64,256]{2,1,0:T(8,128)(2,1)S(1)}, u32[]{:S(2)}, u32[]{:S(2)}) collective-permute-start(bf16[12,64,256]{2,1,0:T(8,128)(2,1)} %get-tuple-element.20), channel_id=1, source_target_pairs={{0,7},{1,4},{2,5},{3,6},{4,15},{5,12},{6,13},{7,14},{8,3},{9,0},{1... | collective-permute-start | bytes 1179656 | tf_op jit(solution)/shard_map/ppermute | solution.py:219

commit v2 on v1

v2 whole, which is shorter than its diff:
```python
import functools
import math

import jax
import jax.numpy as jnp
from jax import lax
from jax.experimental import pallas as pl
from jax.experimental.pallas import tpu as pltpu
from jax.sharding import PartitionSpec as P

L = 8192
LAGS = 12
HALF = LAGS // 2
EPS = 1e-06

NZ = 4
CH = 64
FB = 128
NB = 1024 // FB
BF = jnp.bfloat16
F32 = jnp.float32


def pack_kernel(group, sel, block, low, high, white, sems):
    step = pl.program_id(0)
    for g in range(group):
        re = block[0, 0, g].astype(F32)
        im = block[1, 0, g].astype(F32)
        energy = jnp.mean(re * re + im * im, axis=-1, keepdims=True)
        gain = lax.rsqrt(energy + EPS)
        for comp, val in enumerate((re, im)):
            scaled = (val * gain).astype(BF)
            for k in range(NB):
                white[step * group + g, k, comp] = scaled[:, k * FB : (k + 1) * FB]

    def copies(pair, core):
        return [
            pltpu.make_async_copy(
                white.at[sel[pair, core], pl.ds(part * NZ, NZ)],
                out.at[pair // 2, core, pair % 2],
                sems.at[part, pair, core],
            )
            for part, out in enumerate((low, high))
        ]

    for pair in range(16):
        for core in range(2):

            @pl.when(sel[pair, core] // group == step)
            def _(pair=pair, core=core):
                for copy in copies(pair, core):
                    copy.start()

    @pl.when(step == pl.num_programs(0) - 1)
    def _():
        for pair in range(16):
            for core in range(2):
                for copy in copies(pair, core):
                    copy.wait()


def pack(spectra, sel):
    blocks = spectra.shape[2]
    group = 4
    out = jax.ShapeDtypeStruct((8, 2, 2, NZ, 2, CH, FB), BF)
    return pl.pallas_call(
        functools.partial(pack_kernel, group),
        grid_spec=pltpu.PrefetchScalarGridSpec(
            num_scalar_prefetch=1,
            grid=(blocks // group,),
            in_specs=[pl.BlockSpec((2, 1, group, CH, 1024), lambda p, sel: (0, 0, p, 0, 0))],
            out_specs=[pl.BlockSpec(memory_space=pl.ANY)] * 2,
            scratch_shapes=[
                pltpu.VMEM((blocks, NB, 2, CH, FB), BF),
                pltpu.SemaphoreType.DMA((2, 16, 2)),
            ],
        ),
        out_shape=[out] * 2,
        compiler_params=pltpu.CompilerParams(vmem_limit_bytes=60 * 2**20),
        cost_estimate=pl.CostEstimate(flops=16 * 2**20, bytes_accessed=12 * 2**20, transcendentals=0),
        name="pack",
    )(sel, spectra)


def turn_and_multiply(group, where, left, rights, cos_ref, sin_ref, even, odd, flipped, add):
    rows_all = NZ * CH

    def col(g, comp):
        return slice((2 * g + comp) * FB, (2 * g + comp + 1) * FB)

    for g in range(group):
        for comp in range(2):
            for h, right in enumerate(rights):
                block = right[g, 0, :, comp].reshape(rows_all, FB)
                flipped[col(g, comp), h * rows_all : (h + 1) * rows_all] = block.T

    def turn(m, turned, both):
        cos = jnp.broadcast_to(cos_ref[pl.ds(m, 1), :], (CH, FB)).astype(BF)
        sin = jnp.broadcast_to(sin_ref[pl.ds(m, 1), :], (CH, FB)).astype(BF)
        for g in range(group):
            for dz in range(NZ):
                z = where[2 + dz]
                re = left[g, 0, z, 0]
                im = left[g, 0, z, 1]
                rc, rs, ic, isn = re * cos, re * sin, im * cos, im * sin
                rows = slice(dz * CH, dz * CH + CH)
                more = slice(rows_all + dz * CH, rows_all + dz * CH + CH)
                turned[rows, col(g, 0)] = rc + isn
                turned[rows, col(g, 1)] = ic - rs
                turned[more, col(g, 0)] = rc - isn if both else re
                turned[more, col(g, 1)] = rs + ic if both else im

    def multiply(m, turned):
        product = jnp.dot(turned[...], flipped[...], preferred_element_type=F32)
        add(HALF - m if isinstance(m, int) else jnp.where(m == 0, 0, HALF - m), product[:rows_all])
        add(HALF + m, product[rows_all:])

    turn(HALF, even, False)

    def step(i, carry):
        m = 2 * i + 1
        turn(m, odd, True)
        multiply(m - 1, even)
        turn(m + 1, even, True)
        multiply(m, odd)
        return carry

    lax.fori_loop(0, 2, step, 0)
    turn(HALF - 1, odd, True)
    multiply(HALF - 2, even)
    multiply(HALF - 1, odd)


def first_kernel(group, where, left, own, other, cos_ref, sin_ref, own_sum, other_sum, even, odd, flipped):
    @pl.when(pl.program_id(0) == 0)
    def _():
        own_sum[...] = jnp.zeros_like(own_sum)
        other_sum[...] = jnp.zeros_like(other_sum)

    def add(lag, product):
        own_sum[lag] += product[:, : NZ * CH]
        other_sum[lag] += product[:, NZ * CH :]

    turn_and_multiply(group, where, left, (own, other), cos_ref, sin_ref, even, odd, flipped, add)


def second_kernel(group, where, left, right, cos_ref, sin_ref, before, o0, o1, o2, o3, even, odd, flipped):
    def add(lag, product):
        for dz, out in enumerate((o0, o1, o2, o3)):
            rows = slice(dz * CH, dz * CH + CH)
            out[lag] = ((before[lag, rows] + product[rows]) * (1.0 / 128.0)).astype(BF)

    turn_and_multiply(group, where, left, (right,), cos_ref, sin_ref, even, odd, flipped, add)


SUMS = (LAGS, NZ * CH, NZ * CH)


def spec(group, at=None):
    index_map = (lambda s, where: (s, 0, 0, 0, 0, 0)) if at is None else (lambda s, where: (s, where[at], 0, 0, 0, 0))
    return pl.BlockSpec((group, 1, NZ, 2, CH, FB), index_map)


def table_spec():
    return pl.BlockSpec((8, FB), lambda s, where: (0, 0))


def whole(shape):
    return pl.BlockSpec(shape, lambda s, where: (0, 0, 0))


def first_half(where, landed, theirs, cosine, sine):
    group = 8
    return pl.pallas_call(
        functools.partial(first_kernel, group),
        grid_spec=pltpu.PrefetchScalarGridSpec(
            num_scalar_prefetch=1,
            grid=(landed.shape[0] // group,),
            in_specs=[spec(group, 0), spec(group, 1), spec(group), table_spec(), table_spec()],
            out_specs=[whole(SUMS)] * 2,
            scratch_shapes=[
                pltpu.VMEM((2 * NZ * CH, 2 * group * FB), BF),
                pltpu.VMEM((2 * NZ * CH, 2 * group * FB), BF),
                pltpu.VMEM((2 * group * FB, 2 * NZ * CH), BF),
            ],
        ),
        out_shape=[jax.ShapeDtypeStruct(SUMS, F32)] * 2,
        compiler_params=pltpu.CompilerParams(vmem_limit_bytes=40 * 2**20),
        cost_estimate=pl.CostEstimate(flops=13 * 10**9, bytes_accessed=12 * 2**20, transcendentals=0),
        name="first_half",
    )(where, landed, landed, theirs, cosine, sine)


def second_half(where, landed, right, at, cosine, sine, before):
    group = landed.shape[0]
    piece = jax.ShapeDtypeStruct((LAGS, CH, NZ * CH), BF)
    return pl.pallas_call(
        functools.partial(second_kernel, group),
        grid_spec=pltpu.PrefetchScalarGridSpec(
            num_scalar_prefetch=1,
            grid=(1,),
            in_specs=[spec(group, 0), spec(group, at), table_spec(), table_spec(), whole(SUMS)],
            out_specs=[whole(piece.shape)] * NZ,
            scratch_shapes=[
                pltpu.VMEM((2 * NZ * CH, 2 * group * FB), BF),
                pltpu.VMEM((2 * NZ * CH, 2 * group * FB), BF),
                pltpu.VMEM((2 * group * FB, NZ * CH), BF),
            ],
        ),
        out_shape=[piece] * NZ,
        compiler_params=pltpu.CompilerParams(vmem_limit_bytes=40 * 2**20),
        cost_estimate=pl.CostEstimate(flops=65 * 10**8, bytes_accessed=8 * 2**20, transcendentals=0),
        name="second_half",
    )(where, landed, right, cosine, sine, before)


def total_kernel(where, *refs):
    out = refs[-1]
    own, other = refs[:NZ], refs[NZ : 2 * NZ]
    width = NZ * CH
    for k, group in enumerate((own, other)):
        at = pl.multiple_of(where[k] * width, width)
        for t in range(LAGS):
            val = group[0][t].astype(F32)
            for ref in group[1:]:
                val = val + ref[t].astype(F32)
            out[0, t, :, pl.ds(at, width)] = val


def total(where, parts):
    shape = (1, LAGS, CH, 2 * NZ * CH)
    return pl.pallas_call(
        total_kernel,
        grid_spec=pltpu.PrefetchScalarGridSpec(
            num_scalar_prefetch=1,
            grid=(1,),
            in_specs=[pl.BlockSpec((LAGS, CH, NZ * CH), lambda i, where: (0, 0, 0))] * len(parts),
            out_specs=pl.BlockSpec(shape, lambda i, where: (0, 0, 0, 0)),
        ),
        out_shape=jax.ShapeDtypeStruct(shape, F32),
        compiler_params=pltpu.CompilerParams(vmem_limit_bytes=32 * 2**20),
        name="total",
    )(where, *parts)


def places():
    return [
        (y, xl, c, xh, z)
        for y in range(4)
        for xl in range(2)
        for c in range(2)
        for xh in range(2)
        for z in range(NZ)
    ]


def index(y, xl, c, xh, z):
    return ((y * 2 + xl) * 2 + c) * 8 + xh * 4 + z


def body(spectra, block_pairs, band_bins):
    both = ("row", "col")
    row = lax.axis_index("row")
    col = lax.axis_index("col")
    core = row % 2
    xh = col // 4
    z = col % 4

    bins_there = lax.ppermute(
        band_bins, both, [(index(*p), index(p[0], p[1], p[2], 1 - p[3], p[4])) for p in places()]
    )
    low = jnp.where(xh == 0, band_bins, bins_there)
    high = jnp.where(xh == 0, bins_there, band_bins)
    steps = jnp.arange(8, dtype=jnp.int32)
    angle = jnp.mod(jnp.stack([low, high])[:, None, :] * steps[:, None], L).astype(F32) * (2.0 * math.pi / L)
    cosine, sine = jnp.cos(angle), jnp.sin(angle)

    sel = jnp.where(xh == 0, block_pairs[:, ::-1], block_pairs)
    where = jnp.stack([1 - core, core] + [(z + dz) % NZ for dz in range(NZ)]).astype(jnp.int32)
    halves = jnp.stack([1 - xh, xh]).astype(jnp.int32)

    def swap(mine):
        return lax.ppermute(
            mine, both, [(index(*p), index(p[0], p[1], 1 - p[2], p[3], p[4])) for p in places()]
        )

    def exchange(packed):
        landed = lax.all_to_all(packed.reshape(128, 2, CH, FB), both, split_axis=0, concat_axis=0, tiled=True)
        landed = landed.reshape(16, 2, NZ, 2, CH, FB)
        return landed, swap(lax.dynamic_slice_in_dim(landed, core, 1, axis=1))

    def send(parts):
        return [
            lax.ppermute(
                part,
                both,
                [(index(*p), index(p[0], p[1], p[3], 1 - p[2], (p[4] + dz) % NZ)) for p in places()],
            )
            for dz, part in enumerate(parts)
        ]

    packed0, packed1 = pack(spectra, sel)
    packed1, cosine, sine, where, halves = lax.optimization_barrier((packed1, cosine, sine, where, halves))
    landed0, theirs0 = exchange(packed0)
    own, other = first_half(where, landed0, theirs0, cosine[0], sine[0])
    landed1 = lax.all_to_all(packed1.reshape(128, 2, CH, FB), both, split_axis=0, concat_axis=0, tiled=True)
    landed1, own, other = lax.optimization_barrier((landed1, own, other))
    landed1 = landed1.reshape(16, 2, NZ, 2, CH, FB)
    theirs1 = swap(lax.dynamic_slice_in_dim(landed1, core, 1, axis=1))
    first = send(second_half(where, landed1, landed1, 1, cosine[1], sine[1], own))
    second = send(second_half(where, landed1, theirs1, None, cosine[1], sine[1], other))
    return jnp.transpose(total(halves, first + second), (0, 2, 1, 3))


def solution(mesh):
    in_specs = (P(None, "row", None, "col", None), P(), P("col"))
    out_specs = P("row", "col", None, None)
    return jax.shard_map(body, mesh=mesh, in_specs=in_specs, out_specs=out_specs, check_vma=False)
```

time: 216 us -> 193 us (0.89)
  waiting for transfers between devices: 121 us -> 89.4 us
  Pallas kernels: 46.5 us -> 54.7 us
  starting transfers between devices: 33.1 us -> 40.8 us
  local copies, waits for them, and re-layouts: 13.1 us -> 6.26 us
    all_to_all x1 -> x2, waiting for transfers between devices: 102 us -> 26.5 us  [the longest x1 23.3 us: body(): lax.all_to_all(packed1.reshape(128, 2, CH, FB), both, split_axis=0, conca...]
    ppermute x1, waiting for transfers between devices: 3.12 us -> 44.4 us  [body(): lax.ppermute(band_bins, both, [(index(*p), index(p[0], p[1], p[2], 1 - p[...]
    all_to_all x1 -> x2, starting transfers between devices: 12 us -> 20.1 us  [the longest x1 12 us: exchange(): lax.all_to_all(packed.reshape(128, 2, CH, FB), both, split_axis=0, concat...]
    pallas_call x3 -> x4, Pallas kernels: 45.1 us -> 52.6 us  [the longest x2 25.8 us: second_half(): pl.pallas_call(functools.partial(second_kernel, group), grid_spec=pltpu.P...]
    ppermute x1 -> x2, waiting for transfers between devices: 0.01 us -> 3.79 us  [swap(): lax.ppermute(mine, both, [(index(*p), index(p[0], p[1], 1 - p[2], p[3], p...]
    unnamed x7, local copies, waits for them, and re-layouts: 6.19 us -> 2.44 us
    ppermute x1, starting transfers between devices: 0.69 us -> 2.97 us  [body(): lax.ppermute(band_bins, both, [(index(*p), index(p[0], p[1], p[2], 1 - p[...]
    ppermute x1 -> x2, starting transfers between devices: 6.07 us -> 3.94 us  [swap(): lax.ppermute(mine, both, [(index(*p), index(p[0], p[1], 1 - p[2], p[3], p...]
  transfers between devices with their start and end apart: 11 -> 13, of which waited for: 6 -> 7; matrix products, arithmetic and copies ran while one was open for 0% -> 1% of each run, Pallas kernels for 18% -> 23%
where the time goes in v2:
time: 193 us; the launch traced here: 192 us
  waiting for transfers between devices  89.4 us (46%)
  Pallas kernels  54.7 us (28%)
  starting transfers between devices  40.8 us (21%)
  local copies, waits for them, and re-layouts  6.26 us (3%)
    ppermute x1, waiting for transfers between devices, body(): lax.ppermute(band_bins, both, [(index(*p), index(p[0], p[1], p[2], 1 - p[...  44.4 us
    pallas_call x2, Pallas kernels, second_half(): pl.pallas_call(functools.partial(second_kernel, group), grid_spec=pltpu.P...  25.8 us
    all_to_all x1, waiting for transfers between devices, body(): lax.all_to_all(packed1.reshape(128, 2, CH, FB), both, split_axis=0, conca...  23.3 us
    pallas_call x1, Pallas kernels, first_half(): pl.pallas_call(functools.partial(first_kernel, group), grid_spec=pltpu.Pr...  19.1 us
    ppermute x8, waiting for transfers between devices, send(): lax.ppermute(part, both, [(index(*p), index(p[0], p[1], p[3], 1 - p[2], (...  14.7 us
    ppermute x8, starting transfers between devices, send(): lax.ppermute(part, both, [(index(*p), index(p[0], p[1], p[3], 1 - p[2], (...  13.8 us
    all_to_all x1, starting transfers between devices, exchange(): lax.all_to_all(packed.reshape(128, 2, CH, FB), both, split_axis=0, concat...  12 us
    all_to_all x1, starting transfers between devices, body(): lax.all_to_all(packed1.reshape(128, 2, CH, FB), both, split_axis=0, conca...  8.17 us
  transfers between devices with their start and end apart: 13, of which 7 were waited for; matrix products, arithmetic and copies ran while one was open for 1% of the time, Pallas kernels for 23%

profile of v2, /device:TPU:1, one launch (start us, length us, event | category | flops | bytes accessed | tf_op | source)
XLA Modules:
  0.0 192.0 jit_solution(10352592131336072101)
XLA Ops:
  1.4 7.8 %pack.1 = (bf16[8,2,2,4,2,64,128]{6,5,4,3,2,1,0:T(8,128)(2,1)}, bf16[8,2,2,4,2,64,128]{6,5,4,3,2,1,0:T(8,128)(2,1)}) custom-call(s32[16,2]{1,0:T(8,128)} %broadcast_select_fusion.sel, bf16[2,1,16,64,1024]{4,3,2,1,0:T(8,128)(2,1)} %block.1), custom_call_target="tpu_custom_call" | custom-call | flops 16777216 | bytes 12582912 | tf_op jit(solution)/shard_map/pack/pallas_call | solution.py:66
  9.2 12.0 %all-to-all-start.1 = ((bf16[128,2,64,128]{3,2,1,0:T(8,128)(2,1)}), bf16[128,2,64,128]{3,2,1,0:T(8,128)(2,1)}, u32[]{:S(2)}, u32[]{:S(2)}) async-start(bf16[128,2,64,128]{3,2,1,0:T(8,128)(2,1)} %bitcast.26), calls=%async_computation.1 | async-start | bytes 8388608 | tf_op jit(solution)/shard_map/all_to_all | solution.py:288
  21.2 3.0 %collective-permute-start = (s32[128]{0:T(128)S(1)}, s32[128]{0:T(128)S(1)}, u32[]{:S(2)}, u32[]{:S(2)}) collective-permute-start(s32[128]{0:T(128)S(1)} %copy-done.2), channel_id=1, source_target_pairs={{0,4},{1,5},{2,6},{3,7},{4,0},{5,1},{6,2},{7,3},{8,12},{9,13},{10,... | collective-permute-start | bytes 1544 | tf_op jit(solution)/shard_map/ppermute | solution.py:269
  24.3 44.4 %collective-permute-done = s32[128]{0:T(128)S(1)} collective-permute-done((s32[128]{0:T(128)S(1)}, s32[128]{0:T(128)S(1)}, u32[]{:S(2)}, u32[]{:S(2)}) %collective-permute-start) | collective-permute-done | bytes 544 | tf_op jit(solution)/shard_map/ppermute | solution.py:269
  68.8 3.2 %all-to-all-done.1 = bf16[128,2,64,128]{3,2,1,0:T(8,128)(2,1)} async-done(((bf16[128,2,64,128]{3,2,1,0:T(8,128)(2,1)}), bf16[128,2,64,128]{3,2,1,0:T(8,128)(2,1)}, u32[]{:S(2)}, u32[]{:S(2)}) %all-to-all-start.1) | async-done | bytes 4194336 | tf_op jit(solution)/shard_map/all_to_all | solution.py:288
  72.0 8.2 %all-to-all-start = ((bf16[128,2,64,128]{3,2,1,0:T(8,128)(2,1)}), bf16[128,2,64,128]{3,2,1,0:T(8,128)(2,1)}, u32[]{:S(2)}, u32[]{:S(2)}) async-start(bf16[128,2,64,128]{3,2,1,0:T(8,128)(2,1)} %bitcast.25), calls=%async_computation | async-start | bytes 8388608 | tf_op jit(solution)/shard_map/all_to_all | solution.py:306
  80.2 1.8 constant_dynamic-slice_fusion.1
  83.2 3.8 %collective-permute-done.1.other = bf16[16,1,4,2,64,128]{5,4,3,2,1,0:T(8,128)(2,1)S(1)} collective-permute-done((bf16[16,1,4,2,64,128]{5,4,3,2,1,0:T(8,128)(2,1)S(1)}, bf16[16,1,4,2,64,128]{5,4,3,2,1,0:T(8,128)(2,1)S(1)}, u32[]{:S(2)}, u32[]{:S(2)}) %collective-permute-start.1) | collective-permute-done | bytes 2097184 | tf_op jit(solution)/shard_map/ppermute | solution.py:283
  87.0 19.1 %first_half.1 = (f32[12,256,256]{2,1,0:T(8,128)S(1)}, f32[12,256,256]{2,1,0:T(8,128)S(1)}) custom-call(s32[6]{0:T(128)S(1)} %stack.48.where, bf16[16,2,4,2,64,128]{5,4,3,2,1,0:T(8,128)(2,1)} %bitcast.12.left.own, bf16[16,2,4,2,64,128]{5,4,3,2,1,0:T(8,128)(2,1)} %bitcast.12.left.own, bf16[16,1,4,2,64,128]{5,4,3,2,1,0:T(8,128)(2,1)S(1)} %collective-permute-done.1.other, ...), custom_call_target="tpu_custom_call" | custom-call | flops 12999999488 | bytes 12582912 | tf_op jit(solution)/shard_map/first_half/pallas_call | solution.py:174
  106.1 1.7 copy-done
  107.8 23.3 %all-to-all-done = bf16[128,2,64,128]{3,2,1,0:T(8,128)(2,1)} async-done(((bf16[128,2,64,128]{3,2,1,0:T(8,128)(2,1)}), bf16[128,2,64,128]{3,2,1,0:T(8,128)(2,1)}, u32[]{:S(2)}, u32[]{:S(2)}) %all-to-all-start) | async-done | bytes 4194336 | tf_op jit(solution)/shard_map/all_to_all | solution.py:306
  131.0 1.9 constant_dynamic-slice_fusion
  132.9 2.7 %collective-permute-start.6 = (bf16[16,1,4,2,64,128]{5,4,3,2,1,0:T(8,128)(2,1)S(1)}, bf16[16,1,4,2,64,128]{5,4,3,2,1,0:T(8,128)(2,1)S(1)}, u32[]{:S(2)}, u32[]{:S(2)}) collective-permute-start(bf16[16,1,4,2,64,128]{5,4,3,2,1,0:T(8,128)(2,1)S(1)} %constant_dynamic-slice_fusion), channel_id=1, source_target_pairs={{0,8},{1,9},{2,10},{3,11},{4,12},{5,13},{6,14},{7,15},{8,0},{9,1},... | collective-permute-start | bytes 6291464 | tf_op jit(solution)/shard_map/ppermute | solution.py:283
  135.7 13.4 %second_half.2 = (bf16[12,64,256]{2,1,0:T(8,128)(2,1)S(1)}, bf16[12,64,256]{2,1,0:T(8,128)(2,1)S(1)}, bf16[12,64,256]{2,1,0:T(8,128)(2,1)S(1)}, bf16[12,64,256]{2,1,0:T(8,128)(2,1)S(1)}) custom-call(s32[6]{0:T(128)S(1)} %stack.48.where, bf16[16,2,4,2,64,128]{5,4,3,2,1,0:T(8,128)(2,1)} %bitcast.15.left.right, ...), custom_call_target="tpu_custom_call" | custom-call | flops 6499999744 | bytes 8388608 | tf_op jit(solution)/shard_map/second_half/pallas_call | solution.py:197
  150.5 2.3 %collective-permute-start.4 = (bf16[12,64,256]{2,1,0:T(8,128)(2,1)S(1)}, bf16[12,64,256]{2,1,0:T(8,128)(2,1)S(1)}, u32[]{:S(2)}, u32[]{:S(2)}) collective-permute-start(bf16[12,64,256]{2,1,0:T(8,128)(2,1)S(1)} %get-tuple-element.38), channel_id=1, source_target_pairs={{0,6},{1,7},{2,4},{3,5},{4,14},{5,15},{6,12},{7,13},{8,2},{9,3},{1... | collective-permute-start | bytes 1179656 | tf_op jit(solution)/shard_map/ppermute | solution.py:294
  152.8 1.8 collective-permute-start.5
  154.6 12.4 %second_half.3 = (bf16[12,64,256]{2,1,0:T(8,128)(2,1)S(1)}, bf16[12,64,256]{2,1,0:T(8,128)(2,1)S(1)}, bf16[12,64,256]{2,1,0:T(8,128)(2,1)S(1)}, bf16[12,64,256]{2,1,0:T(8,128)(2,1)S(1)}) custom-call(s32[6]{0:T(128)S(1)} %stack.48.where, bf16[16,2,4,2,64,128]{5,4,3,2,1,0:T(8,128)(2,1)} %bitcast.15.left.right, ...), custom_call_target="tpu_custom_call" | custom-call | flops 6499999744 | bytes 8388608 | tf_op jit(solution)/shard_map/second_half/pallas_call | solution.py:197
  167.9 2.0 %collective-permute-start.8 = (bf16[12,64,256]{2,1,0:T(8,128)(2,1)S(1)}, bf16[12,64,256]{2,1,0:T(8,128)(2,1)S(1)}, u32[]{:S(2)}, u32[]{:S(2)}) collective-permute-start(bf16[12,64,256]{2,1,0:T(8,128)(2,1)S(1)} %get-tuple-element.42), channel_id=1, source_target_pairs={{0,5},{1,6},{2,7},{3,4},{4,13},{5,14},{6,15},{7,12},{8,1},{9,2},{1... | collective-permute-start | bytes 1179656 | tf_op jit(solution)/shard_map/ppermute | solution.py:294
  169.9 2.4 %collective-permute-start.9 = (bf16[12,64,256]{2,1,0:T(8,128)(2,1)S(1)}, bf16[12,64,256]{2,1,0:T(8,128)(2,1)S(1)}, u32[]{:S(2)}, u32[]{:S(2)}) collective-permute-start(bf16[12,64,256]{2,1,0:T(8,128)(2,1)S(1)} %get-tuple-element.43), channel_id=1, source_target_pairs={{0,6},{1,7},{2,4},{3,5},{4,14},{5,15},{6,12},{7,13},{8,2},{9,3},{1... | collective-permute-start | bytes 1179656 | tf_op jit(solution)/shard_map/ppermute | solution.py:294
  172.3 3.0 %collective-permute-start.10 = (bf16[12,64,256]{2,1,0:T(8,128)(2,1)S(1)}, bf16[12,64,256]{2,1,0:T(8,128)(2,1)S(1)}, u32[]{:S(2)}, u32[]{:S(2)}) collective-permute-start(bf16[12,64,256]{2,1,0:T(8,128)(2,1)S(1)} %get-tuple-element.44), channel_id=1, source_target_pairs={{0,7},{1,4},{2,5},{3,6},{4,15},{5,12},{6,13},{7,14},{8,3},{9,0},{1... | collective-permute-start | bytes 1179656 | tf_op jit(solution)/shard_map/ppermute | solution.py:294
  175.3 6.7 %collective-permute-done.8.refs_5_ = bf16[12,64,256]{2,1,0:T(8,128)(2,1)S(1)} collective-permute-done((bf16[12,64,256]{2,1,0:T(8,128)(2,1)S(1)}, bf16[12,64,256]{2,1,0:T(8,128)(2,1)S(1)}, u32[]{:S(2)}, u32[]{:S(2)}) %collective-permute-start.8) | collective-permute-done | bytes 393248 | tf_op jit(solution)/shard_map/ppermute | solution.py:294
  182.0 5.3 %collective-permute-done.9.refs_6_ = bf16[12,64,256]{2,1,0:T(8,128)(2,1)S(1)} collective-permute-done((bf16[12,64,256]{2,1,0:T(8,128)(2,1)S(1)}, bf16[12,64,256]{2,1,0:T(8,128)(2,1)S(1)}, u32[]{:S(2)}, u32[]{:S(2)}) %collective-permute-start.9) | collective-permute-done | bytes 393248 | tf_op jit(solution)/shard_map/ppermute | solution.py:294
  187.3 2.7 %collective-permute-done.10.refs_7_ = bf16[12,64,256]{2,1,0:T(8,128)(2,1)S(1)} collective-permute-done((bf16[12,64,256]{2,1,0:T(8,128)(2,1)S(1)}, bf16[12,64,256]{2,1,0:T(8,128)(2,1)S(1)}, u32[]{:S(2)}, u32[]{:S(2)}) %collective-permute-start.10) | collective-permute-done | bytes 393248 | tf_op jit(solution)/shard_map/ppermute | solution.py:294
  190.0 2.0 %total.1 = f32[1,12,64,512]{3,2,1,0:T(8,128)} custom-call(s32[2]{0:T(128)S(1)} %pad_add_fusion.1.where, bf16[12,64,256]{2,1,0:T(8,128)(2,1)S(1)} %collective-permute-done.2.refs_0_, bf16[12,64,256]{2,1,0:T(8,128)(2,1)S(1)} %collective-permute-done.3.refs_1_, bf16[12,64,256]{2,1,0:T(8,128)(2,1)S(1)} %collective-permute-done.4.refs_2_, ...), custom_call_target="tpu_custom_call" | custom-call | tf_op jit(solution)/shard_map/total/pallas_call | solution.py:232
  (24 shorter events, 5.2 us)
Async XLA Ops:
  9.2 12.0 %copy-start.2 = (s32[128]{0:T(128)S(1)}, s32[128]{0:T(128)}, u32[]{:S(2)}) copy-start(s32[128]{0:T(128)} %param.5) | copy-start | bytes 1540
  9.2 62.8 %all-to-all-start.1 = ((bf16[128,2,64,128]{3,2,1,0:T(8,128)(2,1)}), bf16[128,2,64,128]{3,2,1,0:T(8,128)(2,1)}, u32[]{:S(2)}, u32[]{:S(2)}) async-start(bf16[128,2,64,128]{3,2,1,0:T(8,128)(2,1)} %bitcast.26), calls=%async_computation.1 | async-start | bytes 8388608 | tf_op jit(solution)/shard_map/all_to_all | solution.py:288
  21.2 47.6 %collective-permute-start = (s32[128]{0:T(128)S(1)}, s32[128]{0:T(128)S(1)}, u32[]{:S(2)}, u32[]{:S(2)}) collective-permute-start(s32[128]{0:T(128)S(1)} %copy-done.2), channel_id=1, source_target_pairs={{0,4},{1,5},{2,6},{3,7},{4,0},{5,1},{6,2},{7,3},{8,12},{9,13},{10,... | collective-permute-start | bytes 1544 | tf_op jit(solution)/shard_map/ppermute | solution.py:269
  72.0 59.0 %all-to-all-start = ((bf16[128,2,64,128]{3,2,1,0:T(8,128)(2,1)}), bf16[128,2,64,128]{3,2,1,0:T(8,128)(2,1)}, u32[]{:S(2)}, u32[]{:S(2)}) async-start(bf16[128,2,64,128]{3,2,1,0:T(8,128)(2,1)} %bitcast.25), calls=%async_computation | async-start | bytes 8388608 | tf_op jit(solution)/shard_map/all_to_all | solution.py:306
  82.0 5.0 %collective-permute-start.1 = (bf16[16,1,4,2,64,128]{5,4,3,2,1,0:T(8,128)(2,1)S(1)}, bf16[16,1,4,2,64,128]{5,4,3,2,1,0:T(8,128)(2,1)S(1)}, u32[]{:S(2)}, u32[]{:S(2)}) collective-permute-start(bf16[16,1,4,2,64,128]{5,4,3,2,1,0:T(8,128)(2,1)S(1)} %constant_dynamic-slice_fusion.1), channel_id=1, source_target_pairs={{0,8},{1,9},{2,10},{3,11},{4,12},{5,13},{6,14},{7,15},{8,0},{9,1},... | collective-permute-start | bytes 6291464 | tf_op jit(solution)/shard_map/ppermute | solution.py:283
  106.1 1.7 copy-start
  132.9 21.7 %collective-permute-start.6 = (bf16[16,1,4,2,64,128]{5,4,3,2,1,0:T(8,128)(2,1)S(1)}, bf16[16,1,4,2,64,128]{5,4,3,2,1,0:T(8,128)(2,1)S(1)}, u32[]{:S(2)}, u32[]{:S(2)}) collective-permute-start(bf16[16,1,4,2,64,128]{5,4,3,2,1,0:T(8,128)(2,1)S(1)} %constant_dynamic-slice_fusion), channel_id=1, source_target_pairs={{0,8},{1,9},{2,10},{3,11},{4,12},{5,13},{6,14},{7,15},{8,0},{9,1},... | collective-permute-start | bytes 6291464 | tf_op jit(solution)/shard_map/ppermute | solution.py:283
  135.7 18.9 %copy-start.1 = (f32[12,256,256]{2,1,0:T(8,128)S(1)}, f32[12,256,256]{2,1,0:T(8,128)}, u32[]{:S(2)}) copy-start(f32[12,256,256]{2,1,0:T(8,128)} %copy-done) | copy-start | bytes 9437188
  149.0 18.8 %collective-permute-start.2 = (bf16[12,64,256]{2,1,0:T(8,128)(2,1)S(1)}, bf16[12,64,256]{2,1,0:T(8,128)(2,1)S(1)}, u32[]{:S(2)}, u32[]{:S(2)}) collective-permute-start(bf16[12,64,256]{2,1,0:T(8,128)(2,1)S(1)} %get-tuple-element.36), channel_id=1, source_target_pairs={{0,4},{1,5},{2,6},{3,7},{4,12},{5,13},{6,14},{7,15},{8,0},{9,1},{1... | collective-permute-start | bytes 1179656 | tf_op jit(solution)/shard_map/ppermute | solution.py:294
  149.1 20.7 %collective-permute-start.3 = (bf16[12,64,256]{2,1,0:T(8,128)(2,1)S(1)}, bf16[12,64,256]{2,1,0:T(8,128)(2,1)S(1)}, u32[]{:S(2)}, u32[]{:S(2)}) collective-permute-start(bf16[12,64,256]{2,1,0:T(8,128)(2,1)S(1)} %get-tuple-element.37), channel_id=1, source_target_pairs={{0,5},{1,6},{2,7},{3,4},{4,13},{5,14},{6,15},{7,12},{8,1},{9,2},{1... | collective-permute-start | bytes 1179656 | tf_op jit(solution)/shard_map/ppermute | solution.py:294
  150.5 21.8 %collective-permute-start.4 = (bf16[12,64,256]{2,1,0:T(8,128)(2,1)S(1)}, bf16[12,64,256]{2,1,0:T(8,128)(2,1)S(1)}, u32[]{:S(2)}, u32[]{:S(2)}) collective-permute-start(bf16[12,64,256]{2,1,0:T(8,128)(2,1)S(1)} %get-tuple-element.38), channel_id=1, source_target_pairs={{0,6},{1,7},{2,4},{3,5},{4,14},{5,15},{6,12},{7,13},{8,2},{9,3},{1... | collective-permute-start | bytes 1179656 | tf_op jit(solution)/shard_map/ppermute | solution.py:294
  152.8 22.5 %collective-permute-start.5 = (bf16[12,64,256]{2,1,0:T(8,128)(2,1)S(1)}, bf16[12,64,256]{2,1,0:T(8,128)(2,1)S(1)}, u32[]{:S(2)}, u32[]{:S(2)}) collective-permute-start(bf16[12,64,256]{2,1,0:T(8,128)(2,1)S(1)} %get-tuple-element.39), channel_id=1, source_target_pairs={{0,7},{1,4},{2,5},{3,6},{4,15},{5,12},{6,13},{7,14},{8,3},{9,0},{1... | collective-permute-start | bytes 1179656 | tf_op jit(solution)/shard_map/ppermute | solution.py:294
  167.0 8.2 %collective-permute-start.7 = (bf16[12,64,256]{2,1,0:T(8,128)(2,1)S(1)}, bf16[12,64,256]{2,1,0:T(8,128)(2,1)S(1)}, u32[]{:S(2)}, u32[]{:S(2)}) collective-permute-start(bf16[12,64,256]{2,1,0:T(8,128)(2,1)S(1)} %get-tuple-element.41), channel_id=1, source_target_pairs={{0,4},{1,5},{2,6},{3,7},{4,12},{5,13},{6,14},{7,15},{8,0},{9,1},{1... | collective-permute-start | bytes 1179656 | tf_op jit(solution)/shard_map/ppermute | solution.py:294
  167.9 14.1 %collective-permute-start.8 = (bf16[12,64,256]{2,1,0:T(8,128)(2,1)S(1)}, bf16[12,64,256]{2,1,0:T(8,128)(2,1)S(1)}, u32[]{:S(2)}, u32[]{:S(2)}) collective-permute-start(bf16[12,64,256]{2,1,0:T(8,128)(2,1)S(1)} %get-tuple-element.42), channel_id=1, source_target_pairs={{0,5},{1,6},{2,7},{3,4},{4,13},{5,14},{6,15},{7,12},{8,1},{9,2},{1... | collective-permute-start | bytes 1179656 | tf_op jit(solution)/shard_map/ppermute | solution.py:294
  169.9 17.4 %collective-permute-start.9 = (bf16[12,64,256]{2,1,0:T(8,128)(2,1)S(1)}, bf16[12,64,256]{2,1,0:T(8,128)(2,1)S(1)}, u32[]{:S(2)}, u32[]{:S(2)}) collective-permute-start(bf16[12,64,256]{2,1,0:T(8,128)(2,1)S(1)} %get-tuple-element.43), channel_id=1, source_target_pairs={{0,6},{1,7},{2,4},{3,5},{4,14},{5,15},{6,12},{7,13},{8,2},{9,3},{1... | collective-permute-start | bytes 1179656 | tf_op jit(solution)/shard_map/ppermute | solution.py:294
  172.3 17.7 %collective-permute-start.10 = (bf16[12,64,256]{2,1,0:T(8,128)(2,1)S(1)}, bf16[12,64,256]{2,1,0:T(8,128)(2,1)S(1)}, u32[]{:S(2)}, u32[]{:S(2)}) collective-permute-start(bf16[12,64,256]{2,1,0:T(8,128)(2,1)S(1)} %get-tuple-element.44), channel_id=1, source_target_pairs={{0,7},{1,4},{2,5},{3,6},{4,15},{5,12},{6,13},{7,14},{8,3},{9,0},{1... | collective-permute-start | bytes 1179656 | tf_op jit(solution)/shard_map/ppermute | solution.py:294

commit v3 on v2

v3 whole, which is shorter than its diff:
```python
import functools
import math

import jax
import jax.numpy as jnp
from jax import lax
from jax.experimental import pallas as pl
from jax.experimental.pallas import tpu as pltpu
from jax.sharding import PartitionSpec as P

L = 8192
LAGS = 12
HALF = LAGS // 2
EPS = 1e-06

NZ = 4
CH = 64
FB = 128
CHUNKS = ((0, 0, 6), (1, 0, 6))
HOPS = (2, 1, 3, 0)
BF = jnp.bfloat16
F32 = jnp.float32


def pack_kernel(group, part, pairs, xh, block, out, white, sems):
    step = pl.program_id(0)
    for g in range(group):
        re = block[0, 0, g].astype(F32)
        im = block[1, 0, g].astype(F32)
        energy = jnp.mean(re * re + im * im, axis=-1, keepdims=True)
        gain = lax.rsqrt(energy + EPS)
        for comp, val in enumerate((re, im)):
            for z in range(NZ):
                at = (part * NZ + z) * FB
                white[step * group + g, z, comp] = (val[:, at : at + FB] * gain).astype(BF)

    def chosen(pair, core):
        return pairs[jnp.where(xh[0] == core, 1, 0), pair]

    def copy(pair, core):
        return pltpu.make_async_copy(
            white.at[chosen(pair, core)], out.at[pair // 2, core, pair % 2], sems.at[pair, core]
        )

    for pair in range(16):
        for core in range(2):

            @pl.when(chosen(pair, core) // group == step)
            def _(pair=pair, core=core):
                copy(pair, core).start()

    @pl.when(step == pl.num_programs(0) - 1)
    def _():
        for pair in range(16):
            for core in range(2):
                copy(pair, core).wait()


def pack(spectra, pairs, xh, part):
    blocks = spectra.shape[2]
    group = 4
    return pl.pallas_call(
        functools.partial(pack_kernel, group, part),
        grid_spec=pltpu.PrefetchScalarGridSpec(
            num_scalar_prefetch=2,
            grid=(blocks // group,),
            in_specs=[pl.BlockSpec((2, 1, group, CH, 1024), lambda p, pairs, xh: (0, 0, p, 0, 0))],
            out_specs=pl.BlockSpec(memory_space=pl.ANY),
            scratch_shapes=[
                pltpu.VMEM((blocks, NZ, 2, CH, FB), BF),
                pltpu.SemaphoreType.DMA((16, 2)),
            ],
        ),
        out_shape=jax.ShapeDtypeStruct((8, 2, 2, NZ, 2, CH, FB), BF),
        compiler_params=pltpu.CompilerParams(vmem_limit_bytes=60 * 2**20),
        cost_estimate=pl.CostEstimate(flops=16 * 2**20, bytes_accessed=8 * 2**20, transcendentals=0),
        name="pack",
    )(pairs, xh, spectra)


def turn_and_multiply(group, first, count, where, left, rights, cos_ref, sin_ref, even, odd, flat, add):
    rows_all = NZ * CH

    def col(g, comp):
        return slice((2 * g + comp) * FB, (2 * g + comp + 1) * FB)

    for h, right in enumerate(rights):
        for g in range(group):
            for comp in range(2):
                for z in range(NZ):
                    flat[h * rows_all + z * CH : h * rows_all + (z + 1) * CH, col(g, comp)] = right[g, 0, z, comp]

    def turn(m, turned):
        lag = HALF if isinstance(m, int) and m == 0 else m
        both = lag is m
        cos = jnp.broadcast_to(cos_ref[pl.ds(lag, 1), :], (CH, FB)).astype(BF)
        sin = jnp.broadcast_to(sin_ref[pl.ds(lag, 1), :], (CH, FB)).astype(BF)
        for g in range(group):
            for dz in range(NZ):
                z = where[2 + dz]
                re = left[g, 0, z, 0]
                im = left[g, 0, z, 1]
                rc, rs, ic, isn = re * cos, re * sin, im * cos, im * sin
                rows = slice(dz * CH, dz * CH + CH)
                more = slice(rows_all + dz * CH, rows_all + dz * CH + CH)
                turned[rows, col(g, 0)] = rc + isn
                turned[rows, col(g, 1)] = ic - rs
                turned[more, col(g, 0)] = rc - isn if both else re
                turned[more, col(g, 1)] = rs + ic if both else im

    def multiply(m, turned):
        product = lax.dot_general(
            turned[...], flat[...], (((1,), (1,)), ((), ())), preferred_element_type=F32
        )
        add(2 * (m - first), product[:rows_all])
        add(2 * (m - first) + 1, product[rows_all:])

    turn(first, even)
    loops = (count - 2) // 2 if count > 4 else 0

    def step(i, carry):
        m = first + 2 * i + 1
        turn(m, odd)
        multiply(m - 1, even)
        turn(m + 1, even)
        multiply(m, odd)
        return carry

    if loops:
        lax.fori_loop(0, loops, step, 0)
    now, later = even, odd
    for m in range(first + 2 * loops, first + count):
        if m + 1 < first + count:
            turn(m + 1, later)
        multiply(m, now)
        now, later = later, now


def first_kernel(group, where, left, own, other, cos_ref, sin_ref, own_sum, other_sum, even, odd, flat):
    @pl.when(pl.program_id(0) == 0)
    def _():
        own_sum[...] = jnp.zeros_like(own_sum)
        other_sum[...] = jnp.zeros_like(other_sum)

    def add(at, product):
        own_sum[at] += product[:, : NZ * CH]
        other_sum[at] += product[:, NZ * CH :]

    turn_and_multiply(group, 0, HALF, where, left, (own, other), cos_ref, sin_ref, even, odd, flat, add)


def second_kernel(group, first, count, where, left, right, cos_ref, sin_ref, before, o0, o1, o2, o3, even, odd, flat):
    def add(at, product):
        for dz, out in enumerate((o0, o1, o2, o3)):
            rows = slice(dz * CH, dz * CH + CH)
            out[at] = ((before[at, rows] + product[rows]) * (1.0 / 128.0)).astype(BF)

    turn_and_multiply(group, first, count, where, left, (right,), cos_ref, sin_ref, even, odd, flat, add)


SUMS = (LAGS, NZ * CH, NZ * CH)


def spec(group, at=None):
    index_map = (lambda s, where: (s, 0, 0, 0, 0, 0)) if at is None else (lambda s, where: (s, where[at], 0, 0, 0, 0))
    return pl.BlockSpec((group, 1, NZ, 2, CH, FB), index_map)


def table_spec():
    return pl.BlockSpec((8, FB), lambda s, where: (0, 0))


def whole(shape, at=0):
    return pl.BlockSpec(shape, lambda s, where: (at, 0, 0))


def first_half(where, landed, theirs, cosine, sine):
    group = 8
    return pl.pallas_call(
        functools.partial(first_kernel, group),
        grid_spec=pltpu.PrefetchScalarGridSpec(
            num_scalar_prefetch=1,
            grid=(landed.shape[0] // group,),
            in_specs=[spec(group, 0), spec(group, 1), spec(group), table_spec(), table_spec()],
            out_specs=[whole(SUMS)] * 2,
            scratch_shapes=[
                pltpu.VMEM((2 * NZ * CH, 2 * group * FB), BF),
                pltpu.VMEM((2 * NZ * CH, 2 * group * FB), BF),
                pltpu.VMEM((2 * NZ * CH, 2 * group * FB), BF),
            ],
        ),
        out_shape=[jax.ShapeDtypeStruct(SUMS, F32)] * 2,
        compiler_params=pltpu.CompilerParams(vmem_limit_bytes=40 * 2**20),
        cost_estimate=pl.CostEstimate(flops=13 * 10**9, bytes_accessed=12 * 2**20, transcendentals=0),
        name="first_half",
    )(where, landed, landed, theirs, cosine, sine)


def second_half(where, landed, right, at, cosine, sine, before, first=0, count=HALF):
    group = landed.shape[0]
    piece = jax.ShapeDtypeStruct((2 * count, CH, NZ * CH), BF)
    return pl.pallas_call(
        functools.partial(second_kernel, group, first, count),
        grid_spec=pltpu.PrefetchScalarGridSpec(
            num_scalar_prefetch=1,
            grid=(1,),
            in_specs=[spec(group, 0), spec(group, at), table_spec(), table_spec(), whole((2 * count, *SUMS[1:]), first // count)],
            out_specs=[whole(piece.shape)] * NZ,
            scratch_shapes=[
                pltpu.VMEM((2 * NZ * CH, 2 * group * FB), BF),
                pltpu.VMEM((2 * NZ * CH, 2 * group * FB), BF),
                pltpu.VMEM((NZ * CH, 2 * group * FB), BF),
            ],
        ),
        out_shape=[piece] * NZ,
        compiler_params=pltpu.CompilerParams(vmem_limit_bytes=40 * 2**20),
        cost_estimate=pl.CostEstimate(flops=count * 11 * 10**8, bytes_accessed=8 * 2**20, transcendentals=0),
        name="second_half",
    )(where, landed, right, cosine, sine, before)


def total_kernel(chunks, where, *refs):
    out = refs[-1]
    width = NZ * CH
    for k, (half, first, count) in enumerate(chunks):
        at = pl.multiple_of(where[half] * width, width)
        group = refs[k * NZ : (k + 1) * NZ]
        for m in range(first, first + count):
            for sign in range(2):
                i = 2 * (m - first) + sign
                val = group[0][i].astype(F32)
                for ref in group[1:]:
                    val = val + ref[i].astype(F32)
                lag = HALF + m if sign else (HALF - m if m else 0)
                out[0, lag, :, pl.ds(at, width)] = val


def total(where, chunks, parts):
    shape = (1, LAGS, CH, 2 * NZ * CH)
    return pl.pallas_call(
        functools.partial(total_kernel, chunks),
        grid_spec=pltpu.PrefetchScalarGridSpec(
            num_scalar_prefetch=1,
            grid=(1,),
            in_specs=[pl.BlockSpec(part.shape, lambda i, where: (0, 0, 0)) for part in parts],
            out_specs=pl.BlockSpec(shape, lambda i, where: (0, 0, 0, 0)),
        ),
        out_shape=jax.ShapeDtypeStruct(shape, F32),
        compiler_params=pltpu.CompilerParams(vmem_limit_bytes=32 * 2**20),
        name="total",
    )(where, *parts)


def places():
    return [
        (y, xl, c, xh, z)
        for y in range(4)
        for xl in range(2)
        for c in range(2)
        for xh in range(2)
        for z in range(NZ)
    ]


def index(y, xl, c, xh, z):
    return ((y * 2 + xl) * 2 + c) * 8 + xh * 4 + z


def body(spectra, block_pairs, band_bins):
    both = ("row", "col")
    row = lax.axis_index("row")
    col = lax.axis_index("col")
    core = row % 2
    xh = col // 4
    z = col % 4

    bins_there = lax.ppermute(
        band_bins, both, [(index(*p), index(p[0], p[1], p[2], 1 - p[3], p[4])) for p in places()]
    )
    low = jnp.where(xh == 0, band_bins, bins_there)
    high = jnp.where(xh == 0, bins_there, band_bins)
    steps = jnp.arange(8, dtype=jnp.int32)
    angle = jnp.mod(jnp.stack([low, high])[:, None, :] * steps[:, None], L).astype(F32) * (2.0 * math.pi / L)
    cosine, sine = jnp.cos(angle), jnp.sin(angle)

    where = jnp.stack([1 - core, core] + [(z + hop) % NZ for hop in HOPS]).astype(jnp.int32)
    halves = jnp.stack([1 - xh, xh]).astype(jnp.int32)

    def swap(mine):
        return lax.ppermute(
            mine, both, [(index(*p), index(p[0], p[1], 1 - p[2], p[3], p[4])) for p in places()]
        )

    def exchange(packed):
        landed = lax.all_to_all(packed.reshape(128, 2, CH, FB), both, split_axis=0, concat_axis=0, tiled=True)
        landed = landed.reshape(16, 2, NZ, 2, CH, FB)
        return landed, swap(lax.dynamic_slice_in_dim(landed, core, 1, axis=1))

    def send(parts):
        return [
            lax.ppermute(
                part,
                both,
                [(index(*p), index(p[0], p[1], p[3], 1 - p[2], (p[4] + hop) % NZ)) for p in places()],
            )
            for hop, part in zip(HOPS, parts)
        ]

    pairs, side = block_pairs.T, xh.reshape(1)
    packed0 = pack(spectra, pairs, side, 0)
    packed1 = pack(spectra, pairs, side, 1)
    packed1, cosine, sine, where, halves = lax.optimization_barrier((packed1, cosine, sine, where, halves))
    landed0, theirs0 = exchange(packed0)
    own, other = first_half(where, landed0, theirs0, cosine[0], sine[0])
    landed1 = lax.all_to_all(packed1.reshape(128, 2, CH, FB), both, split_axis=0, concat_axis=0, tiled=True)
    landed1, own, other = lax.optimization_barrier((landed1, own, other))
    landed1 = landed1.reshape(16, 2, NZ, 2, CH, FB)
    theirs1 = swap(lax.dynamic_slice_in_dim(landed1, core, 1, axis=1))
    chunks = CHUNKS
    parts = []
    for half, first, count in chunks:
        right, at, before = (landed1, 1, own) if half == 0 else (theirs1, None, other)
        parts += send(second_half(where, landed1, right, at, cosine[1], sine[1], before, first, count))
    return jnp.transpose(total(halves, chunks, parts), (0, 2, 1, 3))


def solution(mesh):
    in_specs = (P(None, "row", None, "col", None), P(), P("col"))
    out_specs = P("row", "col", None, None)
    return jax.shard_map(body, mesh=mesh, in_specs=in_specs, out_specs=out_specs, check_vma=False)
```

time: 193 us -> 190 us (0.984)
  waiting for transfers between devices: 89.4 us -> 83.4 us
  Pallas kernels: 54.7 us -> 59.1 us
    ppermute x1, waiting for transfers between devices: 44.4 us -> 38.2 us  [body(): lax.ppermute(band_bins, both, [(index(*p), index(p[0], p[1], p[2], 1 - p[...]
    pallas_call x4 -> x5, Pallas kernels: 35.6 us -> 40.1 us  [the longest x2 25.6 us: second_half(): pl.pallas_call(functools.partial(second_kernel, group, first, count), gri...]
  transfers between devices with their start and end apart: 13 -> 13, of which waited for: 7 -> 8; matrix products, arithmetic and copies ran while one was open for 1% -> 1% of each run, Pallas kernels for 23% -> 27%
where the time goes in v3:
time: 190 us; the launch traced here: 189 us
  waiting for transfers between devices  83.4 us (44%)
  Pallas kernels  59.1 us (31%)
  starting transfers between devices  40.5 us (21%)
  local copies, waits for them, and re-layouts  5.39 us (3%)
    ppermute x1, waiting for transfers between devices, body(): lax.ppermute(band_bins, both, [(index(*p), index(p[0], p[1], p[2], 1 - p[...  38.2 us
    pallas_call x2, Pallas kernels, second_half(): pl.pallas_call(functools.partial(second_kernel, group, first, count), gri...  25.6 us
    all_to_all x1, waiting for transfers between devices, body(): lax.all_to_all(packed1.reshape(128, 2, CH, FB), both, split_axis=0, conca...  23.3 us
    pallas_call x1, Pallas kernels, first_half(): pl.pallas_call(functools.partial(first_kernel, group), grid_spec=pltpu.Pr...  19 us
    ppermute x8, waiting for transfers between devices, send(): lax.ppermute(part, both, [(index(*p), index(p[0], p[1], p[3], 1 - p[2], (...  14.9 us
    ppermute x8, starting transfers between devices, send(): lax.ppermute(part, both, [(index(*p), index(p[0], p[1], p[3], 1 - p[2], (...  13.4 us
    pallas_call x2, Pallas kernels, pack(): pl.pallas_call(functools.partial(pack_kernel, group, part), grid_spec=plt...  12.4 us
    all_to_all x1, starting transfers between devices, exchange(): lax.all_to_all(packed.reshape(128, 2, CH, FB), both, split_axis=0, concat...  12 us
  transfers between devices with their start and end apart: 13, of which 8 were waited for; matrix products, arithmetic and copies ran while one was open for 1% of the time, Pallas kernels for 27%

profile of v3, /device:TPU:1, one launch (start us, length us, event | category | flops | bytes accessed | tf_op | source)
XLA Modules:
  0.0 188.6 jit_solution(16043775841276528001)
XLA Ops:
  0.0 6.2 %pack.3 = bf16[8,2,2,4,2,64,128]{6,5,4,3,2,1,0:T(8,128)(2,1)} custom-call(s32[2,16]{1,0:T(2,128)} %bitcast.28, s32[1]{0:T(128)} %bitcast.1.xh, bf16[2,1,16,64,1024]{4,3,2,1,0:T(8,128)(2,1)} %block.3), custom_call_target="tpu_custom_call" | custom-call | flops 16777216 | bytes 8388608 | tf_op jit(solution)/shard_map/pack/pallas_call | solution.py:62
  6.2 12.0 %all-to-all-start.1 = ((bf16[128,2,64,128]{3,2,1,0:T(8,128)(2,1)}), bf16[128,2,64,128]{3,2,1,0:T(8,128)(2,1)}, u32[]{:S(2)}, u32[]{:S(2)}) async-start(bf16[128,2,64,128]{3,2,1,0:T(8,128)(2,1)} %bitcast.26), calls=%async_computation.1 | async-start | bytes 8388608 | tf_op jit(solution)/shard_map/all_to_all | solution.py:295
  18.2 3.0 %collective-permute-start = (s32[128]{0:T(128)S(1)}, s32[128]{0:T(128)S(1)}, u32[]{:S(2)}, u32[]{:S(2)}) collective-permute-start(s32[128]{0:T(128)S(1)} %copy-done.2), channel_id=1, source_target_pairs={{0,4},{1,5},{2,6},{3,7},{4,0},{5,1},{6,2},{7,3},{8,12},{9,13},{10,... | collective-permute-start | bytes 1544 | tf_op jit(solution)/shard_map/ppermute | solution.py:277
  21.2 6.2 %pack.2 = bf16[8,2,2,4,2,64,128]{6,5,4,3,2,1,0:T(8,128)(2,1)} custom-call(s32[2,16]{1,0:T(2,128)} %bitcast.29, s32[1]{0:T(128)} %bitcast.1.xh, bf16[2,1,16,64,1024]{4,3,2,1,0:T(8,128)(2,1)} %block.3), custom_call_target="tpu_custom_call" | custom-call | flops 16777216 | bytes 8388608 | tf_op jit(solution)/shard_map/pack/pallas_call | solution.py:62
  27.5 38.2 %collective-permute-done = s32[128]{0:T(128)S(1)} collective-permute-done((s32[128]{0:T(128)S(1)}, s32[128]{0:T(128)S(1)}, u32[]{:S(2)}, u32[]{:S(2)}) %collective-permute-start) | collective-permute-done | bytes 544 | tf_op jit(solution)/shard_map/ppermute | solution.py:277
  65.8 3.2 %all-to-all-done.1 = bf16[128,2,64,128]{3,2,1,0:T(8,128)(2,1)} async-done(((bf16[128,2,64,128]{3,2,1,0:T(8,128)(2,1)}), bf16[128,2,64,128]{3,2,1,0:T(8,128)(2,1)}, u32[]{:S(2)}, u32[]{:S(2)}) %all-to-all-start.1) | async-done | bytes 4194336 | tf_op jit(solution)/shard_map/all_to_all | solution.py:295
  69.0 8.2 %all-to-all-start = ((bf16[128,2,64,128]{3,2,1,0:T(8,128)(2,1)}), bf16[128,2,64,128]{3,2,1,0:T(8,128)(2,1)}, u32[]{:S(2)}, u32[]{:S(2)}) async-start(bf16[128,2,64,128]{3,2,1,0:T(8,128)(2,1)} %bitcast.27), calls=%async_computation | async-start | bytes 8388608 | tf_op jit(solution)/shard_map/all_to_all | solution.py:315
  77.2 1.8 constant_dynamic-slice_fusion.1
  80.2 3.8 %collective-permute-done.1.other = bf16[16,1,4,2,64,128]{5,4,3,2,1,0:T(8,128)(2,1)S(1)} collective-permute-done((bf16[16,1,4,2,64,128]{5,4,3,2,1,0:T(8,128)(2,1)S(1)}, bf16[16,1,4,2,64,128]{5,4,3,2,1,0:T(8,128)(2,1)S(1)}, u32[]{:S(2)}, u32[]{:S(2)}) %collective-permute-start.1) | collective-permute-done | bytes 2097184 | tf_op jit(solution)/shard_map/ppermute | solution.py:290
  84.0 19.0 %first_half.1 = (f32[12,256,256]{2,1,0:T(8,128)S(1)}, f32[12,256,256]{2,1,0:T(8,128)S(1)}) custom-call(s32[6]{0:T(128)S(1)} %stack.46.where, bf16[16,2,4,2,64,128]{5,4,3,2,1,0:T(8,128)(2,1)} %bitcast.13.left.own, bf16[16,2,4,2,64,128]{5,4,3,2,1,0:T(8,128)(2,1)} %bitcast.13.left.own, bf16[16,1,4,2,64,128]{5,4,3,2,1,0:T(8,128)(2,1)S(1)} %collective-permute-done.1.other, ...), custom_call_target="tpu_custom_call" | custom-call | flops 12999999488 | bytes 12582912 | tf_op jit(solution)/shard_map/first_half/pallas_call | solution.py:179
  103.0 1.6 copy-done
  104.7 23.3 %all-to-all-done = bf16[128,2,64,128]{3,2,1,0:T(8,128)(2,1)} async-done(((bf16[128,2,64,128]{3,2,1,0:T(8,128)(2,1)}), bf16[128,2,64,128]{3,2,1,0:T(8,128)(2,1)}, u32[]{:S(2)}, u32[]{:S(2)}) %all-to-all-start) | async-done | bytes 4194336 | tf_op jit(solution)/shard_map/all_to_all | solution.py:315
  128.0 1.9 %constant_dynamic-slice_fusion = bf16[16,1,4,2,64,128]{5,4,3,2,1,0:T(8,128)(2,1)S(1)} fusion(bf16[16,2,4,2,64,128]{5,4,3,2,1,0:T(8,128)(2,1)} %bitcast.16.left.right, s32[]{:T(128)S(6)} %select_n.64), kind=kLoop, calls=%fused_computation.21 | loop fusion | bytes 4194308 | tf_op jit(solution)/shard_map/dynamic_slice | solution.py:318
  129.9 2.7 %collective-permute-start.6 = (bf16[16,1,4,2,64,128]{5,4,3,2,1,0:T(8,128)(2,1)S(1)}, bf16[16,1,4,2,64,128]{5,4,3,2,1,0:T(8,128)(2,1)S(1)}, u32[]{:S(2)}, u32[]{:S(2)}) collective-permute-start(bf16[16,1,4,2,64,128]{5,4,3,2,1,0:T(8,128)(2,1)S(1)} %constant_dynamic-slice_fusion), channel_id=1, source_target_pairs={{0,8},{1,9},{2,10},{3,11},{4,12},{5,13},{6,14},{7,15},{8,0},{9,1},... | collective-permute-start | bytes 6291464 | tf_op jit(solution)/shard_map/ppermute | solution.py:290
  132.6 13.3 %second_half.2 = (bf16[12,64,256]{2,1,0:T(8,128)(2,1)S(1)}, bf16[12,64,256]{2,1,0:T(8,128)(2,1)S(1)}, bf16[12,64,256]{2,1,0:T(8,128)(2,1)S(1)}, bf16[12,64,256]{2,1,0:T(8,128)(2,1)S(1)}) custom-call(s32[6]{0:T(128)S(1)} %stack.46.where, bf16[16,2,4,2,64,128]{5,4,3,2,1,0:T(8,128)(2,1)} %bitcast.16.left.right, ...), custom_call_target="tpu_custom_call" | custom-call | flops 6600000000 | bytes 8388608 | tf_op jit(solution)/shard_map/second_half/pallas_call | solution.py:202
  146.1 2.5 %collective-permute-start.3 = (bf16[12,64,256]{2,1,0:T(8,128)(2,1)S(1)}, bf16[12,64,256]{2,1,0:T(8,128)(2,1)S(1)}, u32[]{:S(2)}, u32[]{:S(2)}) collective-permute-start(bf16[12,64,256]{2,1,0:T(8,128)(2,1)S(1)} %get-tuple-element.33), channel_id=1, source_target_pairs={{0,5},{1,6},{2,7},{3,4},{4,13},{5,14},{6,15},{7,12},{8,1},{9,2},{1... | collective-permute-start | bytes 1179656 | tf_op jit(solution)/shard_map/ppermute | solution.py:301
  148.6 2.1 %collective-permute-start.4 = (bf16[12,64,256]{2,1,0:T(8,128)(2,1)S(1)}, bf16[12,64,256]{2,1,0:T(8,128)(2,1)S(1)}, u32[]{:S(2)}, u32[]{:S(2)}) collective-permute-start(bf16[12,64,256]{2,1,0:T(8,128)(2,1)S(1)} %get-tuple-element.34), channel_id=1, source_target_pairs={{0,7},{1,4},{2,5},{3,6},{4,15},{5,12},{6,13},{7,14},{8,3},{9,0},{1... | collective-permute-start | bytes 1179656 | tf_op jit(solution)/shard_map/ppermute | solution.py:301
  151.9 12.4 %second_half.3 = (bf16[12,64,256]{2,1,0:T(8,128)(2,1)S(1)}, bf16[12,64,256]{2,1,0:T(8,128)(2,1)S(1)}, bf16[12,64,256]{2,1,0:T(8,128)(2,1)S(1)}, bf16[12,64,256]{2,1,0:T(8,128)(2,1)S(1)}) custom-call(s32[6]{0:T(128)S(1)} %stack.46.where, bf16[16,2,4,2,64,128]{5,4,3,2,1,0:T(8,128)(2,1)} %bitcast.16.left.right, ...), custom_call_target="tpu_custom_call" | custom-call | flops 6600000000 | bytes 8388608 | tf_op jit(solution)/shard_map/second_half/pallas_call | solution.py:202
  164.3 1.8 collective-permute-start.7
  167.1 4.1 %collective-permute-start.9 = (bf16[12,64,256]{2,1,0:T(8,128)(2,1)S(1)}, bf16[12,64,256]{2,1,0:T(8,128)(2,1)S(1)}, u32[]{:S(2)}, u32[]{:S(2)}) collective-permute-start(bf16[12,64,256]{2,1,0:T(8,128)(2,1)S(1)} %get-tuple-element.39), channel_id=1, source_target_pairs={{0,7},{1,4},{2,5},{3,6},{4,15},{5,12},{6,13},{7,14},{8,3},{9,0},{1... | collective-permute-start | bytes 1179656 | tf_op jit(solution)/shard_map/ppermute | solution.py:301
  171.8 7.5 %collective-permute-done.7.refs_4_ = bf16[12,64,256]{2,1,0:T(8,128)(2,1)S(1)} collective-permute-done((bf16[12,64,256]{2,1,0:T(8,128)(2,1)S(1)}, bf16[12,64,256]{2,1,0:T(8,128)(2,1)S(1)}, u32[]{:S(2)}, u32[]{:S(2)}) %collective-permute-start.7) | collective-permute-done | bytes 393248 | tf_op jit(solution)/shard_map/ppermute | solution.py:301
  179.3 4.2 %collective-permute-done.8.refs_5_ = bf16[12,64,256]{2,1,0:T(8,128)(2,1)S(1)} collective-permute-done((bf16[12,64,256]{2,1,0:T(8,128)(2,1)S(1)}, bf16[12,64,256]{2,1,0:T(8,128)(2,1)S(1)}, u32[]{:S(2)}, u32[]{:S(2)}) %collective-permute-start.8) | collective-permute-done | bytes 393248 | tf_op jit(solution)/shard_map/ppermute | solution.py:301
  183.6 3.0 %collective-permute-done.10.refs_7_ = bf16[12,64,256]{2,1,0:T(8,128)(2,1)S(1)} collective-permute-done((bf16[12,64,256]{2,1,0:T(8,128)(2,1)S(1)}, bf16[12,64,256]{2,1,0:T(8,128)(2,1)S(1)}, u32[]{:S(2)}, u32[]{:S(2)}) %collective-permute-start.10) | collective-permute-done | bytes 393248 | tf_op jit(solution)/shard_map/ppermute | solution.py:301
  186.6 2.0 %total.1 = f32[1,12,64,512]{3,2,1,0:T(8,128)} custom-call(s32[2]{0:T(128)S(1)} %pad_add_fusion.1.where, bf16[12,64,256]{2,1,0:T(8,128)(2,1)S(1)} %collective-permute-done.2.refs_0_, bf16[12,64,256]{2,1,0:T(8,128)(2,1)S(1)} %collective-permute-done.3.refs_1_, bf16[12,64,256]{2,1,0:T(8,128)(2,1)S(1)} %collective-permute-done.4.refs_2_, ...), custom_call_target="tpu_custom_call" | custom-call | tf_op jit(solution)/shard_map/total/pallas_call | solution.py:240
  (22 shorter events, 4.5 us)
Async XLA Ops:
  6.2 12.0 %copy-start.2 = (s32[128]{0:T(128)S(1)}, s32[128]{0:T(128)}, u32[]{:S(2)}) copy-start(s32[128]{0:T(128)} %param.5) | copy-start | bytes 1540
  6.2 62.8 %all-to-all-start.1 = ((bf16[128,2,64,128]{3,2,1,0:T(8,128)(2,1)}), bf16[128,2,64,128]{3,2,1,0:T(8,128)(2,1)}, u32[]{:S(2)}, u32[]{:S(2)}) async-start(bf16[128,2,64,128]{3,2,1,0:T(8,128)(2,1)} %bitcast.26), calls=%async_computation.1 | async-start | bytes 8388608 | tf_op jit(solution)/shard_map/all_to_all | solution.py:295
  18.2 47.6 %collective-permute-start = (s32[128]{0:T(128)S(1)}, s32[128]{0:T(128)S(1)}, u32[]{:S(2)}, u32[]{:S(2)}) collective-permute-start(s32[128]{0:T(128)S(1)} %copy-done.2), channel_id=1, source_target_pairs={{0,4},{1,5},{2,6},{3,7},{4,0},{5,1},{6,2},{7,3},{8,12},{9,13},{10,... | collective-permute-start | bytes 1544 | tf_op jit(solution)/shard_map/ppermute | solution.py:277
  69.0 59.0 %all-to-all-start = ((bf16[128,2,64,128]{3,2,1,0:T(8,128)(2,1)}), bf16[128,2,64,128]{3,2,1,0:T(8,128)(2,1)}, u32[]{:S(2)}, u32[]{:S(2)}) async-start(bf16[128,2,64,128]{3,2,1,0:T(8,128)(2,1)} %bitcast.27), calls=%async_computation | async-start | bytes 8388608 | tf_op jit(solution)/shard_map/all_to_all | solution.py:315
  79.0 5.0 %collective-permute-start.1 = (bf16[16,1,4,2,64,128]{5,4,3,2,1,0:T(8,128)(2,1)S(1)}, bf16[16,1,4,2,64,128]{5,4,3,2,1,0:T(8,128)(2,1)S(1)}, u32[]{:S(2)}, u32[]{:S(2)}) collective-permute-start(bf16[16,1,4,2,64,128]{5,4,3,2,1,0:T(8,128)(2,1)S(1)} %constant_dynamic-slice_fusion.1), channel_id=1, source_target_pairs={{0,8},{1,9},{2,10},{3,11},{4,12},{5,13},{6,14},{7,15},{8,0},{9,1},... | collective-permute-start | bytes 6291464 | tf_op jit(solution)/shard_map/ppermute | solution.py:290
  103.0 1.6 copy-start
  129.9 22.0 %collective-permute-start.6 = (bf16[16,1,4,2,64,128]{5,4,3,2,1,0:T(8,128)(2,1)S(1)}, bf16[16,1,4,2,64,128]{5,4,3,2,1,0:T(8,128)(2,1)S(1)}, u32[]{:S(2)}, u32[]{:S(2)}) collective-permute-start(bf16[16,1,4,2,64,128]{5,4,3,2,1,0:T(8,128)(2,1)S(1)} %constant_dynamic-slice_fusion), channel_id=1, source_target_pairs={{0,8},{1,9},{2,10},{3,11},{4,12},{5,13},{6,14},{7,15},{8,0},{9,1},... | collective-permute-start | bytes 6291464 | tf_op jit(solution)/shard_map/ppermute | solution.py:290
  132.6 19.3 %copy-start.1 = (f32[12,256,256]{2,1,0:T(8,128)S(1)}, f32[12,256,256]{2,1,0:T(8,128)}, u32[]{:S(2)}) copy-start(f32[12,256,256]{2,1,0:T(8,128)} %copy-done) | copy-start | bytes 9437188
  145.9 20.2 %collective-permute-start.2 = (bf16[12,64,256]{2,1,0:T(8,128)(2,1)S(1)}, bf16[12,64,256]{2,1,0:T(8,128)(2,1)S(1)}, u32[]{:S(2)}, u32[]{:S(2)}) collective-permute-start(bf16[12,64,256]{2,1,0:T(8,128)(2,1)S(1)} %get-tuple-element.32), channel_id=1, source_target_pairs={{0,6},{1,7},{2,4},{3,5},{4,14},{5,15},{6,12},{7,13},{8,2},{9,3},{1... | collective-permute-start | bytes 1179656 | tf_op jit(solution)/shard_map/ppermute | solution.py:301
  146.1 21.0 %collective-permute-start.3 = (bf16[12,64,256]{2,1,0:T(8,128)(2,1)S(1)}, bf16[12,64,256]{2,1,0:T(8,128)(2,1)S(1)}, u32[]{:S(2)}, u32[]{:S(2)}) collective-permute-start(bf16[12,64,256]{2,1,0:T(8,128)(2,1)S(1)} %get-tuple-element.33), channel_id=1, source_target_pairs={{0,5},{1,6},{2,7},{3,4},{4,13},{5,14},{6,15},{7,12},{8,1},{9,2},{1... | collective-permute-start | bytes 1179656 | tf_op jit(solution)/shard_map/ppermute | solution.py:301
  148.6 22.6 %collective-permute-start.4 = (bf16[12,64,256]{2,1,0:T(8,128)(2,1)S(1)}, bf16[12,64,256]{2,1,0:T(8,128)(2,1)S(1)}, u32[]{:S(2)}, u32[]{:S(2)}) collective-permute-start(bf16[12,64,256]{2,1,0:T(8,128)(2,1)S(1)} %get-tuple-element.34), channel_id=1, source_target_pairs={{0,7},{1,4},{2,5},{3,6},{4,15},{5,12},{6,13},{7,14},{8,3},{9,0},{1... | collective-permute-start | bytes 1179656 | tf_op jit(solution)/shard_map/ppermute | solution.py:301
  150.8 21.0 %collective-permute-start.5 = (bf16[12,64,256]{2,1,0:T(8,128)(2,1)S(1)}, bf16[12,64,256]{2,1,0:T(8,128)(2,1)S(1)}, u32[]{:S(2)}, u32[]{:S(2)}) collective-permute-start(bf16[12,64,256]{2,1,0:T(8,128)(2,1)S(1)} %get-tuple-element.35), channel_id=1, source_target_pairs={{0,4},{1,5},{2,6},{3,7},{4,12},{5,13},{6,14},{7,15},{8,0},{9,1},{1... | collective-permute-start | bytes 1179656 | tf_op jit(solution)/shard_map/ppermute | solution.py:301
  164.3 15.0 %collective-permute-start.7 = (bf16[12,64,256]{2,1,0:T(8,128)(2,1)S(1)}, bf16[12,64,256]{2,1,0:T(8,128)(2,1)S(1)}, u32[]{:S(2)}, u32[]{:S(2)}) collective-permute-start(bf16[12,64,256]{2,1,0:T(8,128)(2,1)S(1)} %get-tuple-element.37), channel_id=1, source_target_pairs={{0,6},{1,7},{2,4},{3,5},{4,14},{5,15},{6,12},{7,13},{8,2},{9,3},{1... | collective-permute-start | bytes 1179656 | tf_op jit(solution)/shard_map/ppermute | solution.py:301
  166.1 17.4 %collective-permute-start.8 = (bf16[12,64,256]{2,1,0:T(8,128)(2,1)S(1)}, bf16[12,64,256]{2,1,0:T(8,128)(2,1)S(1)}, u32[]{:S(2)}, u32[]{:S(2)}) collective-permute-start(bf16[12,64,256]{2,1,0:T(8,128)(2,1)S(1)} %get-tuple-element.38), channel_id=1, source_target_pairs={{0,5},{1,6},{2,7},{3,4},{4,13},{5,14},{6,15},{7,12},{8,1},{9,2},{1... | collective-permute-start | bytes 1179656 | tf_op jit(solution)/shard_map/ppermute | solution.py:301
  167.1 16.5 %collective-permute-start.9 = (bf16[12,64,256]{2,1,0:T(8,128)(2,1)S(1)}, bf16[12,64,256]{2,1,0:T(8,128)(2,1)S(1)}, u32[]{:S(2)}, u32[]{:S(2)}) collective-permute-start(bf16[12,64,256]{2,1,0:T(8,128)(2,1)S(1)} %get-tuple-element.39), channel_id=1, source_target_pairs={{0,7},{1,4},{2,5},{3,6},{4,15},{5,12},{6,13},{7,14},{8,3},{9,0},{1... | collective-permute-start | bytes 1179656 | tf_op jit(solution)/shard_map/ppermute | solution.py:301
  171.2 15.4 %collective-permute-start.10 = (bf16[12,64,256]{2,1,0:T(8,128)(2,1)S(1)}, bf16[12,64,256]{2,1,0:T(8,128)(2,1)S(1)}, u32[]{:S(2)}, u32[]{:S(2)}) collective-permute-start(bf16[12,64,256]{2,1,0:T(8,128)(2,1)S(1)} %get-tuple-element.40), channel_id=1, source_target_pairs={{0,4},{1,5},{2,6},{3,7},{4,12},{5,13},{6,14},{7,15},{8,0},{9,1},{1... | collective-permute-start | bytes 1179656 | tf_op jit(solution)/shard_map/ppermute | solution.py:301

commit v4 on v3

--- a/solution.py
+++ b/solution.py
@@ -16,7 +16,6 @@
 NZ = 4
 CH = 64
 FB = 128
-CHUNKS = ((0, 0, 6), (1, 0, 6))
 HOPS = (2, 1, 3, 0)
 BF = jnp.bfloat16
 F32 = jnp.float32
@@ -78,24 +77,21 @@
     )(pairs, xh, spectra)
 
 
-def turn_and_multiply(group, first, count, where, left, rights, cos_ref, sin_ref, even, odd, flat, add):
+def col(g, comp):
+    return slice((2 * g + comp) * FB, (2 * g + comp + 1) * FB)
+
+
+def turn_and_multiply(group, where, left, cos_ref, sin_ref, even, odd, flat, add, arrive=None, ready=None):
     rows_all = NZ * CH
 
-    def col(g, comp):
-        return slice((2 * g + comp) * FB, (2 * g + comp + 1) * FB)
-
-    for h, right in enumerate(rights):
-        for g in range(group):
-            for comp in range(2):
-                for z in range(NZ):
-                    flat[h * rows_all + z * CH : h * rows_all + (z + 1) * CH, col(g, comp)] = right[g, 0, z, comp]
-
-    def turn(m, turned):
+    def turn(m, turned, arrive=None):
         lag = HALF if isinstance(m, int) and m == 0 else m
         both = lag is m
         cos = jnp.broadcast_to(cos_ref[pl.ds(lag, 1), :], (CH, FB)).astype(BF)
         sin = jnp.broadcast_to(sin_ref[pl.ds(lag, 1), :], (CH, FB)).astype(BF)
         for g in range(group):
+            if arrive is not None:
+                arrive(g)
             for dz in range(NZ):
                 z = where[2 + dz]
                 re = left[g, 0, z, 0]
@@ -110,27 +106,28 @@
 
     def multiply(m, turned):
         product = lax.dot_general(
-            turned[...], flat[...], (((1,), (1,)), ((), ())), preferred_element_type=F32
+            turned[...], flat[...].reshape(-1, flat.shape[-1]), (((1,), (1,)), ((), ())), preferred_element_type=F32
         )
-        add(2 * (m - first), product[:rows_all])
-        add(2 * (m - first) + 1, product[rows_all:])
-
-    turn(first, even)
-    loops = (count - 2) // 2 if count > 4 else 0
+        add(2 * m, product[:rows_all])
+        add(2 * m + 1, product[rows_all:])
+
+    turn(0, even, arrive)
+    if ready is not None:
+        ready()
+    loops = (HALF - 2) // 2
 
     def step(i, carry):
-        m = first + 2 * i + 1
+        m = 2 * i + 1
         turn(m, odd)
         multiply(m - 1, even)
         turn(m + 1, even)
         multiply(m, odd)
         return carry
 
-    if loops:
-        lax.fori_loop(0, loops, step, 0)
+    lax.fori_loop(0, loops, step, 0)
     now, later = even, odd
-    for m in range(first + 2 * loops, first + count):
-        if m + 1 < first + count:
+    for m in range(2 * loops, HALF):
+        if m + 1 < HALF:
             turn(m + 1, later)
         multiply(m, now)
         now, later = later, now
@@ -146,16 +143,58 @@
         own_sum[at] += product[:, : NZ * CH]
         other_sum[at] += product[:, NZ * CH :]
 
-    turn_and_multiply(group, 0, HALF, where, left, (own, other), cos_ref, sin_ref, even, odd, flat, add)
-
-
-def second_kernel(group, first, count, where, left, right, cos_ref, sin_ref, before, o0, o1, o2, o3, even, odd, flat):
+    for h, right in enumerate((own, other)):
+        for g in range(group):
+            for comp in range(2):
+                flat[h * NZ : (h + 1) * NZ, :, col(g, comp)] = right[g, 0, :, comp]
+    turn_and_multiply(group, where, left, cos_ref, sin_ref, even, odd, flat, add)
+
+
+def second_kernel(is_own, where, landed, right, cos_ref, sin_ref, before, o0, o1, o2, o3, *refs):
+    if is_own:
+        mine, *refs = refs
+    left, sums, even, odd, flat, left_sems, right_sems, other_sems = refs
+    group = landed.shape[0]
+    quarter = group // 4
+    lefts = [
+        pltpu.make_async_copy(
+            landed.at[pl.ds(q * quarter, quarter), where[0]], left.at[pl.ds(q * quarter, quarter), 0], left_sems.at[q]
+        )
+        for q in range(4)
+    ]
+    if is_own:
+        rights = [
+            pltpu.make_async_copy(
+                right.at[g, where[1], :, comp], flat.at[:, :, pl.ds((2 * g + comp) * FB, FB)], right_sems.at[g, comp]
+            )
+            for g in range(group)
+            for comp in range(2)
+        ]
+        keep = pltpu.make_async_copy(flat, mine, other_sems.at[1])
+    else:
+        rights = [pltpu.make_async_copy(right.at[z], flat.at[z], right_sems.at[z, 0]) for z in range(NZ)]
+    past = pltpu.make_async_copy(before, sums, other_sems.at[0])
+    for copy in lefts + rights + [past]:
+        copy.start()
+
+    def arrive(g):
+        if g % quarter == 0:
+            lefts[g // quarter].wait()
+
+    def ready():
+        for copy in rights + [past]:
+            copy.wait()
+        if is_own:
+            keep.start()
+
     def add(at, product):
         for dz, out in enumerate((o0, o1, o2, o3)):
             rows = slice(dz * CH, dz * CH + CH)
-            out[at] = ((before[at, rows] + product[rows]) * (1.0 / 128.0)).astype(BF)
-
-    turn_and_multiply(group, first, count, where, left, (right,), cos_ref, sin_ref, even, odd, flat, add)
+            out[at] = ((sums[at, rows] + product[rows]) * (1.0 / 128.0)).astype(BF)
+
+    turn_and_multiply(group, where, left, cos_ref, sin_ref, even, odd, flat, add, arrive, ready)
+    if is_own:
+        keep.wait()
 
 
 SUMS = (LAGS, NZ * CH, NZ * CH)
@@ -186,7 +225,7 @@
             scratch_shapes=[
                 pltpu.VMEM((2 * NZ * CH, 2 * group * FB), BF),
                 pltpu.VMEM((2 * NZ * CH, 2 * group * FB), BF),
-                pltpu.VMEM((2 * NZ * CH, 2 * group * FB), BF),
+                pltpu.VMEM((2 * NZ, CH, 2 * group * FB), BF),
             ],
         ),
         out_shape=[jax.ShapeDtypeStruct(SUMS, F32)] * 2,
@@ -196,38 +235,51 @@
     )(where, landed, landed, theirs, cosine, sine)
 
 
-def second_half(where, landed, right, at, cosine, sine, before, first=0, count=HALF):
+def second_half(where, landed, right, cosine, sine, before):
+    is_own = right is None
     group = landed.shape[0]
-    piece = jax.ShapeDtypeStruct((2 * count, CH, NZ * CH), BF)
+    width = 2 * group * FB
+    piece = jax.ShapeDtypeStruct((LAGS, CH, NZ * CH), BF)
+    out_specs, out_shape = [whole(piece.shape)] * NZ, [piece] * NZ
+    anywhere = pl.BlockSpec(memory_space=pl.ANY)
+    if is_own:
+        right = landed
+        out_specs = out_specs + [anywhere]
+        out_shape = out_shape + [jax.ShapeDtypeStruct((NZ, CH, width), BF)]
     return pl.pallas_call(
-        functools.partial(second_kernel, group, first, count),
+        functools.partial(second_kernel, is_own),
         grid_spec=pltpu.PrefetchScalarGridSpec(
             num_scalar_prefetch=1,
             grid=(1,),
-            in_specs=[spec(group, 0), spec(group, at), table_spec(), table_spec(), whole((2 * count, *SUMS[1:]), first // count)],
-            out_specs=[whole(piece.shape)] * NZ,
+            in_specs=[anywhere, anywhere, table_spec(), table_spec(), anywhere],
+            out_specs=out_specs,
             scratch_shapes=[
-                pltpu.VMEM((2 * NZ * CH, 2 * group * FB), BF),
-                pltpu.VMEM((2 * NZ * CH, 2 * group * FB), BF),
-                pltpu.VMEM((NZ * CH, 2 * group * FB), BF),
+                pltpu.VMEM((group, 1, NZ, 2, CH, FB), BF),
+                pltpu.VMEM(SUMS, F32),
+                pltpu.VMEM((2 * NZ * CH, width), BF),
+                pltpu.VMEM((2 * NZ * CH, width), BF),
+                pltpu.VMEM((NZ, CH, width), BF),
+                pltpu.SemaphoreType.DMA((4,)),
+                pltpu.SemaphoreType.DMA((group, 2)),
+                pltpu.SemaphoreType.DMA((2,)),
             ],
         ),
-        out_shape=[piece] * NZ,
+        out_shape=out_shape,
         compiler_params=pltpu.CompilerParams(vmem_limit_bytes=40 * 2**20),
-        cost_estimate=pl.CostEstimate(flops=count * 11 * 10**8, bytes_accessed=8 * 2**20, transcendentals=0),
+        cost_estimate=pl.CostEstimate(flops=65 * 10**8, bytes_accessed=8 * 2**20, transcendentals=0),
         name="second_half",
     )(where, landed, right, cosine, sine, before)
 
 
-def total_kernel(chunks, where, *refs):
+def total_kernel(where, *refs):
     out = refs[-1]
     width = NZ * CH
-    for k, (half, first, count) in enumerate(chunks):
+    for half in range(2):
         at = pl.multiple_of(where[half] * width, width)
-        group = refs[k * NZ : (k + 1) * NZ]
-        for m in range(first, first + count):
+        group = refs[half * NZ : (half + 1) * NZ]
+        for m in range(HALF):
             for sign in range(2):
-                i = 2 * (m - first) + sign
+                i = 2 * m + sign
                 val = group[0][i].astype(F32)
                 for ref in group[1:]:
                     val = val + ref[i].astype(F32)
@@ -235,10 +287,10 @@
                 out[0, lag, :, pl.ds(at, width)] = val
 
 
-def total(where, chunks, parts):
+def total(where, parts):
     shape = (1, LAGS, CH, 2 * NZ * CH)
     return pl.pallas_call(
-        functools.partial(total_kernel, chunks),
+        total_kernel,
         grid_spec=pltpu.PrefetchScalarGridSpec(
             num_scalar_prefetch=1,
             grid=(1,),
@@ -315,13 +367,11 @@
     landed1 = lax.all_to_all(packed1.reshape(128, 2, CH, FB), both, split_axis=0, concat_axis=0, tiled=True)
     landed1, own, other = lax.optimization_barrier((landed1, own, other))
     landed1 = landed1.reshape(16, 2, NZ, 2, CH, FB)
-    theirs1 = swap(lax.dynamic_slice_in_dim(landed1, core, 1, axis=1))
-    chunks = CHUNKS
-    parts = []
-    for half, first, count in chunks:
-        right, at, before = (landed1, 1, own) if half == 0 else (theirs1, None, other)
-        parts += send(second_half(where, landed1, right, at, cosine[1], sine[1], before, first, count))
-    return jnp.transpose(total(halves, chunks, parts), (0, 2, 1, 3))
+    *first, mine1 = second_half(where, landed1, None, cosine[1], sine[1], own)
+    theirs1 = swap(mine1)
+    first = send(first)
+    second = send(second_half(where, landed1, theirs1, cosine[1], sine[1], other))
+    return jnp.transpose(total(halves, first + second), (0, 2, 1, 3))
 
 
 def solution(mesh):

time: 190 us -> 186 us (0.979)
  transfers between devices with their start and end apart: 13 -> 13, of which waited for: 8 -> 8; matrix products, arithmetic and copies ran while one was open for 1% -> 1% of each run, Pallas kernels for 27% -> 20%
where the time goes in v4:
time: 186 us; the launch traced here: 185 us
  waiting for transfers between devices  83 us (45%)
  Pallas kernels  57.9 us (31%)
  starting transfers between devices  40.4 us (22%)
  local copies, waits for them, and re-layouts  3.5 us (2%)
    ppermute x1, waiting for transfers between devices, body(): lax.ppermute(band_bins, both, [(index(*p), index(p[0], p[1], p[2], 1 - p[...  38 us
    pallas_call x2, Pallas kernels, second_half(): pl.pallas_call(functools.partial(second_kernel, is_own), grid_spec=pltpu....  24 us
    all_to_all x1, waiting for transfers between devices, body(): lax.all_to_all(packed1.reshape(128, 2, CH, FB), both, split_axis=0, conca...  23.2 us
    pallas_call x1, Pallas kernels, first_half(): pl.pallas_call(functools.partial(first_kernel, group), grid_spec=pltpu.Pr...  19 us
    ppermute x8, waiting for transfers between devices, send(): lax.ppermute(part, both, [(index(*p), index(p[0], p[1], p[3], 1 - p[2], (...  14.9 us
    ppermute x8, starting transfers between devices, send(): lax.ppermute(part, both, [(index(*p), index(p[0], p[1], p[3], 1 - p[2], (...  13.4 us
    pallas_call x2, Pallas kernels, pack(): pl.pallas_call(functools.partial(pack_kernel, group, part), grid_spec=plt...  12.8 us
    all_to_all x1, starting transfers between devices, exchange(): lax.all_to_all(packed.reshape(128, 2, CH, FB), both, split_axis=0, concat...  12 us
  transfers between devices with their start and end apart: 13, of which 8 were waited for; matrix products, arithmetic and copies ran while one was open for 1% of the time, Pallas kernels for 20%

profile of v4, /device:TPU:1, one launch (start us, length us, event | category | flops | bytes accessed | tf_op | source)
XLA Modules:
  0.0 185.1 jit_solution(16727894825506298166)
XLA Ops:
  0.0 6.4 %pack.3 = bf16[8,2,2,4,2,64,128]{6,5,4,3,2,1,0:T(8,128)(2,1)} custom-call(s32[2,16]{1,0:T(2,128)} %bitcast.28, s32[1]{0:T(128)} %bitcast.1.xh, bf16[2,1,16,64,1024]{4,3,2,1,0:T(8,128)(2,1)} %block.3), custom_call_target="tpu_custom_call" | custom-call | flops 16777216 | bytes 8388608 | tf_op jit(solution)/shard_map/pack/pallas_call | solution.py:61
  6.4 12.0 %all-to-all-start.1 = ((bf16[128,2,64,128]{3,2,1,0:T(8,128)(2,1)}), bf16[128,2,64,128]{3,2,1,0:T(8,128)(2,1)}, u32[]{:S(2)}, u32[]{:S(2)}) async-start(bf16[128,2,64,128]{3,2,1,0:T(8,128)(2,1)} %bitcast.26), calls=%async_computation.1 | async-start | bytes 8388608 | tf_op jit(solution)/shard_map/all_to_all | solution.py:347
  18.4 3.0 %collective-permute-start = (s32[128]{0:T(128)S(1)}, s32[128]{0:T(128)S(1)}, u32[]{:S(2)}, u32[]{:S(2)}) collective-permute-start(s32[128]{0:T(128)S(1)} %copy-done.2), channel_id=1, source_target_pairs={{0,4},{1,5},{2,6},{3,7},{4,0},{5,1},{6,2},{7,3},{8,12},{9,13},{10,... | collective-permute-start | bytes 1544 | tf_op jit(solution)/shard_map/ppermute | solution.py:329
  21.3 6.4 %pack.2 = bf16[8,2,2,4,2,64,128]{6,5,4,3,2,1,0:T(8,128)(2,1)} custom-call(s32[2,16]{1,0:T(2,128)} %bitcast.29, s32[1]{0:T(128)} %bitcast.1.xh, bf16[2,1,16,64,1024]{4,3,2,1,0:T(8,128)(2,1)} %block.3), custom_call_target="tpu_custom_call" | custom-call | flops 16777216 | bytes 8388608 | tf_op jit(solution)/shard_map/pack/pallas_call | solution.py:61
  27.9 38.0 %collective-permute-done = s32[128]{0:T(128)S(1)} collective-permute-done((s32[128]{0:T(128)S(1)}, s32[128]{0:T(128)S(1)}, u32[]{:S(2)}, u32[]{:S(2)}) %collective-permute-start) | collective-permute-done | bytes 544 | tf_op jit(solution)/shard_map/ppermute | solution.py:329
  66.0 3.2 %all-to-all-done.1 = bf16[128,2,64,128]{3,2,1,0:T(8,128)(2,1)} async-done(((bf16[128,2,64,128]{3,2,1,0:T(8,128)(2,1)}), bf16[128,2,64,128]{3,2,1,0:T(8,128)(2,1)}, u32[]{:S(2)}, u32[]{:S(2)}) %all-to-all-start.1) | async-done | bytes 4194336 | tf_op jit(solution)/shard_map/all_to_all | solution.py:347
  69.2 8.2 %all-to-all-start = ((bf16[128,2,64,128]{3,2,1,0:T(8,128)(2,1)}), bf16[128,2,64,128]{3,2,1,0:T(8,128)(2,1)}, u32[]{:S(2)}, u32[]{:S(2)}) async-start(bf16[128,2,64,128]{3,2,1,0:T(8,128)(2,1)} %bitcast.27), calls=%async_computation | async-start | bytes 8388608 | tf_op jit(solution)/shard_map/all_to_all | solution.py:367
  77.4 1.8 constant_dynamic-slice_fusion
  79.2 1.4 collective-permute-start.1
  80.6 3.8 %collective-permute-done.1.other = bf16[16,1,4,2,64,128]{5,4,3,2,1,0:T(8,128)(2,1)S(1)} collective-permute-done((bf16[16,1,4,2,64,128]{5,4,3,2,1,0:T(8,128)(2,1)S(1)}, bf16[16,1,4,2,64,128]{5,4,3,2,1,0:T(8,128)(2,1)S(1)}, u32[]{:S(2)}, u32[]{:S(2)}) %collective-permute-start.1) | collective-permute-done | bytes 2097184 | tf_op jit(solution)/shard_map/ppermute | solution.py:342
  84.3 19.0 %first_half.1 = (f32[12,256,256]{2,1,0:T(8,128)S(1)}, f32[12,256,256]{2,1,0:T(8,128)S(1)}) custom-call(s32[6]{0:T(128)S(1)} %stack.46.where, bf16[16,2,4,2,64,128]{5,4,3,2,1,0:T(8,128)(2,1)} %bitcast.13.left.own, bf16[16,2,4,2,64,128]{5,4,3,2,1,0:T(8,128)(2,1)} %bitcast.13.left.own, bf16[16,1,4,2,64,128]{5,4,3,2,1,0:T(8,128)(2,1)S(1)} %collective-permute-done.1.other, ...), custom_call_target="tpu_custom_call" | custom-call | flops 12999999488 | bytes 12582912 | tf_op jit(solution)/shard_map/first_half/pallas_call | solution.py:218
  103.4 1.6 copy-done
  105.0 23.2 %all-to-all-done = bf16[128,2,64,128]{3,2,1,0:T(8,128)(2,1)} async-done(((bf16[128,2,64,128]{3,2,1,0:T(8,128)(2,1)}), bf16[128,2,64,128]{3,2,1,0:T(8,128)(2,1)}, u32[]{:S(2)}, u32[]{:S(2)}) %all-to-all-start) | async-done | bytes 4194336 | tf_op jit(solution)/shard_map/all_to_all | solution.py:367
  128.2 12.4 %second_half.2 = (bf16[12,64,256]{2,1,0:T(8,128)(2,1)S(1)}, bf16[12,64,256]{2,1,0:T(8,128)(2,1)S(1)}, bf16[12,64,256]{2,1,0:T(8,128)(2,1)S(1)}, bf16[12,64,256]{2,1,0:T(8,128)(2,1)S(1)}, bf16[4,64,4096]{2,1,0:T(8,128)(2,1)S(1)}) custom-call(s32[6]{0:T(128)S(1)} %stack.46.where, bf16[16,2,4,2,64,128]{5,4,3,2,1,0:T(8,128)(2,1)} %bitcast.16.landed.right, ...), custom_call_target="tpu_custom_call" | custom-call | flops 6499999744 | bytes 8388608 | tf_op jit(solution)/shard_map/second_half/pallas_call | solution.py:249
  140.7 2.5 %collective-permute-start.6 = (bf16[4,64,4096]{2,1,0:T(8,128)(2,1)S(1)}, bf16[4,64,4096]{2,1,0:T(8,128)(2,1)S(1)}, u32[]{:S(2)}, u32[]{:S(2)}) collective-permute-start(bf16[4,64,4096]{2,1,0:T(8,128)(2,1)S(1)} %get-tuple-element.37), channel_id=1, source_target_pairs={{0,8},{1,9},{2,10},{3,11},{4,12},{5,13},{6,14},{7,15},{8,0},{9,1},... | collective-permute-start | bytes 6291464 | tf_op jit(solution)/shard_map/ppermute | solution.py:342
  143.3 2.5 %collective-permute-start.3 = (bf16[12,64,256]{2,1,0:T(8,128)(2,1)S(1)}, bf16[12,64,256]{2,1,0:T(8,128)(2,1)S(1)}, u32[]{:S(2)}, u32[]{:S(2)}) collective-permute-start(bf16[12,64,256]{2,1,0:T(8,128)(2,1)S(1)} %get-tuple-element.34), channel_id=1, source_target_pairs={{0,5},{1,6},{2,7},{3,4},{4,13},{5,14},{6,15},{7,12},{8,1},{9,2},{1... | collective-permute-start | bytes 1179656 | tf_op jit(solution)/shard_map/ppermute | solution.py:353
  145.9 2.1 %collective-permute-start.4 = (bf16[12,64,256]{2,1,0:T(8,128)(2,1)S(1)}, bf16[12,64,256]{2,1,0:T(8,128)(2,1)S(1)}, u32[]{:S(2)}, u32[]{:S(2)}) collective-permute-start(bf16[12,64,256]{2,1,0:T(8,128)(2,1)S(1)} %get-tuple-element.35), channel_id=1, source_target_pairs={{0,7},{1,4},{2,5},{3,6},{4,15},{5,12},{6,13},{7,14},{8,3},{9,0},{1... | collective-permute-start | bytes 1179656 | tf_op jit(solution)/shard_map/ppermute | solution.py:353
  149.1 11.6 %second_half.3 = (bf16[12,64,256]{2,1,0:T(8,128)(2,1)S(1)}, bf16[12,64,256]{2,1,0:T(8,128)(2,1)S(1)}, bf16[12,64,256]{2,1,0:T(8,128)(2,1)S(1)}, bf16[12,64,256]{2,1,0:T(8,128)(2,1)S(1)}) custom-call(s32[6]{0:T(128)S(1)} %stack.46.where, bf16[16,2,4,2,64,128]{5,4,3,2,1,0:T(8,128)(2,1)} %bitcast.16.landed.right, ...), custom_call_target="tpu_custom_call" | custom-call | flops 6499999744 | bytes 8388608 | tf_op jit(solution)/shard_map/second_half/pallas_call | solution.py:249
  160.7 1.8 collective-permute-start.7
  163.5 4.1 %collective-permute-start.9 = (bf16[12,64,256]{2,1,0:T(8,128)(2,1)S(1)}, bf16[12,64,256]{2,1,0:T(8,128)(2,1)S(1)}, u32[]{:S(2)}, u32[]{:S(2)}) collective-permute-start(bf16[12,64,256]{2,1,0:T(8,128)(2,1)S(1)} %get-tuple-element.41), channel_id=1, source_target_pairs={{0,7},{1,4},{2,5},{3,6},{4,15},{5,12},{6,13},{7,14},{8,3},{9,0},{1... | collective-permute-start | bytes 1179656 | tf_op jit(solution)/shard_map/ppermute | solution.py:353
  168.2 7.6 %collective-permute-done.7.refs_4_ = bf16[12,64,256]{2,1,0:T(8,128)(2,1)S(1)} collective-permute-done((bf16[12,64,256]{2,1,0:T(8,128)(2,1)S(1)}, bf16[12,64,256]{2,1,0:T(8,128)(2,1)S(1)}, u32[]{:S(2)}, u32[]{:S(2)}) %collective-permute-start.7) | collective-permute-done | bytes 393248 | tf_op jit(solution)/shard_map/ppermute | solution.py:353
  175.7 4.2 %collective-permute-done.8.refs_5_ = bf16[12,64,256]{2,1,0:T(8,128)(2,1)S(1)} collective-permute-done((bf16[12,64,256]{2,1,0:T(8,128)(2,1)S(1)}, bf16[12,64,256]{2,1,0:T(8,128)(2,1)S(1)}, u32[]{:S(2)}, u32[]{:S(2)}) %collective-permute-start.8) | collective-permute-done | bytes 393248 | tf_op jit(solution)/shard_map/ppermute | solution.py:353
  180.1 2.9 %collective-permute-done.10.refs_7_ = bf16[12,64,256]{2,1,0:T(8,128)(2,1)S(1)} collective-permute-done((bf16[12,64,256]{2,1,0:T(8,128)(2,1)S(1)}, bf16[12,64,256]{2,1,0:T(8,128)(2,1)S(1)}, u32[]{:S(2)}, u32[]{:S(2)}) %collective-permute-start.10) | collective-permute-done | bytes 393248 | tf_op jit(solution)/shard_map/ppermute | solution.py:353
  183.0 2.0 %total.1 = f32[1,12,64,512]{3,2,1,0:T(8,128)} custom-call(s32[2]{0:T(128)S(1)} %pad_add_fusion.1.where, bf16[12,64,256]{2,1,0:T(8,128)(2,1)S(1)} %collective-permute-done.2.refs_0_, bf16[12,64,256]{2,1,0:T(8,128)(2,1)S(1)} %collective-permute-done.3.refs_1_, bf16[12,64,256]{2,1,0:T(8,128)(2,1)S(1)} %collective-permute-done.4.refs_2_, ...), custom_call_target="tpu_custom_call" | custom-call | tf_op jit(solution)/shard_map/total/pallas_call | solution.py:292
  (21 shorter events, 3.2 us)
Async XLA Ops:
  6.4 12.0 %copy-start.2 = (s32[128]{0:T(128)S(1)}, s32[128]{0:T(128)}, u32[]{:S(2)}) copy-start(s32[128]{0:T(128)} %param.5) | copy-start | bytes 1540
  6.4 62.8 %all-to-all-start.1 = ((bf16[128,2,64,128]{3,2,1,0:T(8,128)(2,1)}), bf16[128,2,64,128]{3,2,1,0:T(8,128)(2,1)}, u32[]{:S(2)}, u32[]{:S(2)}) async-start(bf16[128,2,64,128]{3,2,1,0:T(8,128)(2,1)} %bitcast.26), calls=%async_computation.1 | async-start | bytes 8388608 | tf_op jit(solution)/shard_map/all_to_all | solution.py:347
  18.4 47.6 %collective-permute-start = (s32[128]{0:T(128)S(1)}, s32[128]{0:T(128)S(1)}, u32[]{:S(2)}, u32[]{:S(2)}) collective-permute-start(s32[128]{0:T(128)S(1)} %copy-done.2), channel_id=1, source_target_pairs={{0,4},{1,5},{2,6},{3,7},{4,0},{5,1},{6,2},{7,3},{8,12},{9,13},{10,... | collective-permute-start | bytes 1544 | tf_op jit(solution)/shard_map/ppermute | solution.py:329
  69.2 59.0 %all-to-all-start = ((bf16[128,2,64,128]{3,2,1,0:T(8,128)(2,1)}), bf16[128,2,64,128]{3,2,1,0:T(8,128)(2,1)}, u32[]{:S(2)}, u32[]{:S(2)}) async-start(bf16[128,2,64,128]{3,2,1,0:T(8,128)(2,1)} %bitcast.27), calls=%async_computation | async-start | bytes 8388608 | tf_op jit(solution)/shard_map/all_to_all | solution.py:367
  79.2 5.2 %collective-permute-start.1 = (bf16[16,1,4,2,64,128]{5,4,3,2,1,0:T(8,128)(2,1)S(1)}, bf16[16,1,4,2,64,128]{5,4,3,2,1,0:T(8,128)(2,1)S(1)}, u32[]{:S(2)}, u32[]{:S(2)}) collective-permute-start(bf16[16,1,4,2,64,128]{5,4,3,2,1,0:T(8,128)(2,1)S(1)} %constant_dynamic-slice_fusion), channel_id=1, source_target_pairs={{0,8},{1,9},{2,10},{3,11},{4,12},{5,13},{6,14},{7,15},{8,0},{9,1},... | collective-permute-start | bytes 6291464 | tf_op jit(solution)/shard_map/ppermute | solution.py:342
  103.4 1.6 copy-start
  128.2 20.9 %copy-start.1 = (f32[12,256,256]{2,1,0:T(8,128)S(1)}, f32[12,256,256]{2,1,0:T(8,128)}, u32[]{:S(2)}) copy-start(f32[12,256,256]{2,1,0:T(8,128)} %copy-done) | copy-start | bytes 9437188
  140.7 8.5 %collective-permute-start.6 = (bf16[4,64,4096]{2,1,0:T(8,128)(2,1)S(1)}, bf16[4,64,4096]{2,1,0:T(8,128)(2,1)S(1)}, u32[]{:S(2)}, u32[]{:S(2)}) collective-permute-start(bf16[4,64,4096]{2,1,0:T(8,128)(2,1)S(1)} %get-tuple-element.37), channel_id=1, source_target_pairs={{0,8},{1,9},{2,10},{3,11},{4,12},{5,13},{6,14},{7,15},{8,0},{9,1},... | collective-permute-start | bytes 6291464 | tf_op jit(solution)/shard_map/ppermute | solution.py:342
  143.2 19.4 %collective-permute-start.2 = (bf16[12,64,256]{2,1,0:T(8,128)(2,1)S(1)}, bf16[12,64,256]{2,1,0:T(8,128)(2,1)S(1)}, u32[]{:S(2)}, u32[]{:S(2)}) collective-permute-start(bf16[12,64,256]{2,1,0:T(8,128)(2,1)S(1)} %get-tuple-element.33), channel_id=1, source_target_pairs={{0,6},{1,7},{2,4},{3,5},{4,14},{5,15},{6,12},{7,13},{8,2},{9,3},{1... | collective-permute-start | bytes 1179656 | tf_op jit(solution)/shard_map/ppermute | solution.py:353
  143.3 20.2 %collective-permute-start.3 = (bf16[12,64,256]{2,1,0:T(8,128)(2,1)S(1)}, bf16[12,64,256]{2,1,0:T(8,128)(2,1)S(1)}, u32[]{:S(2)}, u32[]{:S(2)}) collective-permute-start(bf16[12,64,256]{2,1,0:T(8,128)(2,1)S(1)} %get-tuple-element.34), channel_id=1, source_target_pairs={{0,5},{1,6},{2,7},{3,4},{4,13},{5,14},{6,15},{7,12},{8,1},{9,2},{1... | collective-permute-start | bytes 1179656 | tf_op jit(solution)/shard_map/ppermute | solution.py:353
  145.9 21.7 %collective-permute-start.4 = (bf16[12,64,256]{2,1,0:T(8,128)(2,1)S(1)}, bf16[12,64,256]{2,1,0:T(8,128)(2,1)S(1)}, u32[]{:S(2)}, u32[]{:S(2)}) collective-permute-start(bf16[12,64,256]{2,1,0:T(8,128)(2,1)S(1)} %get-tuple-element.35), channel_id=1, source_target_pairs={{0,7},{1,4},{2,5},{3,6},{4,15},{5,12},{6,13},{7,14},{8,3},{9,0},{1... | collective-permute-start | bytes 1179656 | tf_op jit(solution)/shard_map/ppermute | solution.py:353
  148.0 20.2 %collective-permute-start.5 = (bf16[12,64,256]{2,1,0:T(8,128)(2,1)S(1)}, bf16[12,64,256]{2,1,0:T(8,128)(2,1)S(1)}, u32[]{:S(2)}, u32[]{:S(2)}) collective-permute-start(bf16[12,64,256]{2,1,0:T(8,128)(2,1)S(1)} %get-tuple-element.36), channel_id=1, source_target_pairs={{0,4},{1,5},{2,6},{3,7},{4,12},{5,13},{6,14},{7,15},{8,0},{9,1},{1... | collective-permute-start | bytes 1179656 | tf_op jit(solution)/shard_map/ppermute | solution.py:353
  160.7 15.0 %collective-permute-start.7 = (bf16[12,64,256]{2,1,0:T(8,128)(2,1)S(1)}, bf16[12,64,256]{2,1,0:T(8,128)(2,1)S(1)}, u32[]{:S(2)}, u32[]{:S(2)}) collective-permute-start(bf16[12,64,256]{2,1,0:T(8,128)(2,1)S(1)} %get-tuple-element.39), channel_id=1, source_target_pairs={{0,6},{1,7},{2,4},{3,5},{4,14},{5,15},{6,12},{7,13},{8,2},{9,3},{1... | collective-permute-start | bytes 1179656 | tf_op jit(solution)/shard_map/ppermute | solution.py:353
  162.6 17.4 %collective-permute-start.8 = (bf16[12,64,256]{2,1,0:T(8,128)(2,1)S(1)}, bf16[12,64,256]{2,1,0:T(8,128)(2,1)S(1)}, u32[]{:S(2)}, u32[]{:S(2)}) collective-permute-start(bf16[12,64,256]{2,1,0:T(8,128)(2,1)S(1)} %get-tuple-element.40), channel_id=1, source_target_pairs={{0,5},{1,6},{2,7},{3,4},{4,13},{5,14},{6,15},{7,12},{8,1},{9,2},{1... | collective-permute-start | bytes 1179656 | tf_op jit(solution)/shard_map/ppermute | solution.py:353
  163.5 16.5 %collective-permute-start.9 = (bf16[12,64,256]{2,1,0:T(8,128)(2,1)S(1)}, bf16[12,64,256]{2,1,0:T(8,128)(2,1)S(1)}, u32[]{:S(2)}, u32[]{:S(2)}) collective-permute-start(bf16[12,64,256]{2,1,0:T(8,128)(2,1)S(1)} %get-tuple-element.41), channel_id=1, source_target_pairs={{0,7},{1,4},{2,5},{3,6},{4,15},{5,12},{6,13},{7,14},{8,3},{9,0},{1... | collective-permute-start | bytes 1179656 | tf_op jit(solution)/shard_map/ppermute | solution.py:353
  167.6 15.4 %collective-permute-start.10 = (bf16[12,64,256]{2,1,0:T(8,128)(2,1)S(1)}, bf16[12,64,256]{2,1,0:T(8,128)(2,1)S(1)}, u32[]{:S(2)}, u32[]{:S(2)}) collective-permute-start(bf16[12,64,256]{2,1,0:T(8,128)(2,1)S(1)} %get-tuple-element.42), channel_id=1, source_target_pairs={{0,4},{1,5},{2,6},{3,7},{4,12},{5,13},{6,14},{7,15},{8,0},{9,1},{1... | collective-permute-start | bytes 1179656 | tf_op jit(solution)/shard_map/ppermute | solution.py:353

commit v5 on v4

--- a/solution.py
+++ b/solution.py
@@ -57,7 +57,7 @@
 
 def pack(spectra, pairs, xh, part):
     blocks = spectra.shape[2]
-    group = 4
+    group = 8
     return pl.pallas_call(
         functools.partial(pack_kernel, group, part),
         grid_spec=pltpu.PrefetchScalarGridSpec(
@@ -133,7 +133,7 @@
         now, later = later, now
 
 
-def first_kernel(group, where, left, own, other, cos_ref, sin_ref, own_sum, other_sum, even, odd, flat):
+def first_kernel(group, where, left, own, other, cos_ref, sin_ref, own_out, other_out, own_sum, other_sum, even, odd, flat):
     @pl.when(pl.program_id(0) == 0)
     def _():
         own_sum[...] = jnp.zeros_like(own_sum)
@@ -148,6 +148,11 @@
             for comp in range(2):
                 flat[h * NZ : (h + 1) * NZ, :, col(g, comp)] = right[g, 0, :, comp]
     turn_and_multiply(group, where, left, cos_ref, sin_ref, even, odd, flat, add)
+
+    @pl.when(pl.program_id(0) == pl.num_programs(0) - 1)
+    def _():
+        own_out[...] = own_sum[...].astype(BF)
+        other_out[...] = other_sum[...].astype(BF)
 
 
 def second_kernel(is_own, where, landed, right, cos_ref, sin_ref, before, o0, o1, o2, o3, *refs):
@@ -190,7 +195,7 @@
     def add(at, product):
         for dz, out in enumerate((o0, o1, o2, o3)):
             rows = slice(dz * CH, dz * CH + CH)
-            out[at] = ((sums[at, rows] + product[rows]) * (1.0 / 128.0)).astype(BF)
+            out[at] = ((sums[at, rows].astype(F32) + product[rows]) * (1.0 / 128.0)).astype(BF)
 
     turn_and_multiply(group, where, left, cos_ref, sin_ref, even, odd, flat, add, arrive, ready)
     if is_own:
@@ -223,12 +228,14 @@
             in_specs=[spec(group, 0), spec(group, 1), spec(group), table_spec(), table_spec()],
             out_specs=[whole(SUMS)] * 2,
             scratch_shapes=[
+                pltpu.VMEM(SUMS, F32),
+                pltpu.VMEM(SUMS, F32),
                 pltpu.VMEM((2 * NZ * CH, 2 * group * FB), BF),
                 pltpu.VMEM((2 * NZ * CH, 2 * group * FB), BF),
                 pltpu.VMEM((2 * NZ, CH, 2 * group * FB), BF),
             ],
         ),
-        out_shape=[jax.ShapeDtypeStruct(SUMS, F32)] * 2,
+        out_shape=[jax.ShapeDtypeStruct(SUMS, BF)] * 2,
         compiler_params=pltpu.CompilerParams(vmem_limit_bytes=40 * 2**20),
         cost_estimate=pl.CostEstimate(flops=13 * 10**9, bytes_accessed=12 * 2**20, transcendentals=0),
         name="first_half",
@@ -255,7 +262,7 @@
             out_specs=out_specs,
             scratch_shapes=[
                 pltpu.VMEM((group, 1, NZ, 2, CH, FB), BF),
-                pltpu.VMEM(SUMS, F32),
+                pltpu.VMEM(SUMS, BF),
                 pltpu.VMEM((2 * NZ * CH, width), BF),
                 pltpu.VMEM((2 * NZ * CH, width), BF),
                 pltpu.VMEM((NZ, CH, width), BF),
@@ -273,34 +280,34 @@
 
 def total_kernel(where, *refs):
     out = refs[-1]
-    width = NZ * CH
-    for half in range(2):
-        at = pl.multiple_of(where[half] * width, width)
-        group = refs[half * NZ : (half + 1) * NZ]
-        for m in range(HALF):
-            for sign in range(2):
-                i = 2 * m + sign
-                val = group[0][i].astype(F32)
-                for ref in group[1:]:
-                    val = val + ref[i].astype(F32)
-                lag = HALF + m if sign else (HALF - m if m else 0)
-                out[0, lag, :, pl.ds(at, width)] = val
-
-
-def total(where, parts):
+    group = refs[:NZ]
+    for m in range(HALF):
+        for sign in range(2):
+            i = 2 * m + sign
+            val = group[0][i].astype(F32)
+            for ref in group[1:]:
+                val = val + ref[i].astype(F32)
+            lag = HALF + m if sign else (HALF - m if m else 0)
+            out[0, lag] = val
+
+
+def total(where, half, parts, filled=None):
     shape = (1, LAGS, CH, 2 * NZ * CH)
+    given = [] if filled is None else [filled]
     return pl.pallas_call(
         total_kernel,
         grid_spec=pltpu.PrefetchScalarGridSpec(
             num_scalar_prefetch=1,
             grid=(1,),
-            in_specs=[pl.BlockSpec(part.shape, lambda i, where: (0, 0, 0)) for part in parts],
-            out_specs=pl.BlockSpec(shape, lambda i, where: (0, 0, 0, 0)),
+            in_specs=[pl.BlockSpec(part.shape, lambda i, where: (0, 0, 0)) for part in parts]
+            + [pl.BlockSpec(memory_space=pl.ANY)] * len(given),
+            out_specs=pl.BlockSpec((1, LAGS, CH, NZ * CH), lambda i, where: (0, 0, 0, where[half])),
         ),
         out_shape=jax.ShapeDtypeStruct(shape, F32),
+        input_output_aliases={1 + len(parts): 0} if given else {},
         compiler_params=pltpu.CompilerParams(vmem_limit_bytes=32 * 2**20),
         name="total",
-    )(where, *parts)
+    )(where, *parts, *given)
 
 
 def places():
@@ -371,7 +378,8 @@
     theirs1 = swap(mine1)
     first = send(first)
     second = send(second_half(where, landed1, theirs1, cosine[1], sine[1], other))
-    return jnp.transpose(total(halves, first + second), (0, 2, 1, 3))
+    filled = total(halves, 1, second, total(halves, 0, first))
+    return jnp.transpose(filled, (0, 2, 1, 3))
 
 
 def solution(mesh):

time: 186 us -> 184 us (0.989)
    pallas_call x2, Pallas kernels: 12.8 us -> 10.4 us  [pack(): pl.pallas_call(functools.partial(pack_kernel, group, part), grid_spec=plt...]
  transfers between devices with their start and end apart: 13 -> 13, of which waited for: 8 -> 8; matrix products, arithmetic and copies ran while one was open for 1% -> 1% of each run, Pallas kernels for 20% -> 21%
where the time goes in v5:
time: 184 us; the launch traced here: 183 us
  waiting for transfers between devices  84.1 us (46%)
  Pallas kernels  56.6 us (31%)
  starting transfers between devices  40.4 us (22%)
  local copies, waits for them, and re-layouts  1.86 us (1%)
    ppermute x1, waiting for transfers between devices, body(): lax.ppermute(band_bins, both, [(index(*p), index(p[0], p[1], p[2], 1 - p[...  39.2 us
    all_to_all x1, waiting for transfers between devices, body(): lax.all_to_all(packed1.reshape(128, 2, CH, FB), both, split_axis=0, conca...  24.6 us
    pallas_call x2, Pallas kernels, second_half(): pl.pallas_call(functools.partial(second_kernel, is_own), grid_spec=pltpu....  23.8 us
    pallas_call x1, Pallas kernels, first_half(): pl.pallas_call(functools.partial(first_kernel, group), grid_spec=pltpu.Pr...  19.2 us
    ppermute x8, starting transfers between devices, send(): lax.ppermute(part, both, [(index(*p), index(p[0], p[1], p[3], 1 - p[2], (...  13.3 us
    ppermute x8, waiting for transfers between devices, send(): lax.ppermute(part, both, [(index(*p), index(p[0], p[1], p[3], 1 - p[2], (...  13.3 us
    all_to_all x1, starting transfers between devices, exchange(): lax.all_to_all(packed.reshape(128, 2, CH, FB), both, split_axis=0, concat...  11.9 us
    pallas_call x2, Pallas kernels, pack(): pl.pallas_call(functools.partial(pack_kernel, group, part), grid_spec=plt...  10.4 us
  transfers between devices with their start and end apart: 13, of which 8 were waited for; matrix products, arithmetic and copies ran while one was open for 1% of the time, Pallas kernels for 21%

profile of v5, /device:TPU:1, one launch (start us, length us, event | category | flops | bytes accessed | tf_op | source)
XLA Modules:
  0.0 183.2 jit_solution(5634185827879025002)
XLA Ops:
  0.0 5.2 %pack.3 = bf16[8,2,2,4,2,64,128]{6,5,4,3,2,1,0:T(8,128)(2,1)} custom-call(s32[2,16]{1,0:T(2,128)} %bitcast.28, s32[1]{0:T(128)} %bitcast.1.xh, bf16[2,1,16,64,1024]{4,3,2,1,0:T(8,128)(2,1)} %block.3), custom_call_target="tpu_custom_call" | custom-call | flops 16777216 | bytes 8388608 | tf_op jit(solution)/shard_map/pack/pallas_call | solution.py:61
  5.2 11.9 %all-to-all-start.1 = ((bf16[128,2,64,128]{3,2,1,0:T(8,128)(2,1)}), bf16[128,2,64,128]{3,2,1,0:T(8,128)(2,1)}, u32[]{:S(2)}, u32[]{:S(2)}) async-start(bf16[128,2,64,128]{3,2,1,0:T(8,128)(2,1)} %bitcast.26), calls=%async_computation.1 | async-start | bytes 8388608 | tf_op jit(solution)/shard_map/all_to_all | solution.py:354
  17.2 3.0 %collective-permute-start = (s32[128]{0:T(128)S(1)}, s32[128]{0:T(128)S(1)}, u32[]{:S(2)}, u32[]{:S(2)}) collective-permute-start(s32[128]{0:T(128)S(1)} %copy-done), channel_id=1, source_target_pairs={{0,4},{1,5},{2,6},{3,7},{4,0},{5,1},{6,2},{7,3},{8,12},{9,13},{10,... | collective-permute-start | bytes 1544 | tf_op jit(solution)/shard_map/ppermute | solution.py:336
  20.1 5.2 %pack.2 = bf16[8,2,2,4,2,64,128]{6,5,4,3,2,1,0:T(8,128)(2,1)} custom-call(s32[2,16]{1,0:T(2,128)} %bitcast.29, s32[1]{0:T(128)} %bitcast.1.xh, bf16[2,1,16,64,1024]{4,3,2,1,0:T(8,128)(2,1)} %block.3), custom_call_target="tpu_custom_call" | custom-call | flops 16777216 | bytes 8388608 | tf_op jit(solution)/shard_map/pack/pallas_call | solution.py:61
  25.5 39.2 %collective-permute-done = s32[128]{0:T(128)S(1)} collective-permute-done((s32[128]{0:T(128)S(1)}, s32[128]{0:T(128)S(1)}, u32[]{:S(2)}, u32[]{:S(2)}) %collective-permute-start) | collective-permute-done | bytes 544 | tf_op jit(solution)/shard_map/ppermute | solution.py:336
  64.8 3.2 %all-to-all-done.1 = bf16[128,2,64,128]{3,2,1,0:T(8,128)(2,1)} async-done(((bf16[128,2,64,128]{3,2,1,0:T(8,128)(2,1)}), bf16[128,2,64,128]{3,2,1,0:T(8,128)(2,1)}, u32[]{:S(2)}, u32[]{:S(2)}) %all-to-all-start.1) | async-done | bytes 4194336 | tf_op jit(solution)/shard_map/all_to_all | solution.py:354
  68.0 8.2 %all-to-all-start = ((bf16[128,2,64,128]{3,2,1,0:T(8,128)(2,1)}), bf16[128,2,64,128]{3,2,1,0:T(8,128)(2,1)}, u32[]{:S(2)}, u32[]{:S(2)}) async-start(bf16[128,2,64,128]{3,2,1,0:T(8,128)(2,1)} %bitcast.27), calls=%async_computation | async-start | bytes 8388608 | tf_op jit(solution)/shard_map/all_to_all | solution.py:374
  76.2 1.8 constant_dynamic-slice_fusion
  77.9 1.4 collective-permute-start.1
  79.4 3.8 %collective-permute-done.1.other = bf16[16,1,4,2,64,128]{5,4,3,2,1,0:T(8,128)(2,1)S(1)} collective-permute-done((bf16[16,1,4,2,64,128]{5,4,3,2,1,0:T(8,128)(2,1)S(1)}, bf16[16,1,4,2,64,128]{5,4,3,2,1,0:T(8,128)(2,1)S(1)}, u32[]{:S(2)}, u32[]{:S(2)}) %collective-permute-start.1) | collective-permute-done | bytes 2097184 | tf_op jit(solution)/shard_map/ppermute | solution.py:349
  83.1 19.2 %first_half.1 = (bf16[12,256,256]{2,1,0:T(8,128)(2,1)S(1)}, bf16[12,256,256]{2,1,0:T(8,128)(2,1)S(1)}) custom-call(s32[6]{0:T(128)S(1)} %stack.46.where, bf16[16,2,4,2,64,128]{5,4,3,2,1,0:T(8,128)(2,1)} %bitcast.13.left.own, bf16[16,2,4,2,64,128]{5,4,3,2,1,0:T(8,128)(2,1)} %bitcast.13.left.own, ...), custom_call_target="tpu_custom_call" | custom-call | flops 12999999488 | bytes 12582912 | tf_op jit(solution)/shard_map/first_half/pallas_call | solution.py:223
  102.4 24.6 %all-to-all-done = bf16[128,2,64,128]{3,2,1,0:T(8,128)(2,1)} async-done(((bf16[128,2,64,128]{3,2,1,0:T(8,128)(2,1)}), bf16[128,2,64,128]{3,2,1,0:T(8,128)(2,1)}, u32[]{:S(2)}, u32[]{:S(2)}) %all-to-all-start) | async-done | bytes 4194336 | tf_op jit(solution)/shard_map/all_to_all | solution.py:374
  127.0 12.2 %second_half.2 = (bf16[12,64,256]{2,1,0:T(8,128)(2,1)S(1)}, bf16[12,64,256]{2,1,0:T(8,128)(2,1)S(1)}, bf16[12,64,256]{2,1,0:T(8,128)(2,1)S(1)}, bf16[12,64,256]{2,1,0:T(8,128)(2,1)S(1)}, bf16[4,64,4096]{2,1,0:T(8,128)(2,1)S(1)}) custom-call(s32[6]{0:T(128)S(1)} %stack.46.where, bf16[16,2,4,2,64,128]{5,4,3,2,1,0:T(8,128)(2,1)} %bitcast.16.landed.right, ...), custom_call_target="tpu_custom_call" | custom-call | flops 6499999744 | bytes 8388608 | tf_op jit(solution)/shard_map/second_half/pallas_call | solution.py:256
  139.2 2.5 %collective-permute-start.2 = (bf16[4,64,4096]{2,1,0:T(8,128)(2,1)S(1)}, bf16[4,64,4096]{2,1,0:T(8,128)(2,1)S(1)}, u32[]{:S(2)}, u32[]{:S(2)}) collective-permute-start(bf16[4,64,4096]{2,1,0:T(8,128)(2,1)S(1)} %get-tuple-element.33), channel_id=1, source_target_pairs={{0,8},{1,9},{2,10},{3,11},{4,12},{5,13},{6,14},{7,15},{8,0},{9,1},... | collective-permute-start | bytes 6291464 | tf_op jit(solution)/shard_map/ppermute | solution.py:349
  141.9 2.5 %collective-permute-start.8 = (bf16[12,64,256]{2,1,0:T(8,128)(2,1)S(1)}, bf16[12,64,256]{2,1,0:T(8,128)(2,1)S(1)}, u32[]{:S(2)}, u32[]{:S(2)}) collective-permute-start(bf16[12,64,256]{2,1,0:T(8,128)(2,1)S(1)} %get-tuple-element.40), channel_id=1, source_target_pairs={{0,5},{1,6},{2,7},{3,4},{4,13},{5,14},{6,15},{7,12},{8,1},{9,2},{1... | collective-permute-start | bytes 1179656 | tf_op jit(solution)/shard_map/ppermute | solution.py:360
  144.4 2.1 %collective-permute-start.9 = (bf16[12,64,256]{2,1,0:T(8,128)(2,1)S(1)}, bf16[12,64,256]{2,1,0:T(8,128)(2,1)S(1)}, u32[]{:S(2)}, u32[]{:S(2)}) collective-permute-start(bf16[12,64,256]{2,1,0:T(8,128)(2,1)S(1)} %get-tuple-element.41), channel_id=1, source_target_pairs={{0,7},{1,4},{2,5},{3,6},{4,15},{5,12},{6,13},{7,14},{8,3},{9,0},{1... | collective-permute-start | bytes 1179656 | tf_op jit(solution)/shard_map/ppermute | solution.py:360
  147.7 11.6 %second_half.3 = (bf16[12,64,256]{2,1,0:T(8,128)(2,1)S(1)}, bf16[12,64,256]{2,1,0:T(8,128)(2,1)S(1)}, bf16[12,64,256]{2,1,0:T(8,128)(2,1)S(1)}, bf16[12,64,256]{2,1,0:T(8,128)(2,1)S(1)}) custom-call(s32[6]{0:T(128)S(1)} %stack.46.where, bf16[16,2,4,2,64,128]{5,4,3,2,1,0:T(8,128)(2,1)} %bitcast.16.landed.right, ...), custom_call_target="tpu_custom_call" | custom-call | flops 6499999744 | bytes 8388608 | tf_op jit(solution)/shard_map/second_half/pallas_call | solution.py:256
  159.3 1.8 collective-permute-start.3
  162.1 4.1 %collective-permute-start.5 = (bf16[12,64,256]{2,1,0:T(8,128)(2,1)S(1)}, bf16[12,64,256]{2,1,0:T(8,128)(2,1)S(1)}, u32[]{:S(2)}, u32[]{:S(2)}) collective-permute-start(bf16[12,64,256]{2,1,0:T(8,128)(2,1)S(1)} %get-tuple-element.37), channel_id=1, source_target_pairs={{0,7},{1,4},{2,5},{3,6},{4,15},{5,12},{6,13},{7,14},{8,3},{9,0},{1... | collective-permute-start | bytes 1179656 | tf_op jit(solution)/shard_map/ppermute | solution.py:360
  166.7 1.6 total.2.refs_4_
  168.3 6.0 %collective-permute-done.3.refs_0_ = bf16[12,64,256]{2,1,0:T(8,128)(2,1)S(1)} collective-permute-done((bf16[12,64,256]{2,1,0:T(8,128)(2,1)S(1)}, bf16[12,64,256]{2,1,0:T(8,128)(2,1)S(1)}, u32[]{:S(2)}, u32[]{:S(2)}) %collective-permute-start.3) | collective-permute-done | bytes 393248 | tf_op jit(solution)/shard_map/ppermute | solution.py:360
  174.3 4.2 %collective-permute-done.4.refs_1_ = bf16[12,64,256]{2,1,0:T(8,128)(2,1)S(1)} collective-permute-done((bf16[12,64,256]{2,1,0:T(8,128)(2,1)S(1)}, bf16[12,64,256]{2,1,0:T(8,128)(2,1)S(1)}, u32[]{:S(2)}, u32[]{:S(2)}) %collective-permute-start.4) | collective-permute-done | bytes 393248 | tf_op jit(solution)/shard_map/ppermute | solution.py:360
  178.6 2.9 %collective-permute-done.6.refs_3_ = bf16[12,64,256]{2,1,0:T(8,128)(2,1)S(1)} collective-permute-done((bf16[12,64,256]{2,1,0:T(8,128)(2,1)S(1)}, bf16[12,64,256]{2,1,0:T(8,128)(2,1)S(1)}, u32[]{:S(2)}, u32[]{:S(2)}) %collective-permute-start.6) | collective-permute-done | bytes 393248 | tf_op jit(solution)/shard_map/ppermute | solution.py:360
  181.6 1.6 total.3
  (18 shorter events, 3.2 us)
Async XLA Ops:
  5.2 11.9 %copy-start = (s32[128]{0:T(128)S(1)}, s32[128]{0:T(128)}, u32[]{:S(2)}) copy-start(s32[128]{0:T(128)} %param.5) | copy-start | bytes 1540
  5.2 62.8 %all-to-all-start.1 = ((bf16[128,2,64,128]{3,2,1,0:T(8,128)(2,1)}), bf16[128,2,64,128]{3,2,1,0:T(8,128)(2,1)}, u32[]{:S(2)}, u32[]{:S(2)}) async-start(bf16[128,2,64,128]{3,2,1,0:T(8,128)(2,1)} %bitcast.26), calls=%async_computation.1 | async-start | bytes 8388608 | tf_op jit(solution)/shard_map/all_to_all | solution.py:354
  17.2 47.6 %collective-permute-start = (s32[128]{0:T(128)S(1)}, s32[128]{0:T(128)S(1)}, u32[]{:S(2)}, u32[]{:S(2)}) collective-permute-start(s32[128]{0:T(128)S(1)} %copy-done), channel_id=1, source_target_pairs={{0,4},{1,5},{2,6},{3,7},{4,0},{5,1},{6,2},{7,3},{8,12},{9,13},{10,... | collective-permute-start | bytes 1544 | tf_op jit(solution)/shard_map/ppermute | solution.py:336
  68.0 59.0 %all-to-all-start = ((bf16[128,2,64,128]{3,2,1,0:T(8,128)(2,1)}), bf16[128,2,64,128]{3,2,1,0:T(8,128)(2,1)}, u32[]{:S(2)}, u32[]{:S(2)}) async-start(bf16[128,2,64,128]{3,2,1,0:T(8,128)(2,1)} %bitcast.27), calls=%async_computation | async-start | bytes 8388608 | tf_op jit(solution)/shard_map/all_to_all | solution.py:374
  77.9 5.2 %collective-permute-start.1 = (bf16[16,1,4,2,64,128]{5,4,3,2,1,0:T(8,128)(2,1)S(1)}, bf16[16,1,4,2,64,128]{5,4,3,2,1,0:T(8,128)(2,1)S(1)}, u32[]{:S(2)}, u32[]{:S(2)}) collective-permute-start(bf16[16,1,4,2,64,128]{5,4,3,2,1,0:T(8,128)(2,1)S(1)} %constant_dynamic-slice_fusion), channel_id=1, source_target_pairs={{0,8},{1,9},{2,10},{3,11},{4,12},{5,13},{6,14},{7,15},{8,0},{9,1},... | collective-permute-start | bytes 6291464 | tf_op jit(solution)/shard_map/ppermute | solution.py:349
  139.2 8.5 %collective-permute-start.2 = (bf16[4,64,4096]{2,1,0:T(8,128)(2,1)S(1)}, bf16[4,64,4096]{2,1,0:T(8,128)(2,1)S(1)}, u32[]{:S(2)}, u32[]{:S(2)}) collective-permute-start(bf16[4,64,4096]{2,1,0:T(8,128)(2,1)S(1)} %get-tuple-element.33), channel_id=1, source_target_pairs={{0,8},{1,9},{2,10},{3,11},{4,12},{5,13},{6,14},{7,15},{8,0},{9,1},... | collective-permute-start | bytes 6291464 | tf_op jit(solution)/shard_map/ppermute | solution.py:349
  141.7 19.3 %collective-permute-start.7 = (bf16[12,64,256]{2,1,0:T(8,128)(2,1)S(1)}, bf16[12,64,256]{2,1,0:T(8,128)(2,1)S(1)}, u32[]{:S(2)}, u32[]{:S(2)}) collective-permute-start(bf16[12,64,256]{2,1,0:T(8,128)(2,1)S(1)} %get-tuple-element.39), channel_id=1, source_target_pairs={{0,6},{1,7},{2,4},{3,5},{4,14},{5,15},{6,12},{7,13},{8,2},{9,3},{1... | collective-permute-start | bytes 1179656 | tf_op jit(solution)/shard_map/ppermute | solution.py:360
  141.9 20.2 %collective-permute-start.8 = (bf16[12,64,256]{2,1,0:T(8,128)(2,1)S(1)}, bf16[12,64,256]{2,1,0:T(8,128)(2,1)S(1)}, u32[]{:S(2)}, u32[]{:S(2)}) collective-permute-start(bf16[12,64,256]{2,1,0:T(8,128)(2,1)S(1)} %get-tuple-element.40), channel_id=1, source_target_pairs={{0,5},{1,6},{2,7},{3,4},{4,13},{5,14},{6,15},{7,12},{8,1},{9,2},{1... | collective-permute-start | bytes 1179656 | tf_op jit(solution)/shard_map/ppermute | solution.py:360
  144.4 21.7 %collective-permute-start.9 = (bf16[12,64,256]{2,1,0:T(8,128)(2,1)S(1)}, bf16[12,64,256]{2,1,0:T(8,128)(2,1)S(1)}, u32[]{:S(2)}, u32[]{:S(2)}) collective-permute-start(bf16[12,64,256]{2,1,0:T(8,128)(2,1)S(1)} %get-tuple-element.41), channel_id=1, source_target_pairs={{0,7},{1,4},{2,5},{3,6},{4,15},{5,12},{6,13},{7,14},{8,3},{9,0},{1... | collective-permute-start | bytes 1179656 | tf_op jit(solution)/shard_map/ppermute | solution.py:360
  146.6 20.1 %collective-permute-start.10 = (bf16[12,64,256]{2,1,0:T(8,128)(2,1)S(1)}, bf16[12,64,256]{2,1,0:T(8,128)(2,1)S(1)}, u32[]{:S(2)}, u32[]{:S(2)}) collective-permute-start(bf16[12,64,256]{2,1,0:T(8,128)(2,1)S(1)} %get-tuple-element.42), channel_id=1, source_target_pairs={{0,4},{1,5},{2,6},{3,7},{4,12},{5,13},{6,14},{7,15},{8,0},{9,1},{1... | collective-permute-start | bytes 1179656 | tf_op jit(solution)/shard_map/ppermute | solution.py:360
  159.3 15.0 %collective-permute-start.3 = (bf16[12,64,256]{2,1,0:T(8,128)(2,1)S(1)}, bf16[12,64,256]{2,1,0:T(8,128)(2,1)S(1)}, u32[]{:S(2)}, u32[]{:S(2)}) collective-permute-start(bf16[12,64,256]{2,1,0:T(8,128)(2,1)S(1)} %get-tuple-element.35), channel_id=1, source_target_pairs={{0,6},{1,7},{2,4},{3,5},{4,14},{5,15},{6,12},{7,13},{8,2},{9,3},{1... | collective-permute-start | bytes 1179656 | tf_op jit(solution)/shard_map/ppermute | solution.py:360
  161.1 17.4 %collective-permute-start.4 = (bf16[12,64,256]{2,1,0:T(8,128)(2,1)S(1)}, bf16[12,64,256]{2,1,0:T(8,128)(2,1)S(1)}, u32[]{:S(2)}, u32[]{:S(2)}) collective-permute-start(bf16[12,64,256]{2,1,0:T(8,128)(2,1)S(1)} %get-tuple-element.36), channel_id=1, source_target_pairs={{0,5},{1,6},{2,7},{3,4},{4,13},{5,14},{6,15},{7,12},{8,1},{9,2},{1... | collective-permute-start | bytes 1179656 | tf_op jit(solution)/shard_map/ppermute | solution.py:360
  162.1 16.5 %collective-permute-start.5 = (bf16[12,64,256]{2,1,0:T(8,128)(2,1)S(1)}, bf16[12,64,256]{2,1,0:T(8,128)(2,1)S(1)}, u32[]{:S(2)}, u32[]{:S(2)}) collective-permute-start(bf16[12,64,256]{2,1,0:T(8,128)(2,1)S(1)} %get-tuple-element.37), channel_id=1, source_target_pairs={{0,7},{1,4},{2,5},{3,6},{4,15},{5,12},{6,13},{7,14},{8,3},{9,0},{1... | collective-permute-start | bytes 1179656 | tf_op jit(solution)/shard_map/ppermute | solution.py:360
  166.1 15.4 %collective-permute-start.6 = (bf16[12,64,256]{2,1,0:T(8,128)(2,1)S(1)}, bf16[12,64,256]{2,1,0:T(8,128)(2,1)S(1)}, u32[]{:S(2)}, u32[]{:S(2)}) collective-permute-start(bf16[12,64,256]{2,1,0:T(8,128)(2,1)S(1)} %get-tuple-element.38), channel_id=1, source_target_pairs={{0,4},{1,5},{2,6},{3,7},{4,12},{5,13},{6,14},{7,15},{8,0},{9,1},{1... | collective-permute-start | bytes 1179656 | tf_op jit(solution)/shard_map/ppermute | solution.py:360

commit v6 on v5

--- a/solution.py
+++ b/solution.py
@@ -16,7 +16,7 @@
 NZ = 4
 CH = 64
 FB = 128
-HOPS = (2, 1, 3, 0)
+HOPS = (2, 0, 1, 3)
 BF = jnp.bfloat16
 F32 = jnp.float32
 
@@ -81,8 +81,8 @@
     return slice((2 * g + comp) * FB, (2 * g + comp + 1) * FB)
 
 
-def turn_and_multiply(group, where, left, cos_ref, sin_ref, even, odd, flat, add, arrive=None, ready=None):
-    rows_all = NZ * CH
+def turn_and_multiply(group, slots, get, cos_ref, sin_ref, even, odd, flat, add, arrive=None, ready=None):
+    rows_all = slots * CH
 
     def turn(m, turned, arrive=None):
         lag = HALF if isinstance(m, int) and m == 0 else m
@@ -92,10 +92,9 @@
         for g in range(group):
             if arrive is not None:
                 arrive(g)
-            for dz in range(NZ):
-                z = where[2 + dz]
-                re = left[g, 0, z, 0]
-                im = left[g, 0, z, 1]
+            for dz in range(slots):
+                re = get(g, dz, 0)
+                im = get(g, dz, 1)
                 rc, rs, ic, isn = re * cos, re * sin, im * cos, im * sin
                 rows = slice(dz * CH, dz * CH + CH)
                 more = slice(rows_all + dz * CH, rows_all + dz * CH + CH)
@@ -147,7 +146,11 @@
         for g in range(group):
             for comp in range(2):
                 flat[h * NZ : (h + 1) * NZ, :, col(g, comp)] = right[g, 0, :, comp]
-    turn_and_multiply(group, where, left, cos_ref, sin_ref, even, odd, flat, add)
+
+    def get(g, dz, comp):
+        return left[g, 0, where[2 + dz], comp]
+
+    turn_and_multiply(group, NZ, get, cos_ref, sin_ref, even, odd, flat, add)
 
     @pl.when(pl.program_id(0) == pl.num_programs(0) - 1)
     def _():
@@ -155,16 +158,22 @@
         other_out[...] = other_sum[...].astype(BF)
 
 
-def second_kernel(is_own, where, landed, right, cos_ref, sin_ref, before, o0, o1, o2, o3, *refs):
+def second_kernel(is_own, start, count, where, landed, right, cos_ref, sin_ref, before, *refs):
+    outs, refs = refs[:count], refs[count:]
     if is_own:
         mine, *refs = refs
     left, sums, even, odd, flat, left_sems, right_sems, other_sems = refs
     group = landed.shape[0]
     quarter = group // 4
     lefts = [
-        pltpu.make_async_copy(
-            landed.at[pl.ds(q * quarter, quarter), where[0]], left.at[pl.ds(q * quarter, quarter), 0], left_sems.at[q]
-        )
+        [
+            pltpu.make_async_copy(
+                landed.at[pl.ds(q * quarter, quarter), where[0], where[2 + start + k]],
+                left.at[k, pl.ds(q * quarter, quarter)],
+                left_sems.at[q, k],
+            )
+            for k in range(count)
+        ]
         for q in range(4)
     ]
     if is_own:
@@ -178,13 +187,17 @@
         keep = pltpu.make_async_copy(flat, mine, other_sems.at[1])
     else:
         rights = [pltpu.make_async_copy(right.at[z], flat.at[z], right_sems.at[z, 0]) for z in range(NZ)]
-    past = pltpu.make_async_copy(before, sums, other_sems.at[0])
-    for copy in lefts + rights + [past]:
+    past = pltpu.make_async_copy(before.at[:, pl.ds(start * CH, count * CH)], sums, other_sems.at[0])
+    for copy in sum(lefts, []) + rights + [past]:
         copy.start()
+
+    def get(g, dz, comp):
+        return left[dz, g, comp]
 
     def arrive(g):
         if g % quarter == 0:
-            lefts[g // quarter].wait()
+            for copy in lefts[g // quarter]:
+                copy.wait()
 
     def ready():
         for copy in rights + [past]:
@@ -193,11 +206,11 @@
             keep.start()
 
     def add(at, product):
-        for dz, out in enumerate((o0, o1, o2, o3)):
-            rows = slice(dz * CH, dz * CH + CH)
+        for k, out in enumerate(outs):
+            rows = slice(k * CH, k * CH + CH)
             out[at] = ((sums[at, rows].astype(F32) + product[rows]) * (1.0 / 128.0)).astype(BF)
 
-    turn_and_multiply(group, where, left, cos_ref, sin_ref, even, odd, flat, add, arrive, ready)
+    turn_and_multiply(group, count, get, cos_ref, sin_ref, even, odd, flat, add, arrive, ready)
     if is_own:
         keep.wait()
 
@@ -242,38 +255,38 @@
     )(where, landed, landed, theirs, cosine, sine)
 
 
-def second_half(where, landed, right, cosine, sine, before):
+def second_half(where, landed, right, cosine, sine, before, start, count):
     is_own = right is None
     group = landed.shape[0]
     width = 2 * group * FB
     piece = jax.ShapeDtypeStruct((LAGS, CH, NZ * CH), BF)
-    out_specs, out_shape = [whole(piece.shape)] * NZ, [piece] * NZ
+    out_specs, out_shape = [whole(piece.shape)] * count, [piece] * count
     anywhere = pl.BlockSpec(memory_space=pl.ANY)
     if is_own:
         right = landed
         out_specs = out_specs + [anywhere]
         out_shape = out_shape + [jax.ShapeDtypeStruct((NZ, CH, width), BF)]
     return pl.pallas_call(
-        functools.partial(second_kernel, is_own),
+        functools.partial(second_kernel, is_own, start, count),
         grid_spec=pltpu.PrefetchScalarGridSpec(
             num_scalar_prefetch=1,
             grid=(1,),
             in_specs=[anywhere, anywhere, table_spec(), table_spec(), anywhere],
             out_specs=out_specs,
             scratch_shapes=[
-                pltpu.VMEM((group, 1, NZ, 2, CH, FB), BF),
-                pltpu.VMEM(SUMS, BF),
-                pltpu.VMEM((2 * NZ * CH, width), BF),
-                pltpu.VMEM((2 * NZ * CH, width), BF),
+                pltpu.VMEM((count, group, 2, CH, FB), BF),
+                pltpu.VMEM((LAGS, count * CH, NZ * CH), BF),
+                pltpu.VMEM((2 * count * CH, width), BF),
+                pltpu.VMEM((2 * count * CH, width), BF),
                 pltpu.VMEM((NZ, CH, width), BF),
-                pltpu.SemaphoreType.DMA((4,)),
+                pltpu.SemaphoreType.DMA((4, count)),
                 pltpu.SemaphoreType.DMA((group, 2)),
                 pltpu.SemaphoreType.DMA((2,)),
             ],
         ),
         out_shape=out_shape,
         compiler_params=pltpu.CompilerParams(vmem_limit_bytes=40 * 2**20),
-        cost_estimate=pl.CostEstimate(flops=65 * 10**8, bytes_accessed=8 * 2**20, transcendentals=0),
+        cost_estimate=pl.CostEstimate(flops=10**8, bytes_accessed=2**20, transcendentals=0),
         name="second_half",
     )(where, landed, right, cosine, sine, before)
 
@@ -355,14 +368,14 @@
         landed = landed.reshape(16, 2, NZ, 2, CH, FB)
         return landed, swap(lax.dynamic_slice_in_dim(landed, core, 1, axis=1))
 
-    def send(parts):
+    def send(parts, start):
         return [
             lax.ppermute(
                 part,
                 both,
                 [(index(*p), index(p[0], p[1], p[3], 1 - p[2], (p[4] + hop) % NZ)) for p in places()],
             )
-            for hop, part in zip(HOPS, parts)
+            for hop, part in zip(HOPS[start:], parts)
         ]
 
     pairs, side = block_pairs.T, xh.reshape(1)
@@ -374,10 +387,16 @@
     landed1 = lax.all_to_all(packed1.reshape(128, 2, CH, FB), both, split_axis=0, concat_axis=0, tiled=True)
     landed1, own, other = lax.optimization_barrier((landed1, own, other))
     landed1 = landed1.reshape(16, 2, NZ, 2, CH, FB)
-    *first, mine1 = second_half(where, landed1, None, cosine[1], sine[1], own)
+    def chunk(right, before, start, count):
+        return second_half(where, landed1, right, cosine[1], sine[1], before, start, count)
+
+    *pieces, mine1 = chunk(None, own, 0, NZ)
     theirs1 = swap(mine1)
-    first = send(first)
-    second = send(second_half(where, landed1, theirs1, cosine[1], sine[1], other))
+    early = chunk(theirs1, other, 0, 2)
+    theirs1, _ = lax.optimization_barrier((theirs1, early[0]))
+    late = chunk(theirs1, other, 2, 2)
+    first = send(pieces, 0)
+    second = send(early, 0) + send(late, 2)
     filled = total(halves, 1, second, total(halves, 0, first))
     return jnp.transpose(filled, (0, 2, 1, 3))
 

time: 184 us -> 183 us (level)
  waiting for transfers between devices: 84.1 us -> 80.2 us
  Pallas kernels: 56.6 us -> 59.3 us
    ppermute x8, waiting for transfers between devices: 13.3 us -> 9.56 us  [send(): lax.ppermute(part, both, [(index(*p), index(p[0], p[1], p[3], 1 - p[2], (...]
    pallas_call x2 -> x3, Pallas kernels: 23.8 us -> 26.2 us  [second_half(): pl.pallas_call(functools.partial(second_kernel, is_own, start, count), gr...]
  transfers between devices with their start and end apart: 13 -> 13, of which waited for: 8 -> 7; matrix products, arithmetic and copies ran while one was open for 1% -> 1% of each run, Pallas kernels for 21% -> 22%
where the time goes in v6:
time: 183 us; the launch traced here: 182 us
  waiting for transfers between devices  80.2 us (44%)
  Pallas kernels  59.3 us (32%)
  starting transfers between devices  40.5 us (22%)
  local copies, waits for them, and re-layouts  1.86 us (1%)
    ppermute x1, waiting for transfers between devices, body(): lax.ppermute(band_bins, both, [(index(*p), index(p[0], p[1], p[2], 1 - p[...  39.1 us
    pallas_call x3, Pallas kernels, second_half(): pl.pallas_call(functools.partial(second_kernel, is_own, start, count), gr...  26.2 us
    all_to_all x1, waiting for transfers between devices, body(): lax.all_to_all(packed1.reshape(128, 2, CH, FB), both, split_axis=0, conca...  24.6 us
    pallas_call x1, Pallas kernels, first_half(): pl.pallas_call(functools.partial(first_kernel, group), grid_spec=pltpu.Pr...  19.2 us
    ppermute x8, starting transfers between devices, send(): lax.ppermute(part, both, [(index(*p), index(p[0], p[1], p[3], 1 - p[2], (...  13.4 us
    all_to_all x1, starting transfers between devices, exchange(): lax.all_to_all(packed.reshape(128, 2, CH, FB), both, split_axis=0, concat...  12 us
    pallas_call x2, Pallas kernels, pack(): pl.pallas_call(functools.partial(pack_kernel, group, part), grid_spec=plt...  10.7 us
    ppermute x8, waiting for transfers between devices, send(): lax.ppermute(part, both, [(index(*p), index(p[0], p[1], p[3], 1 - p[2], (...  9.56 us
  transfers between devices with their start and end apart: 13, of which 7 were waited for; matrix products, arithmetic and copies ran while one was open for 1% of the time, Pallas kernels for 22%

profile of v6, /device:TPU:1, one launch (start us, length us, event | category | flops | bytes accessed | tf_op | source)
XLA Modules:
  0.0 182.2 jit_solution(7107301799610516366)
XLA Ops:
  0.0 5.4 %pack.3 = bf16[8,2,2,4,2,64,128]{6,5,4,3,2,1,0:T(8,128)(2,1)} custom-call(s32[2,16]{1,0:T(2,128)} %bitcast.28, s32[1]{0:T(128)} %bitcast.1.xh, bf16[2,1,16,64,1024]{4,3,2,1,0:T(8,128)(2,1)} %block.3), custom_call_target="tpu_custom_call" | custom-call | flops 16777216 | bytes 8388608 | tf_op jit(solution)/shard_map/pack/pallas_call | solution.py:61
  5.4 12.0 %all-to-all-start.1 = ((bf16[128,2,64,128]{3,2,1,0:T(8,128)(2,1)}), bf16[128,2,64,128]{3,2,1,0:T(8,128)(2,1)}, u32[]{:S(2)}, u32[]{:S(2)}) async-start(bf16[128,2,64,128]{3,2,1,0:T(8,128)(2,1)} %bitcast.26), calls=%async_computation.1 | async-start | bytes 8388608 | tf_op jit(solution)/shard_map/all_to_all | solution.py:367
  17.4 3.0 %collective-permute-start = (s32[128]{0:T(128)S(1)}, s32[128]{0:T(128)S(1)}, u32[]{:S(2)}, u32[]{:S(2)}) collective-permute-start(s32[128]{0:T(128)S(1)} %copy-done), channel_id=1, source_target_pairs={{0,4},{1,5},{2,6},{3,7},{4,0},{5,1},{6,2},{7,3},{8,12},{9,13},{10,... | collective-permute-start | bytes 1544 | tf_op jit(solution)/shard_map/ppermute | solution.py:349
  20.4 5.3 %pack.2 = bf16[8,2,2,4,2,64,128]{6,5,4,3,2,1,0:T(8,128)(2,1)} custom-call(s32[2,16]{1,0:T(2,128)} %bitcast.29, s32[1]{0:T(128)} %bitcast.1.xh, bf16[2,1,16,64,1024]{4,3,2,1,0:T(8,128)(2,1)} %block.3), custom_call_target="tpu_custom_call" | custom-call | flops 16777216 | bytes 8388608 | tf_op jit(solution)/shard_map/pack/pallas_call | solution.py:61
  25.9 39.1 %collective-permute-done = s32[128]{0:T(128)S(1)} collective-permute-done((s32[128]{0:T(128)S(1)}, s32[128]{0:T(128)S(1)}, u32[]{:S(2)}, u32[]{:S(2)}) %collective-permute-start) | collective-permute-done | bytes 544 | tf_op jit(solution)/shard_map/ppermute | solution.py:349
  65.0 3.2 %all-to-all-done.1 = bf16[128,2,64,128]{3,2,1,0:T(8,128)(2,1)} async-done(((bf16[128,2,64,128]{3,2,1,0:T(8,128)(2,1)}), bf16[128,2,64,128]{3,2,1,0:T(8,128)(2,1)}, u32[]{:S(2)}, u32[]{:S(2)}) %all-to-all-start.1) | async-done | bytes 4194336 | tf_op jit(solution)/shard_map/all_to_all | solution.py:367
  68.2 8.2 %all-to-all-start = ((bf16[128,2,64,128]{3,2,1,0:T(8,128)(2,1)}), bf16[128,2,64,128]{3,2,1,0:T(8,128)(2,1)}, u32[]{:S(2)}, u32[]{:S(2)}) async-start(bf16[128,2,64,128]{3,2,1,0:T(8,128)(2,1)} %bitcast.27), calls=%async_computation | async-start | bytes 8388608 | tf_op jit(solution)/shard_map/all_to_all | solution.py:387
  76.4 1.8 constant_dynamic-slice_fusion
  79.6 3.8 %collective-permute-done.1.other = bf16[16,1,4,2,64,128]{5,4,3,2,1,0:T(8,128)(2,1)S(1)} collective-permute-done((bf16[16,1,4,2,64,128]{5,4,3,2,1,0:T(8,128)(2,1)S(1)}, bf16[16,1,4,2,64,128]{5,4,3,2,1,0:T(8,128)(2,1)S(1)}, u32[]{:S(2)}, u32[]{:S(2)}) %collective-permute-start.1) | collective-permute-done | bytes 2097184 | tf_op jit(solution)/shard_map/ppermute | solution.py:362
  83.4 19.2 %first_half.1 = (bf16[12,256,256]{2,1,0:T(8,128)(2,1)S(1)}, bf16[12,256,256]{2,1,0:T(8,128)(2,1)S(1)}) custom-call(s32[6]{0:T(128)S(1)} %stack.46.where, bf16[16,2,4,2,64,128]{5,4,3,2,1,0:T(8,128)(2,1)} %bitcast.13.left.own, bf16[16,2,4,2,64,128]{5,4,3,2,1,0:T(8,128)(2,1)} %bitcast.13.left.own, ...), custom_call_target="tpu_custom_call" | custom-call | flops 12999999488 | bytes 12582912 | tf_op jit(solution)/shard_map/first_half/pallas_call | solution.py:236
  102.6 24.6 %all-to-all-done = bf16[128,2,64,128]{3,2,1,0:T(8,128)(2,1)} async-done(((bf16[128,2,64,128]{3,2,1,0:T(8,128)(2,1)}), bf16[128,2,64,128]{3,2,1,0:T(8,128)(2,1)}, u32[]{:S(2)}, u32[]{:S(2)}) %all-to-all-start) | async-done | bytes 4194336 | tf_op jit(solution)/shard_map/all_to_all | solution.py:387
  127.2 12.4 %second_half.3 = (bf16[12,64,256]{2,1,0:T(8,128)(2,1)S(1)}, bf16[12,64,256]{2,1,0:T(8,128)(2,1)S(1)}, bf16[12,64,256]{2,1,0:T(8,128)(2,1)S(1)}, bf16[12,64,256]{2,1,0:T(8,128)(2,1)S(1)}, bf16[4,64,4096]{2,1,0:T(8,128)(2,1)S(1)}) custom-call(s32[6]{0:T(128)S(1)} %stack.46.where, bf16[16,2,4,2,64,128]{5,4,3,2,1,0:T(8,128)(2,1)} %bitcast.16.landed.right, ...), custom_call_target="tpu_custom_call" | custom-call | flops 100000000 | bytes 1048576 | tf_op jit(solution)/shard_map/second_half/pallas_call | solution.py:269
  139.6 2.5 %collective-permute-start.2 = (bf16[4,64,4096]{2,1,0:T(8,128)(2,1)S(1)}, bf16[4,64,4096]{2,1,0:T(8,128)(2,1)S(1)}, u32[]{:S(2)}, u32[]{:S(2)}) collective-permute-start(bf16[4,64,4096]{2,1,0:T(8,128)(2,1)S(1)} %get-tuple-element.34), channel_id=1, source_target_pairs={{0,8},{1,9},{2,10},{3,11},{4,12},{5,13},{6,14},{7,15},{8,0},{9,1},... | collective-permute-start | bytes 6291464 | tf_op jit(solution)/shard_map/ppermute | solution.py:362
  143.7 1.7 collective-permute-start.9
  145.4 2.7 %collective-permute-start.10 = (bf16[12,64,256]{2,1,0:T(8,128)(2,1)S(1)}, bf16[12,64,256]{2,1,0:T(8,128)(2,1)S(1)}, u32[]{:S(2)}, u32[]{:S(2)}) collective-permute-start(bf16[12,64,256]{2,1,0:T(8,128)(2,1)S(1)} %get-tuple-element.44), channel_id=1, source_target_pairs={{0,7},{1,4},{2,5},{3,6},{4,15},{5,12},{6,13},{7,14},{8,3},{9,0},{1... | collective-permute-start | bytes 1179656 | tf_op jit(solution)/shard_map/ppermute | solution.py:373
  148.1 6.9 %second_half.4 = (bf16[12,64,256]{2,1,0:T(8,128)(2,1)S(1)}, bf16[12,64,256]{2,1,0:T(8,128)(2,1)S(1)}) custom-call(s32[6]{0:T(128)S(1)} %stack.46.where, bf16[16,2,4,2,64,128]{5,4,3,2,1,0:T(8,128)(2,1)} %bitcast.16.landed.right, bf16[4,64,4096]{2,1,0:T(8,128)(2,1)S(1)} %collective-permute-done.2.right, f32[8,128]{1,0:T(8,128)S(1)} %get-tuple-element.54.cos_ref, ...), custom_call_target="tpu_custom_call" | custom-call | flops 100000000 | bytes 1048576 | tf_op jit(solution)/shard_map/second_half/pallas_call | solution.py:269
  155.0 1.8 collective-permute-start.3
  156.8 6.9 %second_half.5 = (bf16[12,64,256]{2,1,0:T(8,128)(2,1)S(1)}, bf16[12,64,256]{2,1,0:T(8,128)(2,1)S(1)}) custom-call(s32[6]{0:T(128)S(1)} %stack.46.where, bf16[16,2,4,2,64,128]{5,4,3,2,1,0:T(8,128)(2,1)} %bitcast.16.landed.right, bf16[4,64,4096]{2,1,0:T(8,128)(2,1)S(1)} %collective-permute-done.2.right, f32[8,128]{1,0:T(8,128)S(1)} %get-tuple-element.54.cos_ref, ...), custom_call_target="tpu_custom_call" | custom-call | flops 100000000 | bytes 1048576 | tf_op jit(solution)/shard_map/second_half/pallas_call | solution.py:269
  163.8 2.1 %collective-permute-start.4 = (bf16[12,64,256]{2,1,0:T(8,128)(2,1)S(1)}, bf16[12,64,256]{2,1,0:T(8,128)(2,1)S(1)}, u32[]{:S(2)}, u32[]{:S(2)}) collective-permute-start(bf16[12,64,256]{2,1,0:T(8,128)(2,1)S(1)} %get-tuple-element.37), channel_id=1, source_target_pairs={{0,4},{1,5},{2,6},{3,7},{4,12},{5,13},{6,14},{7,15},{8,0},{9,1},{1... | collective-permute-start | bytes 1179656 | tf_op jit(solution)/shard_map/ppermute | solution.py:373
  165.9 3.6 %collective-permute-start.6 = (bf16[12,64,256]{2,1,0:T(8,128)(2,1)S(1)}, bf16[12,64,256]{2,1,0:T(8,128)(2,1)S(1)}, u32[]{:S(2)}, u32[]{:S(2)}) collective-permute-start(bf16[12,64,256]{2,1,0:T(8,128)(2,1)S(1)} %get-tuple-element.40), channel_id=1, source_target_pairs={{0,7},{1,4},{2,5},{3,6},{4,15},{5,12},{6,13},{7,14},{8,3},{9,0},{1... | collective-permute-start | bytes 1179656 | tf_op jit(solution)/shard_map/ppermute | solution.py:373
  169.5 1.6 total.2.refs_4_
  172.0 6.1 %collective-permute-done.5.refs_2_ = bf16[12,64,256]{2,1,0:T(8,128)(2,1)S(1)} collective-permute-done((bf16[12,64,256]{2,1,0:T(8,128)(2,1)S(1)}, bf16[12,64,256]{2,1,0:T(8,128)(2,1)S(1)}, u32[]{:S(2)}, u32[]{:S(2)}) %collective-permute-start.5) | collective-permute-done | bytes 393248 | tf_op jit(solution)/shard_map/ppermute | solution.py:373
  178.1 2.6 %collective-permute-done.6.refs_3_ = bf16[12,64,256]{2,1,0:T(8,128)(2,1)S(1)} collective-permute-done((bf16[12,64,256]{2,1,0:T(8,128)(2,1)S(1)}, bf16[12,64,256]{2,1,0:T(8,128)(2,1)S(1)}, u32[]{:S(2)}, u32[]{:S(2)}) %collective-permute-start.6) | collective-permute-done | bytes 393248 | tf_op jit(solution)/shard_map/ppermute | solution.py:373
  180.6 1.6 total.3
  (19 shorter events, 4.2 us)
Async XLA Ops:
  5.4 12.0 %copy-start = (s32[128]{0:T(128)S(1)}, s32[128]{0:T(128)}, u32[]{:S(2)}) copy-start(s32[128]{0:T(128)} %param.5) | copy-start | bytes 1540
  5.4 62.8 %all-to-all-start.1 = ((bf16[128,2,64,128]{3,2,1,0:T(8,128)(2,1)}), bf16[128,2,64,128]{3,2,1,0:T(8,128)(2,1)}, u32[]{:S(2)}, u32[]{:S(2)}) async-start(bf16[128,2,64,128]{3,2,1,0:T(8,128)(2,1)} %bitcast.26), calls=%async_computation.1 | async-start | bytes 8388608 | tf_op jit(solution)/shard_map/all_to_all | solution.py:367
  17.4 47.6 %collective-permute-start = (s32[128]{0:T(128)S(1)}, s32[128]{0:T(128)S(1)}, u32[]{:S(2)}, u32[]{:S(2)}) collective-permute-start(s32[128]{0:T(128)S(1)} %copy-done), channel_id=1, source_target_pairs={{0,4},{1,5},{2,6},{3,7},{4,0},{5,1},{6,2},{7,3},{8,12},{9,13},{10,... | collective-permute-start | bytes 1544 | tf_op jit(solution)/shard_map/ppermute | solution.py:349
  68.2 59.0 %all-to-all-start = ((bf16[128,2,64,128]{3,2,1,0:T(8,128)(2,1)}), bf16[128,2,64,128]{3,2,1,0:T(8,128)(2,1)}, u32[]{:S(2)}, u32[]{:S(2)}) async-start(bf16[128,2,64,128]{3,2,1,0:T(8,128)(2,1)} %bitcast.27), calls=%async_computation | async-start | bytes 8388608 | tf_op jit(solution)/shard_map/all_to_all | solution.py:387
  78.2 5.2 %collective-permute-start.1 = (bf16[16,1,4,2,64,128]{5,4,3,2,1,0:T(8,128)(2,1)S(1)}, bf16[16,1,4,2,64,128]{5,4,3,2,1,0:T(8,128)(2,1)S(1)}, u32[]{:S(2)}, u32[]{:S(2)}) collective-permute-start(bf16[16,1,4,2,64,128]{5,4,3,2,1,0:T(8,128)(2,1)S(1)} %constant_dynamic-slice_fusion), channel_id=1, source_target_pairs={{0,8},{1,9},{2,10},{3,11},{4,12},{5,13},{6,14},{7,15},{8,0},{9,1},... | collective-permute-start | bytes 6291464 | tf_op jit(solution)/shard_map/ppermute | solution.py:362
  139.6 8.5 %collective-permute-start.2 = (bf16[4,64,4096]{2,1,0:T(8,128)(2,1)S(1)}, bf16[4,64,4096]{2,1,0:T(8,128)(2,1)S(1)}, u32[]{:S(2)}, u32[]{:S(2)}) collective-permute-start(bf16[4,64,4096]{2,1,0:T(8,128)(2,1)S(1)} %get-tuple-element.34), channel_id=1, source_target_pairs={{0,8},{1,9},{2,10},{3,11},{4,12},{5,13},{6,14},{7,15},{8,0},{9,1},... | collective-permute-start | bytes 6291464 | tf_op jit(solution)/shard_map/ppermute | solution.py:362
  142.1 21.6 %collective-permute-start.7 = (bf16[12,64,256]{2,1,0:T(8,128)(2,1)S(1)}, bf16[12,64,256]{2,1,0:T(8,128)(2,1)S(1)}, u32[]{:S(2)}, u32[]{:S(2)}) collective-permute-start(bf16[12,64,256]{2,1,0:T(8,128)(2,1)S(1)} %get-tuple-element.41), channel_id=1, source_target_pairs={{0,6},{1,7},{2,4},{3,5},{4,14},{5,15},{6,12},{7,13},{8,2},{9,3},{1... | collective-permute-start | bytes 1179656 | tf_op jit(solution)/shard_map/ppermute | solution.py:373
  142.3 23.6 %collective-permute-start.8 = (bf16[12,64,256]{2,1,0:T(8,128)(2,1)S(1)}, bf16[12,64,256]{2,1,0:T(8,128)(2,1)S(1)}, u32[]{:S(2)}, u32[]{:S(2)}) collective-permute-start(bf16[12,64,256]{2,1,0:T(8,128)(2,1)S(1)} %get-tuple-element.42), channel_id=1, source_target_pairs={{0,4},{1,5},{2,6},{3,7},{4,12},{5,13},{6,14},{7,15},{8,0},{9,1},{1... | collective-permute-start | bytes 1179656 | tf_op jit(solution)/shard_map/ppermute | solution.py:373
  143.7 22.1 %collective-permute-start.9 = (bf16[12,64,256]{2,1,0:T(8,128)(2,1)S(1)}, bf16[12,64,256]{2,1,0:T(8,128)(2,1)S(1)}, u32[]{:S(2)}, u32[]{:S(2)}) collective-permute-start(bf16[12,64,256]{2,1,0:T(8,128)(2,1)S(1)} %get-tuple-element.43), channel_id=1, source_target_pairs={{0,5},{1,6},{2,7},{3,4},{4,13},{5,14},{6,15},{7,12},{8,1},{9,2},{1... | collective-permute-start | bytes 1179656 | tf_op jit(solution)/shard_map/ppermute | solution.py:373
  145.4 24.1 %collective-permute-start.10 = (bf16[12,64,256]{2,1,0:T(8,128)(2,1)S(1)}, bf16[12,64,256]{2,1,0:T(8,128)(2,1)S(1)}, u32[]{:S(2)}, u32[]{:S(2)}) collective-permute-start(bf16[12,64,256]{2,1,0:T(8,128)(2,1)S(1)} %get-tuple-element.44), channel_id=1, source_target_pairs={{0,7},{1,4},{2,5},{3,6},{4,15},{5,12},{6,13},{7,14},{8,3},{9,0},{1... | collective-permute-start | bytes 1179656 | tf_op jit(solution)/shard_map/ppermute | solution.py:373
  155.0 16.1 %collective-permute-start.3 = (bf16[12,64,256]{2,1,0:T(8,128)(2,1)S(1)}, bf16[12,64,256]{2,1,0:T(8,128)(2,1)S(1)}, u32[]{:S(2)}, u32[]{:S(2)}) collective-permute-start(bf16[12,64,256]{2,1,0:T(8,128)(2,1)S(1)} %get-tuple-element.36), channel_id=1, source_target_pairs={{0,6},{1,7},{2,4},{3,5},{4,14},{5,15},{6,12},{7,13},{8,2},{9,3},{1... | collective-permute-start | bytes 1179656 | tf_op jit(solution)/shard_map/ppermute | solution.py:373
  163.8 8.2 %collective-permute-start.4 = (bf16[12,64,256]{2,1,0:T(8,128)(2,1)S(1)}, bf16[12,64,256]{2,1,0:T(8,128)(2,1)S(1)}, u32[]{:S(2)}, u32[]{:S(2)}) collective-permute-start(bf16[12,64,256]{2,1,0:T(8,128)(2,1)S(1)} %get-tuple-element.37), channel_id=1, source_target_pairs={{0,4},{1,5},{2,6},{3,7},{4,12},{5,13},{6,14},{7,15},{8,0},{9,1},{1... | collective-permute-start | bytes 1179656 | tf_op jit(solution)/shard_map/ppermute | solution.py:373
  165.9 12.2 %collective-permute-start.5 = (bf16[12,64,256]{2,1,0:T(8,128)(2,1)S(1)}, bf16[12,64,256]{2,1,0:T(8,128)(2,1)S(1)}, u32[]{:S(2)}, u32[]{:S(2)}) collective-permute-start(bf16[12,64,256]{2,1,0:T(8,128)(2,1)S(1)} %get-tuple-element.39), channel_id=1, source_target_pairs={{0,5},{1,6},{2,7},{3,4},{4,13},{5,14},{6,15},{7,12},{8,1},{9,2},{1... | collective-permute-start | bytes 1179656 | tf_op jit(solution)/shard_map/ppermute | solution.py:373
  165.9 14.7 %collective-permute-start.6 = (bf16[12,64,256]{2,1,0:T(8,128)(2,1)S(1)}, bf16[12,64,256]{2,1,0:T(8,128)(2,1)S(1)}, u32[]{:S(2)}, u32[]{:S(2)}) collective-permute-start(bf16[12,64,256]{2,1,0:T(8,128)(2,1)S(1)} %get-tuple-element.40), channel_id=1, source_target_pairs={{0,7},{1,4},{2,5},{3,6},{4,15},{5,12},{6,13},{7,14},{8,3},{9,0},{1... | collective-permute-start | bytes 1179656 | tf_op jit(solution)/shard_map/ppermute | solution.py:373

commit v7 on v6

--- a/solution.py
+++ b/solution.py
@@ -16,7 +16,7 @@
 NZ = 4
 CH = 64
 FB = 128
-HOPS = (2, 0, 1, 3)
+HOPS = (2, 1, 3, 0)
 BF = jnp.bfloat16
 F32 = jnp.float32
 
@@ -392,11 +392,11 @@
 
     *pieces, mine1 = chunk(None, own, 0, NZ)
     theirs1 = swap(mine1)
-    early = chunk(theirs1, other, 0, 2)
+    early = chunk(theirs1, other, 0, 3)
     theirs1, _ = lax.optimization_barrier((theirs1, early[0]))
-    late = chunk(theirs1, other, 2, 2)
+    late = chunk(theirs1, other, 3, 1)
     first = send(pieces, 0)
-    second = send(early, 0) + send(late, 2)
+    second = send(early, 0) + send(late, 3)
     filled = total(halves, 1, second, total(halves, 0, first))
     return jnp.transpose(filled, (0, 2, 1, 3))
 

time: 183 us -> 185 us (1.011)
    pallas_call x3, Pallas kernels: 26.2 us -> 28.5 us  [second_half(): pl.pallas_call(functools.partial(second_kernel, is_own, start, count), gr...]
  transfers between devices with their start and end apart: 13 -> 13, of which waited for: 7 -> 7; matrix products, arithmetic and copies ran while one was open for 1% -> 1% of each run, Pallas kernels for 22% -> 23%
where the time goes in v7:
time: 185 us; the launch traced here: 184 us
  waiting for transfers between devices  80.5 us (44%)
  Pallas kernels  61.1 us (33%)
  starting transfers between devices  40.5 us (22%)
  local copies, waits for them, and re-layouts  1.86 us (1%)
    ppermute x1, waiting for transfers between devices, body(): lax.ppermute(band_bins, both, [(index(*p), index(p[0], p[1], p[2], 1 - p[...  39.3 us
    pallas_call x3, Pallas kernels, second_half(): pl.pallas_call(functools.partial(second_kernel, is_own, start, count), gr...  28.5 us
    all_to_all x1, waiting for transfers between devices, body(): lax.all_to_all(packed1.reshape(128, 2, CH, FB), both, split_axis=0, conca...  24.6 us
    pallas_call x1, Pallas kernels, first_half(): pl.pallas_call(functools.partial(first_kernel, group), grid_spec=pltpu.Pr...  19.2 us
    ppermute x8, starting transfers between devices, send(): lax.ppermute(part, both, [(index(*p), index(p[0], p[1], p[3], 1 - p[2], (...  13.4 us
    all_to_all x1, starting transfers between devices, exchange(): lax.all_to_all(packed.reshape(128, 2, CH, FB), both, split_axis=0, concat...  12 us
    pallas_call x2, Pallas kernels, pack(): pl.pallas_call(functools.partial(pack_kernel, group, part), grid_spec=plt...  10.2 us
    ppermute x8, waiting for transfers between devices, send(): lax.ppermute(part, both, [(index(*p), index(p[0], p[1], p[3], 1 - p[2], (...  9.62 us
  transfers between devices with their start and end apart: 13, of which 7 were waited for; matrix products, arithmetic and copies ran while one was open for 1% of the time, Pallas kernels for 23%

profile of v7, /device:TPU:1, one launch (start us, length us, event | category | flops | bytes accessed | tf_op | source)
XLA Modules:
  0.0 184.3 jit_solution(16940059714118592779)
XLA Ops:
  0.0 5.1 %pack.3 = bf16[8,2,2,4,2,64,128]{6,5,4,3,2,1,0:T(8,128)(2,1)} custom-call(s32[2,16]{1,0:T(2,128)} %bitcast.28, s32[1]{0:T(128)} %bitcast.1.xh, bf16[2,1,16,64,1024]{4,3,2,1,0:T(8,128)(2,1)} %block.3), custom_call_target="tpu_custom_call" | custom-call | flops 16777216 | bytes 8388608 | tf_op jit(solution)/shard_map/pack/pallas_call | solution.py:61
  5.1 12.0 %all-to-all-start.1 = ((bf16[128,2,64,128]{3,2,1,0:T(8,128)(2,1)}), bf16[128,2,64,128]{3,2,1,0:T(8,128)(2,1)}, u32[]{:S(2)}, u32[]{:S(2)}) async-start(bf16[128,2,64,128]{3,2,1,0:T(8,128)(2,1)} %bitcast.26), calls=%async_computation.1 | async-start | bytes 8388608 | tf_op jit(solution)/shard_map/all_to_all | solution.py:367
  17.1 3.0 %collective-permute-start = (s32[128]{0:T(128)S(1)}, s32[128]{0:T(128)S(1)}, u32[]{:S(2)}, u32[]{:S(2)}) collective-permute-start(s32[128]{0:T(128)S(1)} %copy-done), channel_id=1, source_target_pairs={{0,4},{1,5},{2,6},{3,7},{4,0},{5,1},{6,2},{7,3},{8,12},{9,13},{10,... | collective-permute-start | bytes 1544 | tf_op jit(solution)/shard_map/ppermute | solution.py:349
  20.1 5.1 %pack.2 = bf16[8,2,2,4,2,64,128]{6,5,4,3,2,1,0:T(8,128)(2,1)} custom-call(s32[2,16]{1,0:T(2,128)} %bitcast.29, s32[1]{0:T(128)} %bitcast.1.xh, bf16[2,1,16,64,1024]{4,3,2,1,0:T(8,128)(2,1)} %block.3), custom_call_target="tpu_custom_call" | custom-call | flops 16777216 | bytes 8388608 | tf_op jit(solution)/shard_map/pack/pallas_call | solution.py:61
  25.4 39.3 %collective-permute-done = s32[128]{0:T(128)S(1)} collective-permute-done((s32[128]{0:T(128)S(1)}, s32[128]{0:T(128)S(1)}, u32[]{:S(2)}, u32[]{:S(2)}) %collective-permute-start) | collective-permute-done | bytes 544 | tf_op jit(solution)/shard_map/ppermute | solution.py:349
  64.8 3.2 %all-to-all-done.1 = bf16[128,2,64,128]{3,2,1,0:T(8,128)(2,1)} async-done(((bf16[128,2,64,128]{3,2,1,0:T(8,128)(2,1)}), bf16[128,2,64,128]{3,2,1,0:T(8,128)(2,1)}, u32[]{:S(2)}, u32[]{:S(2)}) %all-to-all-start.1) | async-done | bytes 4194336 | tf_op jit(solution)/shard_map/all_to_all | solution.py:367
  67.9 8.2 %all-to-all-start = ((bf16[128,2,64,128]{3,2,1,0:T(8,128)(2,1)}), bf16[128,2,64,128]{3,2,1,0:T(8,128)(2,1)}, u32[]{:S(2)}, u32[]{:S(2)}) async-start(bf16[128,2,64,128]{3,2,1,0:T(8,128)(2,1)} %bitcast.27), calls=%async_computation | async-start | bytes 8388608 | tf_op jit(solution)/shard_map/all_to_all | solution.py:387
  76.1 1.8 constant_dynamic-slice_fusion
  79.3 3.8 %collective-permute-done.1.other = bf16[16,1,4,2,64,128]{5,4,3,2,1,0:T(8,128)(2,1)S(1)} collective-permute-done((bf16[16,1,4,2,64,128]{5,4,3,2,1,0:T(8,128)(2,1)S(1)}, bf16[16,1,4,2,64,128]{5,4,3,2,1,0:T(8,128)(2,1)S(1)}, u32[]{:S(2)}, u32[]{:S(2)}) %collective-permute-start.1) | collective-permute-done | bytes 2097184 | tf_op jit(solution)/shard_map/ppermute | solution.py:362
  83.1 19.2 %first_half.1 = (bf16[12,256,256]{2,1,0:T(8,128)(2,1)S(1)}, bf16[12,256,256]{2,1,0:T(8,128)(2,1)S(1)}) custom-call(s32[6]{0:T(128)S(1)} %stack.46.where, bf16[16,2,4,2,64,128]{5,4,3,2,1,0:T(8,128)(2,1)} %bitcast.13.left.own, bf16[16,2,4,2,64,128]{5,4,3,2,1,0:T(8,128)(2,1)} %bitcast.13.left.own, ...), custom_call_target="tpu_custom_call" | custom-call | flops 12999999488 | bytes 12582912 | tf_op jit(solution)/shard_map/first_half/pallas_call | solution.py:236
  102.3 24.6 %all-to-all-done = bf16[128,2,64,128]{3,2,1,0:T(8,128)(2,1)} async-done(((bf16[128,2,64,128]{3,2,1,0:T(8,128)(2,1)}), bf16[128,2,64,128]{3,2,1,0:T(8,128)(2,1)}, u32[]{:S(2)}, u32[]{:S(2)}) %all-to-all-start) | async-done | bytes 4194336 | tf_op jit(solution)/shard_map/all_to_all | solution.py:387
  127.0 12.4 %second_half.3 = (bf16[12,64,256]{2,1,0:T(8,128)(2,1)S(1)}, bf16[12,64,256]{2,1,0:T(8,128)(2,1)S(1)}, bf16[12,64,256]{2,1,0:T(8,128)(2,1)S(1)}, bf16[12,64,256]{2,1,0:T(8,128)(2,1)S(1)}, bf16[4,64,4096]{2,1,0:T(8,128)(2,1)S(1)}) custom-call(s32[6]{0:T(128)S(1)} %stack.46.where, bf16[16,2,4,2,64,128]{5,4,3,2,1,0:T(8,128)(2,1)} %bitcast.16.landed.right, ...), custom_call_target="tpu_custom_call" | custom-call | flops 100000000 | bytes 1048576 | tf_op jit(solution)/shard_map/second_half/pallas_call | solution.py:269
  139.3 2.5 %collective-permute-start.2 = (bf16[4,64,4096]{2,1,0:T(8,128)(2,1)S(1)}, bf16[4,64,4096]{2,1,0:T(8,128)(2,1)S(1)}, u32[]{:S(2)}, u32[]{:S(2)}) collective-permute-start(bf16[4,64,4096]{2,1,0:T(8,128)(2,1)S(1)} %get-tuple-element.33), channel_id=1, source_target_pairs={{0,8},{1,9},{2,10},{3,11},{4,12},{5,13},{6,14},{7,15},{8,0},{9,1},... | collective-permute-start | bytes 6291464 | tf_op jit(solution)/shard_map/ppermute | solution.py:362
  142.0 2.5 %collective-permute-start.8 = (bf16[12,64,256]{2,1,0:T(8,128)(2,1)S(1)}, bf16[12,64,256]{2,1,0:T(8,128)(2,1)S(1)}, u32[]{:S(2)}, u32[]{:S(2)}) collective-permute-start(bf16[12,64,256]{2,1,0:T(8,128)(2,1)S(1)} %get-tuple-element.40), channel_id=1, source_target_pairs={{0,5},{1,6},{2,7},{3,4},{4,13},{5,14},{6,15},{7,12},{8,1},{9,2},{1... | collective-permute-start | bytes 1179656 | tf_op jit(solution)/shard_map/ppermute | solution.py:373
  144.6 2.1 %collective-permute-start.9 = (bf16[12,64,256]{2,1,0:T(8,128)(2,1)S(1)}, bf16[12,64,256]{2,1,0:T(8,128)(2,1)S(1)}, u32[]{:S(2)}, u32[]{:S(2)}) collective-permute-start(bf16[12,64,256]{2,1,0:T(8,128)(2,1)S(1)} %get-tuple-element.41), channel_id=1, source_target_pairs={{0,7},{1,4},{2,5},{3,6},{4,15},{5,12},{6,13},{7,14},{8,3},{9,0},{1... | collective-permute-start | bytes 1179656 | tf_op jit(solution)/shard_map/ppermute | solution.py:373
  147.8 9.3 %second_half.4 = (bf16[12,64,256]{2,1,0:T(8,128)(2,1)S(1)}, bf16[12,64,256]{2,1,0:T(8,128)(2,1)S(1)}, bf16[12,64,256]{2,1,0:T(8,128)(2,1)S(1)}) custom-call(s32[6]{0:T(128)S(1)} %stack.46.where, bf16[16,2,4,2,64,128]{5,4,3,2,1,0:T(8,128)(2,1)} %bitcast.16.landed.right, bf16[4,64,4096]{2,1,0:T(8,128)(2,1)S(1)} %collective-permute-done.2.right, ...), custom_call_target="tpu_custom_call" | custom-call | flops 100000000 | bytes 1048576 | tf_op jit(solution)/shard_map/second_half/pallas_call | solution.py:269
  157.1 1.8 collective-permute-start.3
  158.9 6.8 %second_half.5 = bf16[12,64,256]{2,1,0:T(8,128)(2,1)S(1)} custom-call(s32[6]{0:T(128)S(1)} %stack.46.where, bf16[16,2,4,2,64,128]{5,4,3,2,1,0:T(8,128)(2,1)} %bitcast.16.landed.right, bf16[4,64,4096]{2,1,0:T(8,128)(2,1)S(1)} %collective-permute-done.2.right, f32[8,128]{1,0:T(8,128)S(1)} %get-tuple-element.52.cos_ref, ...), custom_call_target="tpu_custom_call" | custom-call | flops 100000000 | bytes 1048576 | tf_op jit(solution)/shard_map/second_half/pallas_call | solution.py:269
  166.8 4.1 %collective-permute-start.5 = (bf16[12,64,256]{2,1,0:T(8,128)(2,1)S(1)}, bf16[12,64,256]{2,1,0:T(8,128)(2,1)S(1)}, u32[]{:S(2)}, u32[]{:S(2)}) collective-permute-start(bf16[12,64,256]{2,1,0:T(8,128)(2,1)S(1)} %get-tuple-element.37), channel_id=1, source_target_pairs={{0,7},{1,4},{2,5},{3,6},{4,15},{5,12},{6,13},{7,14},{8,3},{9,0},{1... | collective-permute-start | bytes 1179656 | tf_op jit(solution)/shard_map/ppermute | solution.py:373
  171.5 1.6 total.2.refs_4_
  173.1 3.2 %collective-permute-done.4.refs_1_ = bf16[12,64,256]{2,1,0:T(8,128)(2,1)S(1)} collective-permute-done((bf16[12,64,256]{2,1,0:T(8,128)(2,1)S(1)}, bf16[12,64,256]{2,1,0:T(8,128)(2,1)S(1)}, u32[]{:S(2)}, u32[]{:S(2)}) %collective-permute-start.4) | collective-permute-done | bytes 393248 | tf_op jit(solution)/shard_map/ppermute | solution.py:373
  176.3 3.5 %collective-permute-done.5.refs_2_ = bf16[12,64,256]{2,1,0:T(8,128)(2,1)S(1)} collective-permute-done((bf16[12,64,256]{2,1,0:T(8,128)(2,1)S(1)}, bf16[12,64,256]{2,1,0:T(8,128)(2,1)S(1)}, u32[]{:S(2)}, u32[]{:S(2)}) %collective-permute-start.5) | collective-permute-done | bytes 393248 | tf_op jit(solution)/shard_map/ppermute | solution.py:373
  179.8 2.8 %collective-permute-done.6.refs_3_ = bf16[12,64,256]{2,1,0:T(8,128)(2,1)S(1)} collective-permute-done((bf16[12,64,256]{2,1,0:T(8,128)(2,1)S(1)}, bf16[12,64,256]{2,1,0:T(8,128)(2,1)S(1)}, u32[]{:S(2)}, u32[]{:S(2)}) %collective-permute-start.6) | collective-permute-done | bytes 393248 | tf_op jit(solution)/shard_map/ppermute | solution.py:373
  182.7 1.6 total.3
  (19 shorter events, 4.5 us)
Async XLA Ops:
  5.1 12.0 %copy-start = (s32[128]{0:T(128)S(1)}, s32[128]{0:T(128)}, u32[]{:S(2)}) copy-start(s32[128]{0:T(128)} %param.5) | copy-start | bytes 1540
  5.1 62.8 %all-to-all-start.1 = ((bf16[128,2,64,128]{3,2,1,0:T(8,128)(2,1)}), bf16[128,2,64,128]{3,2,1,0:T(8,128)(2,1)}, u32[]{:S(2)}, u32[]{:S(2)}) async-start(bf16[128,2,64,128]{3,2,1,0:T(8,128)(2,1)} %bitcast.26), calls=%async_computation.1 | async-start | bytes 8388608 | tf_op jit(solution)/shard_map/all_to_all | solution.py:367
  17.1 47.6 %collective-permute-start = (s32[128]{0:T(128)S(1)}, s32[128]{0:T(128)S(1)}, u32[]{:S(2)}, u32[]{:S(2)}) collective-permute-start(s32[128]{0:T(128)S(1)} %copy-done), channel_id=1, source_target_pairs={{0,4},{1,5},{2,6},{3,7},{4,0},{5,1},{6,2},{7,3},{8,12},{9,13},{10,... | collective-permute-start | bytes 1544 | tf_op jit(solution)/shard_map/ppermute | solution.py:349
  67.9 59.0 %all-to-all-start = ((bf16[128,2,64,128]{3,2,1,0:T(8,128)(2,1)}), bf16[128,2,64,128]{3,2,1,0:T(8,128)(2,1)}, u32[]{:S(2)}, u32[]{:S(2)}) async-start(bf16[128,2,64,128]{3,2,1,0:T(8,128)(2,1)} %bitcast.27), calls=%async_computation | async-start | bytes 8388608 | tf_op jit(solution)/shard_map/all_to_all | solution.py:387
  77.9 5.2 %collective-permute-start.1 = (bf16[16,1,4,2,64,128]{5,4,3,2,1,0:T(8,128)(2,1)S(1)}, bf16[16,1,4,2,64,128]{5,4,3,2,1,0:T(8,128)(2,1)S(1)}, u32[]{:S(2)}, u32[]{:S(2)}) collective-permute-start(bf16[16,1,4,2,64,128]{5,4,3,2,1,0:T(8,128)(2,1)S(1)} %constant_dynamic-slice_fusion), channel_id=1, source_target_pairs={{0,8},{1,9},{2,10},{3,11},{4,12},{5,13},{6,14},{7,15},{8,0},{9,1},... | collective-permute-start | bytes 6291464 | tf_op jit(solution)/shard_map/ppermute | solution.py:362
  139.3 8.5 %collective-permute-start.2 = (bf16[4,64,4096]{2,1,0:T(8,128)(2,1)S(1)}, bf16[4,64,4096]{2,1,0:T(8,128)(2,1)S(1)}, u32[]{:S(2)}, u32[]{:S(2)}) collective-permute-start(bf16[4,64,4096]{2,1,0:T(8,128)(2,1)S(1)} %get-tuple-element.33), channel_id=1, source_target_pairs={{0,8},{1,9},{2,10},{3,11},{4,12},{5,13},{6,14},{7,15},{8,0},{9,1},... | collective-permute-start | bytes 6291464 | tf_op jit(solution)/shard_map/ppermute | solution.py:362
  141.9 23.9 %collective-permute-start.7 = (bf16[12,64,256]{2,1,0:T(8,128)(2,1)S(1)}, bf16[12,64,256]{2,1,0:T(8,128)(2,1)S(1)}, u32[]{:S(2)}, u32[]{:S(2)}) collective-permute-start(bf16[12,64,256]{2,1,0:T(8,128)(2,1)S(1)} %get-tuple-element.39), channel_id=1, source_target_pairs={{0,6},{1,7},{2,4},{3,5},{4,14},{5,15},{6,12},{7,13},{8,2},{9,3},{1... | collective-permute-start | bytes 1179656 | tf_op jit(solution)/shard_map/ppermute | solution.py:373
  142.0 24.8 %collective-permute-start.8 = (bf16[12,64,256]{2,1,0:T(8,128)(2,1)S(1)}, bf16[12,64,256]{2,1,0:T(8,128)(2,1)S(1)}, u32[]{:S(2)}, u32[]{:S(2)}) collective-permute-start(bf16[12,64,256]{2,1,0:T(8,128)(2,1)S(1)} %get-tuple-element.40), channel_id=1, source_target_pairs={{0,5},{1,6},{2,7},{3,4},{4,13},{5,14},{6,15},{7,12},{8,1},{9,2},{1... | collective-permute-start | bytes 1179656 | tf_op jit(solution)/shard_map/ppermute | solution.py:373
  144.6 26.3 %collective-permute-start.9 = (bf16[12,64,256]{2,1,0:T(8,128)(2,1)S(1)}, bf16[12,64,256]{2,1,0:T(8,128)(2,1)S(1)}, u32[]{:S(2)}, u32[]{:S(2)}) collective-permute-start(bf16[12,64,256]{2,1,0:T(8,128)(2,1)S(1)} %get-tuple-element.41), channel_id=1, source_target_pairs={{0,7},{1,4},{2,5},{3,6},{4,15},{5,12},{6,13},{7,14},{8,3},{9,0},{1... | collective-permute-start | bytes 1179656 | tf_op jit(solution)/shard_map/ppermute | solution.py:373
  146.7 24.8 %collective-permute-start.10 = (bf16[12,64,256]{2,1,0:T(8,128)(2,1)S(1)}, bf16[12,64,256]{2,1,0:T(8,128)(2,1)S(1)}, u32[]{:S(2)}, u32[]{:S(2)}) collective-permute-start(bf16[12,64,256]{2,1,0:T(8,128)(2,1)S(1)} %get-tuple-element.42), channel_id=1, source_target_pairs={{0,4},{1,5},{2,6},{3,7},{4,12},{5,13},{6,14},{7,15},{8,0},{9,1},{1... | collective-permute-start | bytes 1179656 | tf_op jit(solution)/shard_map/ppermute | solution.py:373
  157.1 15.9 %collective-permute-start.3 = (bf16[12,64,256]{2,1,0:T(8,128)(2,1)S(1)}, bf16[12,64,256]{2,1,0:T(8,128)(2,1)S(1)}, u32[]{:S(2)}, u32[]{:S(2)}) collective-permute-start(bf16[12,64,256]{2,1,0:T(8,128)(2,1)S(1)} %get-tuple-element.35), channel_id=1, source_target_pairs={{0,6},{1,7},{2,4},{3,5},{4,14},{5,15},{6,12},{7,13},{8,2},{9,3},{1... | collective-permute-start | bytes 1179656 | tf_op jit(solution)/shard_map/ppermute | solution.py:373
  165.8 10.5 %collective-permute-start.4 = (bf16[12,64,256]{2,1,0:T(8,128)(2,1)S(1)}, bf16[12,64,256]{2,1,0:T(8,128)(2,1)S(1)}, u32[]{:S(2)}, u32[]{:S(2)}) collective-permute-start(bf16[12,64,256]{2,1,0:T(8,128)(2,1)S(1)} %get-tuple-element.36), channel_id=1, source_target_pairs={{0,5},{1,6},{2,7},{3,4},{4,13},{5,14},{6,15},{7,12},{8,1},{9,2},{1... | collective-permute-start | bytes 1179656 | tf_op jit(solution)/shard_map/ppermute | solution.py:373
  166.8 13.0 %collective-permute-start.5 = (bf16[12,64,256]{2,1,0:T(8,128)(2,1)S(1)}, bf16[12,64,256]{2,1,0:T(8,128)(2,1)S(1)}, u32[]{:S(2)}, u32[]{:S(2)}) collective-permute-start(bf16[12,64,256]{2,1,0:T(8,128)(2,1)S(1)} %get-tuple-element.37), channel_id=1, source_target_pairs={{0,7},{1,4},{2,5},{3,6},{4,15},{5,12},{6,13},{7,14},{8,3},{9,0},{1... | collective-permute-start | bytes 1179656 | tf_op jit(solution)/shard_map/ppermute | solution.py:373
  170.9 11.8 %collective-permute-start.6 = (bf16[12,64,256]{2,1,0:T(8,128)(2,1)S(1)}, bf16[12,64,256]{2,1,0:T(8,128)(2,1)S(1)}, u32[]{:S(2)}, u32[]{:S(2)}) collective-permute-start(bf16[12,64,256]{2,1,0:T(8,128)(2,1)S(1)} %second_half.5), channel_id=1, source_target_pairs={{0,4},{1,5},{2,6},{3,7},{4,12},{5,13},{6,14},{7,15},{8,0},{9,1},{1... | collective-permute-start | bytes 1179656 | tf_op jit(solution)/shard_map/ppermute | solution.py:373
